TPU v7x, 32 devices: a whole 2x2x4 slice. The times are simulated.
32 devices in a mesh: col: 4 (over y, x), row: 8 (over z, core).
Axes of the slice: x: 2, y: 2, z: 4, core: 2. Of those that a mesh axis runs over, the one named last changes fastest.
Arguments:
- locked: float32 [1024, 131072], P('col', 'row'), may hold values from -6 to 6
- vectors: float32 [64, 131072], P(None, 'row'), may hold values from -125 to 125
- mass: float32 [131072], P('row'), may hold values from 0.18 to 3.5
Outputs:
- appended: float32 [64, 131072], P(None, 'row')
- factor: float32 [64, 64], replicated
All inputs are finite; a program needn't handle non-finite values.
Results may differ from a plain program's by a relative error of at most 0.0003.
Values sent between devices are 32-bit elements; how exact they have to be, the bound alone decides.
No kernel may reach another device: no remote copies, remote signals or barrier semaphores. Data moves between devices by JAX's collectives and lax.ppermute only.
A program may use at most 128 MiB of HBM per device.

v0:
```python
import jax
import jax.numpy as jnp
from jax import lax
from jax.sharding import PartitionSpec as P


def weighted(left, right, weights, total):
    return jnp.dot(left * weights, right.T, precision=lax.Precision.HIGHEST) / total


def row_gram(block, weights, total):
    return lax.psum(weighted(block, block, weights, total), "row")


def factorize(gram):
    size = gram.shape[0]
    places = jnp.arange(size, dtype=jnp.int32)

    def factorize_step(index, state):
        work, lower = state
        column = lax.dynamic_slice_in_dim(work, index, 1, 1)[:, 0]
        pivot = jnp.sqrt(lax.dynamic_slice_in_dim(column, index, 1, 0)[0])
        column = jnp.where(places >= index, column / pivot, jnp.zeros_like(column))
        pick = (places == index).astype(work.dtype)
        lower = lower + column[:, None] * pick[None, :]
        work = work - column[:, None] * column[None, :]
        return (work, lower)

    work, lower = lax.fori_loop(0, size, factorize_step, (gram, jnp.zeros_like(gram)))
    return lower


def invert_lower(lower):
    size = lower.shape[0]
    places = jnp.arange(size, dtype=jnp.int32)

    def invert_step(index, inverse):
        line = lax.dynamic_slice_in_dim(lower, index, 1, 0)[0]
        pick = (places == index).astype(lower.dtype)
        pivot = jnp.sum(line * pick)
        solved = (pick - jnp.dot(line, inverse, precision=lax.Precision.HIGHEST)) / pivot
        return inverse + pick[:, None] * solved[None, :]

    return lax.fori_loop(0, size, invert_step, jnp.zeros_like(lower))


def orthonormal(block, gram):
    lower = factorize(gram)
    inverse = invert_lower(lower)
    return (jnp.dot(inverse, block, precision=lax.Precision.HIGHEST), lower.T)


def local(locked, vectors, mass):
    rows = vectors.shape[1]
    total = rows * lax.axis_size("row")
    first = lax.psum(weighted(locked, vectors, mass, total), "row")
    once = vectors - lax.psum(jnp.dot(first.T, locked, precision=lax.Precision.HIGHEST), "col")
    second = lax.psum(weighted(locked, once, mass, total), "row")
    term = jnp.dot(second.T, locked, precision=lax.Precision.HIGHEST)
    projected = once - lax.psum(term, "col")
    middle, upper_one = orthonormal(projected, row_gram(projected, mass, total))
    appended, upper_two = orthonormal(middle, row_gram(middle, mass, total))
    factor = jnp.dot(upper_two, upper_one, precision=lax.Precision.HIGHEST)
    return (appended, factor)


def solution(mesh):
    return jax.shard_map(
        local,
        mesh=mesh,
        in_specs=(P("col", "row"), P(None, "row"), P("row")),
        out_specs=(P(None, "row"), P()),
        check_vma=False,
    )
```

profile of v0, /device:TPU:0, one launch (start us, length us, event | category | flops | bytes accessed | tf_op | source)
XLA Modules:
  0.0 848.1 jit_solution(9729364772456209298)
XLA Ops:
  7.2 16.8 %fusion.38 = f32[256,64]{1,0:T(8,128)} fusion(f32[64,16384]{1,0:T(8,128)} %param.12, f32[256,16384]{1,0:T(8,128)} %param.11, f32[16384]{0:T(1024)} %param.13), kind=kOutput, calls=%fused_computation.56 | convolution fusion | flops 3225436160 | bytes 21102592 | tf_op jit(solution)/shard_map/dot_general | solution.py:8
  24.1 57.0 %all-reduce.5.cloned.1.call-done = f32[256,64]{1,0:T(8,128)} async-done(((f32[256,64]{1,0:T(8,128)}), f32[256,64]{1,0:T(8,128)}) %all-reduce.5.cloned.1.call-update) | async-done | bytes 65552 | tf_op jit(solution)/shard_map/psum | solution.py:56
  81.2 14.9 %fusion.50 = f32[64,16384]{1,0:T(8,128)} fusion(f32[256,64]{1,0:T(8,128)} %all-reduce.5.cloned.1.call-done, f32[256,16384]{1,0:T(8,128)} %param.11), kind=kOutput, calls=%fused_computation.60 | convolution fusion | flops 3221225472 | bytes 21037056 | tf_op jit(solution)/shard_map/dot_general | solution.py:57
  96.4 102.8 %all-reduce.7.cloned.1.call-done = f32[64,16384]{1,0:T(8,128)} async-done(((f32[64,16384]{1,0:T(8,128)}), f32[64,16384]{1,0:T(8,128)}) %all-reduce.7.cloned.1.call-update) | async-done | bytes 4194320 | tf_op jit(solution)/shard_map/psum | solution.py:57
  199.1 3.9 sub.42
  203.0 2.0 copy-done.2
  205.0 17.6 %fusion.41 = f32[256,64]{1,0:T(8,128)} fusion(f32[64,16384]{1,0:T(8,128)S(1)} %sub.42, f32[256,16384]{1,0:T(8,128)} %param.11, f32[16384]{0:T(1024)S(1)} %copy-done.3), kind=kOutput, calls=%fused_computation.57 | convolution fusion | flops 3225436160 | bytes 21102592 | tf_op jit(solution)/shard_map/dot_general | solution.py:8
  222.7 54.3 %all-reduce.9.cloned.1.call-done = f32[256,64]{1,0:T(8,128)} async-done(((f32[256,64]{1,0:T(8,128)}), f32[256,64]{1,0:T(8,128)}) %all-reduce.9.cloned.1.call-update) | async-done | bytes 65552 | tf_op jit(solution)/shard_map/psum | solution.py:58
  277.0 15.0 %fusion.51 = f32[64,16384]{1,0:T(8,128)} fusion(f32[256,64]{1,0:T(8,128)} %all-reduce.9.cloned.1.call-done, f32[256,16384]{1,0:T(8,128)} %param.11), kind=kOutput, calls=%fused_computation.61 | convolution fusion | flops 3221225472 | bytes 21037056 | tf_op jit(solution)/shard_map/dot_general | solution.py:59
  292.0 103.0 %all-reduce.11.cloned.1.call-done = f32[64,16384]{1,0:T(8,128)} async-done(((f32[64,16384]{1,0:T(8,128)}), f32[64,16384]{1,0:T(8,128)}) %all-reduce.11.cloned.1.call-update) | async-done | bytes 4194320 | tf_op jit(solution)/shard_map/psum | solution.py:60
  395.0 3.9 sub.43
  398.9 2.0 copy-done
  400.9 3.6 fusion.44
  404.5 28.6 %psum.46 = f32[64,64]{1,0:T(8,128)S(1)} all-reduce(f32[64,64]{1,0:T(8,128)S(1)} %fusion.44), channel_id=1, replica_groups=mesh['col'=4,'row'=8] {'row'}, use_global_device_ids=true, to_apply=%region_4.0 | all-reduce | flops 4096 | bytes 32768 | tf_op jit(solution)/shard_map/psum | solution.py:12
  433.2 86.3 %while.70 = (s32[]{:T(128)}, f32[64,64]{0,1:T(8,128)S(1)}, f32[64,64]{0,1:T(8,128)S(1)}, s32[]{:T(128)}, s32[]{:T(128)}, /*index=5*/s32[]{:T(128)}) while((s32[]{:T(128)}, f32[64,64]{0,1:T(8,128)S(1)}, f32[64,64]{0,1:T(8,128)S(1)}, s32[]{:T(128)}, s32[]{:T(128)}, /*index=5*/s32[]{:T(128)}) %tuple.161), condition=%wide.region_6.7_spmd.clone.clone, body=%wide.region_5.6_spmd.clone.clone.sunk | while | flops 20932 | bytes 69499 | solution.py:29
  519.5 89.0 %while.68 = (s32[]{:T(128)}, f32[64,64]{1,0:T(8,128)S(1)}, f32[64,64]{1,0:T(8,128)S(1)}, s32[]{:T(128)}, s32[]{:T(128)}) while((s32[]{:T(128)}, f32[64,64]{1,0:T(8,128)S(1)}, f32[64,64]{1,0:T(8,128)S(1)}, s32[]{:T(128)}, s32[]{:T(128)}) %tuple.164), condition=%wide.region_9.10_spmd.clone, body=%wide.region_7.9_spmd.clone.sunk | while | flops 66114 | bytes 69968 | solution.py:44
  608.5 5.5 fusion.52
  614.0 1.9 copy-done.1
  615.9 3.6 fusion.47
  619.5 25.9 %psum.47 = f32[64,64]{1,0:T(8,128)S(1)} all-reduce(f32[64,64]{1,0:T(8,128)S(1)} %fusion.47), channel_id=1, replica_groups=mesh['col'=4,'row'=8] {'row'}, use_global_device_ids=true, to_apply=%region_10.11 | all-reduce | flops 4096 | bytes 32768 | tf_op jit(solution)/shard_map/psum | solution.py:12
  645.6 92.3 %while.71 = (s32[]{:T(128)}, f32[64,64]{0,1:T(8,128)S(1)}, f32[64,64]{0,1:T(8,128)S(1)}, s32[]{:T(128)}, s32[]{:T(128)}, /*index=5*/s32[]{:T(128)}) while((s32[]{:T(128)}, f32[64,64]{0,1:T(8,128)S(1)}, f32[64,64]{0,1:T(8,128)S(1)}, s32[]{:T(128)}, s32[]{:T(128)}, /*index=5*/s32[]{:T(128)}) %tuple.167), condition=%wide.region_12.13_spmd.clone.clone, body=%wide.region_11.12_spmd.clone.clone.sunk | while | flops 20932 | bytes 69499 | solution.py:29
  737.9 0.8 fusion.54
  738.7 94.9 %while.69 = (s32[]{:T(128)}, f32[64,64]{1,0:T(8,128)S(1)}, f32[64,64]{1,0:T(8,128)S(1)}, s32[]{:T(128)}, s32[]{:T(128)}) while((s32[]{:T(128)}, f32[64,64]{1,0:T(8,128)S(1)}, f32[64,64]{1,0:T(8,128)S(1)}, s32[]{:T(128)}, s32[]{:T(128)}) %tuple.170), condition=%wide.region_15.16_spmd.clone, body=%wide.region_13.15_spmd.clone.sunk | while | flops 66114 | bytes 69968 | solution.py:44
  739.3 0.8 fusion.86
  740.8 0.8 fusion.86
  742.3 0.8 fusion.86
  745.2 0.8 fusion.86
  746.7 0.8 fusion.86
  748.2 0.8 fusion.86
  749.7 0.8 fusion.86
  752.7 0.8 fusion.86
  833.7 7.9 fusion.53
  (1165 shorter events, 266.8 us)
Async XLA Ops:
  7.2 74.0 %all-reduce.5.cloned.1.call-start = ((), (), s32[]{:S(2)}) async-start(), calls=%async_computation | async-start | bytes 262144 | tf_op jit(solution)/shard_map/psum | solution.py:56
  24.1 175.1 %all-reduce.7.cloned.1.call-start = ((), (), s32[]{:S(2)}) async-start(), calls=%async_computation.1 | async-start | bytes 8388608 | tf_op jit(solution)/shard_map/psum | solution.py:57
  96.1 108.9 %copy-start.3 = (f32[16384]{0:T(1024)S(1)}, f32[16384]{0:T(1024)}, u32[]{:S(2)}) copy-start(f32[16384]{0:T(1024)} %param.13) | copy-start | bytes 196612
  96.1 180.8 %all-reduce.9.cloned.1.call-start = ((), (), s32[]{:S(2)}) async-start(), calls=%async_computation.2 | async-start | bytes 262144 | tf_op jit(solution)/shard_map/psum | solution.py:58
  203.0 2.0 copy-start.2
  222.6 172.3 %all-reduce.11.cloned.1.call-start = ((), (), s32[]{:S(2)}) async-start(), calls=%async_computation.3 | async-start | bytes 8388608 | tf_op jit(solution)/shard_map/psum | solution.py:60
  398.9 2.0 copy-start
  614.0 1.9 copy-start.1
Sparse Core Ops, SparseCore 0:
  24.2 56.9 all-reduce.4
  96.3 102.8 all-reduce.6
  222.7 54.1 all-reduce.8
  292.1 102.8 all-reduce.10
where the time goes:
time: 851 us; the launch traced here: 848 us
  waiting for transfers between devices  317 us (37%)
  matrix products  180 us (21%)
  other arithmetic  111 us (13%)
  loops' own time  90.1 us (11%)
  local copies, waits for them, and re-layouts  81.1 us (10%)
  blocking collectives  54.5 us (6%)
  between operations  13.9 us (2%)
    psum x1, waiting for transfers between devices, local(): projected = once - lax.psum(term, 'col')  103 us
    psum x1, waiting for transfers between devices, local(): lax.psum(jnp.dot(first.T, locked, precision=lax.Precision.HIGHEST), 'col')  103 us
    dot_general x128, matrix products, invert_step(): jnp.dot(line, inverse, precision=lax.Precision.HIGHEST)  94.7 us
    another operation x2, loops' own time, factorize(): lax.fori_loop(0, size, factorize_step, (gram, jnp.zeros_like(gram)))  89.9 us
    reduce_sum x128, other arithmetic, invert_step(): pivot = jnp.sum(line * pick)  78.2 us
    dynamic_slice x128, local copies, waits for them, and re-layouts, factorize_step(): pivot = jnp.sqrt(lax.dynamic_slice_in_dim(column, index, 1, 0)[0])  74.9 us
    psum x1, waiting for transfers between devices, local(): first = lax.psum(weighted(locked, vectors, mass, total), 'row')  57 us
    psum x2, blocking collectives, row_gram(): return lax.psum(weighted(block, block, weights, total), 'row')  54.5 us
  transfers between devices with their start and end apart: 4, of which 4 were waited for; matrix products, arithmetic and copies ran while one was open for 0% of the time, Pallas kernels for 0%

commit v1 on v0

v1 whole, which is shorter than its diff:
```python
import functools

import jax
import jax.numpy as jnp
from jax import lax
from jax.experimental import pallas as pl
from jax.experimental.pallas import tpu as pltpu
from jax.sharding import PartitionSpec as P

F32 = jnp.float32
BF16 = jnp.bfloat16
STEP = 512
VMEM_LIMIT = 48 * 1024 * 1024


def halves(x):
    high = x.astype(BF16)
    return high, (x - high.astype(F32)).astype(BF16)


def thirds(x):
    high = x.astype(BF16)
    rest = x - high.astype(F32)
    middle = rest.astype(BF16)
    return high, middle, (rest - middle.astype(F32)).astype(BF16)


def dot_nt(a, b):
    return lax.dot_general(a, b, (((1,), (1,)), ((), ())), preferred_element_type=F32)


def dot_nn(a, b):
    return lax.dot_general(a, b, (((1,), (0,)), ((), ())), preferred_element_type=F32)


def fold_rows(x, size):
    return (x[2 * size :] + x[size : 2 * size]) + x[:size]


def params():
    return pltpu.CompilerParams(vmem_limit_bytes=VMEM_LIMIT, dimension_semantics=("arbitrary",))


def cost(flops, nbytes):
    return pl.CostEstimate(flops=int(flops), bytes_accessed=int(nbytes), transcendentals=0)


def add_coefficients(acc_ref, locked_ref, block_ref, mass_ref):
    width = locked_ref.shape[1]
    for start in range(0, width, STEP):
        span = pl.ds(start, STEP)
        high, low = halves(locked_ref[:, span])
        pieces = jnp.concatenate(thirds(block_ref[:, span] * mass_ref[:, span]), axis=0)
        acc_ref[...] += dot_nt(
            jnp.concatenate([high, low], axis=1), jnp.concatenate([pieces, pieces], axis=1)
        )


def coefficients_kernel(separate, total, ids_ref, locked_ref, mass_ref, *refs):
    blocks, (out_ref, acc_ref) = refs[:-2], refs[-2:]
    step = pl.program_id(0)

    @pl.when(step == 0)
    def _():
        acc_ref[...] = jnp.zeros_like(acc_ref)

    if separate:
        for place, block_ref in enumerate(blocks):

            @pl.when(step == place)
            def _():
                add_coefficients(acc_ref, locked_ref, block_ref, mass_ref)
    else:
        add_coefficients(acc_ref, locked_ref, blocks[0], mass_ref)

    @pl.when(step == pl.num_programs(0) - 1)
    def _():
        out_ref[...] = fold_rows(acc_ref[...].T, out_ref.shape[0]) * (1.0 / total)


def coefficients(locked, mass, blocks, ids, unit, total):
    separate = isinstance(blocks, (list, tuple))
    held, steps = locked.shape[0], ids.shape[0]
    if not separate:
        blocks = [blocks]
    new = blocks[0].shape[0]
    block_spec = (
        pl.BlockSpec((new, unit), lambda i, ids: (0, 0))
        if separate
        else pl.BlockSpec((new, unit), lambda i, ids: (0, ids[i]))
    )
    return pl.pallas_call(
        functools.partial(coefficients_kernel, separate, total),
        out_shape=jax.ShapeDtypeStruct((new, held), F32),
        grid_spec=pltpu.PrefetchScalarGridSpec(
            num_scalar_prefetch=1,
            grid=(steps,),
            in_specs=[
                pl.BlockSpec((held, unit), lambda i, ids: (0, ids[i])),
                pl.BlockSpec((1, unit), lambda i, ids: (0, ids[i])),
            ]
            + [block_spec] * len(blocks),
            out_specs=pl.BlockSpec((new, held), lambda i, ids: (0, 0)),
            scratch_shapes=[pltpu.VMEM((held, 3 * new), F32)],
        ),
        compiler_params=params(),
        cost_estimate=cost(12 * held * new * steps * unit, 4 * (held + new) * steps * unit),
    )(ids, locked, mass, *blocks)


def corrections_kernel(count, base, extra, ids_ref, coef_ref, locked_ref, *refs):
    bases, refs = refs[: count if base == "list" else (1 if base else 0)], refs[count if base == "list" else (1 if base else 0) :]
    extras, outs = refs[: count * extra], refs[count * extra :]
    step = pl.program_id(0)
    size = coef_ref.shape[0]
    pieces = jnp.concatenate(thirds(coef_ref[...]), axis=0)
    pieces = jnp.concatenate([pieces, pieces], axis=1)
    for place in range(count):

        @pl.when(step == place)
        def _():
            for start in range(0, locked_ref.shape[1], STEP):
                span = pl.ds(start, STEP)
                high, low = halves(locked_ref[:, span])
                term = dot_nn(pieces, jnp.concatenate([high, low], axis=0))
                term = fold_rows(term, size)
                for one in range(extra):
                    term = term + extras[place * extra + one][:, span]
                if base:
                    term = bases[place if base == "list" else 0][:, span] - term
                outs[place][:, span] = term


def corrections(coef, locked, ids, unit, base=None, extras=()):
    held, count, new = locked.shape[0], ids.shape[0], coef.shape[0]
    extra = len(extras[0]) if extras else 0
    fixed = pl.BlockSpec((new, unit), lambda i, ids: (0, 0))
    flat = [x for group in extras for x in group]
    if base is None:
        kind, bases, base_specs = None, [], []
    elif isinstance(base, (list, tuple)):
        kind, bases, base_specs = "list", list(base), [fixed] * count
    else:
        kind, bases = "whole", [base]
        base_specs = [pl.BlockSpec((new, unit), lambda i, ids: (0, ids[i]))]
    return pl.pallas_call(
        functools.partial(corrections_kernel, count, kind, extra),
        out_shape=[jax.ShapeDtypeStruct((new, unit), F32)] * count,
        grid_spec=pltpu.PrefetchScalarGridSpec(
            num_scalar_prefetch=1,
            grid=(count,),
            in_specs=[
                pl.BlockSpec((new, held), lambda i, ids: (0, 0)),
                pl.BlockSpec((held, unit), lambda i, ids: (0, ids[i])),
            ]
            + base_specs
            + [fixed] * len(flat),
            out_specs=[fixed] * count,
        ),
        compiler_params=params(),
        cost_estimate=cost(12 * held * new * count * unit, 4 * (held + 2 * new) * count * unit),
    )(ids, coef, locked, *bases, *flat)


def eliminate(gram):
    size = gram.shape[0]
    rows = lax.broadcasted_iota(jnp.int32, (size, 2 * size), 0)
    lanes = lax.broadcasted_iota(jnp.int32, (size, 2 * size), 1)
    places = lax.broadcasted_iota(jnp.int32, (size, 1), 0)
    eye = (rows[:, :size] == lanes[:, :size]).astype(F32)
    work = jnp.concatenate([gram, eye], axis=1)
    scales = jnp.zeros((size, 1), F32)
    for index in range(size):
        line = work[index : index + 1, :]
        pivot = line[:, index : index + 1]
        scale = lax.rsqrt(pivot)
        scale = scale * (1.5 - 0.5 * pivot * scale * scale)
        line = line * scale
        column = jnp.where(places > index, work[:, index : index + 1] * scale, 0.0)
        scales = jnp.where(places == index, scale, scales)
        work = work - column * line
    work = work * scales
    upper = jnp.where(lanes >= rows, work, 0.0)[:, :size]
    return upper, work[:, size:]


def spread(matrix):
    pieces = jnp.concatenate(thirds(matrix), axis=0)
    return jnp.concatenate([pieces, pieces, pieces], axis=1)


def apply_left(spread_matrix, block):
    size = block.shape[0]
    return fold_rows(dot_nn(spread_matrix, jnp.concatenate(thirds(block), axis=0)), size)


def gram_of(block, mass):
    size = block.shape[0]
    left = jnp.concatenate(thirds(block * mass), axis=0)
    right = jnp.concatenate(thirds(block), axis=0)
    part = fold_rows(dot_nt(left, right), size)
    return (part[:, 2 * size :] + part[:, size : 2 * size]) + part[:, :size]


def own_gram_kernel(total, ids_ref, mass_ref, *refs):
    ins, outs = refs[:4], refs[4:]
    size = outs[0].shape[0]
    acc = jnp.zeros((size, size), F32)
    unit = outs[0].shape[1]
    for place in range(2):
        for start in range(0, unit, STEP):
            span = pl.ds(start, STEP)
            block = ins[place][:, span] - ins[2 + place][:, span]
            outs[place][:, span] = block
            where = pl.ds(pl.multiple_of(ids_ref[place] * unit + start, STEP), STEP)
            acc = acc + gram_of(block, mass_ref[:, where])
    outs[2][...] = acc * (1.0 / total)


def middle_kernel(total, ids_ref, mass_ref, gram_ref, a_ref, b_ref, gram_out, upper_out, inverse_out):
    upper, inverse = eliminate(gram_ref[...])
    upper_out[...] = upper
    inverse_out[...] = inverse
    left = spread(inverse)
    size, unit = a_ref.shape
    acc = jnp.zeros((size, size), F32)
    for place, block_ref in enumerate((a_ref, b_ref)):
        for start in range(0, unit, STEP):
            middle = apply_left(left, block_ref[:, pl.ds(start, STEP)])
            where = pl.ds(pl.multiple_of(ids_ref[place] * unit + start, STEP), STEP)
            acc = acc + gram_of(middle, mass_ref[:, where])
    gram_out[...] = acc * (1.0 / total)


def last_kernel(gram_ref, upper_ref, inverse_ref, factor_out, both_out):
    upper, inverse = eliminate(gram_ref[...])
    high = lax.Precision.HIGHEST
    factor_out[...] = jnp.dot(upper, upper_ref[...], precision=high, preferred_element_type=F32)
    both_out[...] = jnp.dot(inverse, inverse_ref[...], precision=high, preferred_element_type=F32)


def finish_kernel(count, ids_ref, both_ref, *refs):
    blocks, out_ref = refs[:-1], refs[-1]
    left = spread(both_ref[...])
    step = pl.program_id(0)
    for place in range(count):

        @pl.when(step == place)
        def _():
            for start in range(0, out_ref.shape[1], STEP):
                span = pl.ds(start, STEP)
                out_ref[:, span] = apply_left(left, blocks[place][:, span])


def flip(x, axis, bit):
    size = lax.axis_size(axis)
    return lax.ppermute(x, axis, [(i, i ^ bit) for i in range(size)])


def sum_over(x, axis):
    size = lax.axis_size(axis)
    bit = 1
    while bit < size:
        x = x + flip(x, axis, bit)
        bit *= 2
    return x


def local(locked, vectors, mass):
    new, rows = vectors.shape
    total = rows * lax.axis_size("row")
    unit = rows // 8
    mass = mass.reshape(1, rows)
    col = lax.axis_index("col")
    i, j = col % 2, col // 2
    k, m = 1 - i, 1 - j
    ids = lambda *xs: jnp.stack([jnp.asarray(x, jnp.int32) for x in xs])
    own = ids(2 * i + j, 4 + 2 * j + i)
    pass_on = ids(2 * i + m, 4 + 2 * j + k)
    away_first = ids(2 * k + m, 4 + 2 * m + k)
    away_second = ids(2 * k + j, 4 + 2 * m + i)

    def scatter_sum(coef, base):
        a1, b1 = corrections(coef, locked, away_first, unit)
        ra1, rb1 = flip(a1, "col", 1), flip(b1, "col", 2)
        a2, b2 = corrections(coef, locked, away_second, unit)
        ra2, rb2 = flip(a2, "col", 1), flip(b2, "col", 2)
        a3, b3 = corrections(coef, locked, pass_on, unit, extras=((ra1,), (rb1,)))
        ra3, rb3 = flip(a3, "col", 2), flip(b3, "col", 1)
        a4, b4 = corrections(coef, locked, own, unit, base=base, extras=((ra2,), (rb2,)))
        return (a4, b4), (ra3, rb3)

    def spread_out(a, b):
        ay, bx = flip(a, "col", 2), flip(b, "col", 1)
        ax, by = flip(a, "col", 1), flip(b, "col", 2)
        axy, bxy = flip(ay, "col", 1), flip(bx, "col", 2)
        return (ay, bx, ax, by), (axy, bxy)

    near = ids(2 * i + m, 4 + 2 * j + k, 2 * k + j, 4 + 2 * m + i)
    far = ids(2 * k + m, 4 + 2 * m + k)

    first = coefficients(locked, mass, vectors, jnp.arange(8, dtype=jnp.int32), unit, total)
    first = sum_over(first, "row")
    (a4, b4), (ra, rb) = scatter_sum(first, vectors)
    once = (a4 - ra, b4 - rb)
    near_units, far_units = spread_out(*once)
    second = coefficients(locked, mass, list(once), own, unit, total)
    second = second + coefficients(locked, mass, list(near_units), near, unit, total)
    second = second + coefficients(locked, mass, list(far_units), far, unit, total)
    second = sum_over(second, "row")
    (a4, b4), (ra, rb) = scatter_sum(second, list(once))

    square = jax.ShapeDtypeStruct((new, new), F32)
    smem = pl.BlockSpec(memory_space=pltpu.SMEM)
    vmem = pl.BlockSpec(memory_space=pltpu.VMEM)
    plain = pltpu.CompilerParams(vmem_limit_bytes=VMEM_LIMIT)
    a, b, gram = pl.pallas_call(
        functools.partial(own_gram_kernel, total),
        out_shape=[jax.ShapeDtypeStruct((new, unit), F32)] * 2 + [square],
        in_specs=[smem] + [vmem] * 5,
        out_specs=[vmem] * 3,
        compiler_params=plain,
        cost_estimate=cost(18 * new * new * 2 * unit, 24 * new * unit),
    )(own, mass, a4, b4, ra, rb)
    near_units, far_units = spread_out(a, b)
    gram = sum_over(sum_over(gram, "col"), "row")
    gram, upper, inverse = pl.pallas_call(
        functools.partial(middle_kernel, total),
        out_shape=[square] * 3,
        in_specs=[smem] + [vmem] * 4,
        out_specs=[vmem] * 3,
        compiler_params=plain,
        cost_estimate=cost(36 * new * new * 2 * unit, 8 * new * unit),
    )(own, mass, gram, a, b)
    gram = sum_over(sum_over(gram, "col"), "row")
    factor, both = pl.pallas_call(
        last_kernel,
        out_shape=[square] * 2,
        in_specs=[vmem] * 3,
        out_specs=[vmem] * 2,
        compiler_params=plain,
        cost_estimate=cost(1e6, 1e5),
    )(gram, upper, inverse)
    blocks = [a, b, *near_units, *far_units]
    appended = pl.pallas_call(
        functools.partial(finish_kernel, len(blocks)),
        out_shape=jax.ShapeDtypeStruct((new, rows), F32),
        grid_spec=pltpu.PrefetchScalarGridSpec(
            num_scalar_prefetch=1,
            grid=(len(blocks),),
            in_specs=[pl.BlockSpec((new, new), lambda i, ids: (0, 0))]
            + [pl.BlockSpec((new, unit), lambda i, ids: (0, 0))] * len(blocks),
            out_specs=pl.BlockSpec((new, unit), lambda i, ids: (0, ids[i])),
        ),
        compiler_params=params(),
        cost_estimate=cost(18 * new * new * rows, 8 * new * rows),
    )(jnp.concatenate([own, near, far]), both, *blocks)
    return (appended, factor)


def solution(mesh):
    return jax.shard_map(
        local,
        mesh=mesh,
        in_specs=(P("col", "row"), P(None, "row"), P("row")),
        out_specs=(P(None, "row"), P()),
        check_vma=False,
    )
```

time: 851 us -> 246 us (0.29)
  waiting for transfers between devices: 317 us -> 113 us
  matrix products: 180 us -> 0 us
  other arithmetic: 111 us -> 0.65 us
  loops' own time: 90.1 us -> 0 us
  Pallas kernels: 0 us -> 79.8 us
  local copies, waits for them, and re-layouts: 81.1 us -> 3.11 us
  blocking collectives: 54.5 us -> 0 us
  starting transfers between devices: 0.34 us -> 49.1 us
  between operations: 13.9 us -> 0.85 us
    psum x4 -> x0, waiting for transfers between devices: 317 us -> none  [the longest x1 103 us: local(): projected = once - lax.psum(term, 'col')]
    dot_general x137 -> x0, matrix products: 180 us -> none  [the longest x128 94.7 us: invert_step(): jnp.dot(line, inverse, precision=lax.Precision.HIGHEST)]
    ppermute x0 -> x40, waiting for transfers between devices: none -> 113 us  [flip(): return lax.ppermute(x, axis, [(i, i ^ bit) for i in range(size)])]
    another operation x4 -> x0, loops' own time: 90.1 us -> none  [the longest x2 89.9 us: factorize(): lax.fori_loop(0, size, factorize_step, (gram, jnp.zeros_like(gram)))]
    pallas_call x0 -> x16, Pallas kernels: none -> 79.8 us  [the longest x8 30.1 us: corrections(): pl.pallas_call(functools.partial(corrections_kernel, count, kind, extra),...]
    reduce_sum x128 -> x0, other arithmetic: 78.2 us -> none  [invert_step(): pivot = jnp.sum(line * pick)]
    dynamic_slice x128 -> x0, local copies, waits for them, and re-layouts: 74.9 us -> none  [factorize_step(): pivot = jnp.sqrt(lax.dynamic_slice_in_dim(column, index, 1, 0)[0])]
    psum x2 -> x0, blocking collectives: 54.5 us -> none  [row_gram(): return lax.psum(weighted(block, block, weights, total), 'row')]
  transfers between devices with their start and end apart: 4 -> 40, of which waited for: 4 -> 31; matrix products, arithmetic and copies ran while one was open for 0% -> 0% of each run, Pallas kernels for 0% -> 19%
where the time goes in v1:
time: 246 us
  waiting for transfers between devices  113 us (46%)
  Pallas kernels  79.8 us (32%)
  starting transfers between devices  49.1 us (20%)
  local copies, waits for them, and re-layouts  3.11 us (1%)
    ppermute x40, waiting for transfers between devices, flip(): return lax.ppermute(x, axis, [(i, i ^ bit) for i in range(size)])  113 us
    ppermute x40, starting transfers between devices, flip(): return lax.ppermute(x, axis, [(i, i ^ bit) for i in range(size)])  49.1 us
    pallas_call x8, Pallas kernels, corrections(): pl.pallas_call(functools.partial(corrections_kernel, count, kind, extra),...  30.1 us
    pallas_call x4, Pallas kernels, coefficients(): pl.pallas_call(functools.partial(coefficients_kernel, separate, total), o...  25.7 us
    pallas_call x1, Pallas kernels, local(): pl.pallas_call(functools.partial(middle_kernel, total), out_shape=[square...  8.36 us
    pallas_call x1, Pallas kernels, local(): pl.pallas_call(functools.partial(finish_kernel, len(blocks)), out_shape=j...  7.32 us
    pallas_call x1, Pallas kernels, local(): pl.pallas_call(last_kernel, out_shape=[square] * 2, in_specs=[vmem] * 3,...  6.95 us
  transfers between devices with their start and end apart: 40, of which 31 were waited for; matrix products, arithmetic and copies ran while one was open for 0% of the time, Pallas kernels for 19%

profile of v1, /device:TPU:0, one launch (start us, length us, event | category | flops | bytes accessed | tf_op | source)
XLA Modules:
  0.0 246.0 jit_solution(1354527454940600869)
XLA Ops:
  3.7 11.6 %shard_map.50 = f32[64,256]{1,0:T(8,128)S(1)} custom-call(s32[8]{0:T(128)S(1)} %iota.3.ids_ref, f32[256,16384]{1,0:T(8,128)} %locked_ref.23, f32[1,16384]{1,0:T(1,128)S(1)} %bitcast.9, f32[64,16384]{1,0:T(8,128)S(1)} %copy-done), custom_call_target="tpu_custom_call" | custom-call | flops 3221225472 | bytes 20971520 | tf_op jit(solution)/shard_map/pallas_call | solution.py:92
  16.7 3.0 %collective-permute-start.1 = (f32[64,256]{1,0:T(8,128)S(1)}, f32[64,256]{1,0:T(8,128)S(1)}, u32[]{:S(2)}, u32[]{:S(2)}) collective-permute-start(f32[64,256]{1,0:T(8,128)S(1)} %add.111), channel_id=1, source_target_pairs={{0,2},{1,3},{2,0},{3,1},{4,6},{5,7},{6,4},{7,5},{8,10},{9,11},{10,... | collective-permute-start | bytes 196616 | tf_op jit(solution)/shard_map/ppermute | solution.py:257
  22.1 2.9 %collective-permute-start.2 = (f32[64,256]{1,0:T(8,128)S(1)}, f32[64,256]{1,0:T(8,128)S(1)}, u32[]{:S(2)}, u32[]{:S(2)}) collective-permute-start(f32[64,256]{1,0:T(8,128)S(1)} %add.112), channel_id=1, source_target_pairs={{0,4},{1,5},{2,6},{3,7},{4,0},{5,1},{6,2},{7,3},{8,12},{9,13},{10,... | collective-permute-start | bytes 196616 | tf_op jit(solution)/shard_map/ppermute | solution.py:257
  27.4 4.2 %shard_map.53 = (f32[64,2048]{1,0:T(8,128)}, f32[64,2048]{1,0:T(8,128)S(1)}) custom-call(s32[2]{0:T(128)S(1)} %pad_add_fusion.3.ids_ref, f32[64,256]{1,0:T(8,128)S(1)} %add.113.coef_ref, f32[256,16384]{1,0:T(8,128)} %locked_ref.23), custom_call_target="tpu_custom_call" | custom-call | flops 805306368 | bytes 6291456 | tf_op jit(solution)/shard_map/pallas_call | solution.py:146
  35.0 4.2 %shard_map.51 = (f32[64,2048]{1,0:T(8,128)}, f32[64,2048]{1,0:T(8,128)S(1)}) custom-call(s32[2]{0:T(128)S(1)} %pad_add_fusion.1.ids_ref, f32[64,256]{1,0:T(8,128)S(1)} %add.113.coef_ref, f32[256,16384]{1,0:T(8,128)} %locked_ref.23), custom_call_target="tpu_custom_call" | custom-call | flops 805306368 | bytes 6291456 | tf_op jit(solution)/shard_map/pallas_call | solution.py:146
  40.0 6.7 %collective-permute-done.5.refs_0_ = f32[64,2048]{1,0:T(8,128)S(1)} collective-permute-done((f32[64,2048]{1,0:T(8,128)}, f32[64,2048]{1,0:T(8,128)S(1)}, u32[]{:S(2)}, u32[]{:S(2)}) %collective-permute-start.5) | collective-permute-done | bytes 524320 | tf_op jit(solution)/shard_map/ppermute | solution.py:257
  48.2 4.2 %shard_map.54 = (f32[64,2048]{1,0:T(8,128)S(1)}, f32[64,2048]{1,0:T(8,128)}) custom-call(s32[2]{0:T(128)S(1)} %pad_add_fusion.2.ids_ref, f32[64,256]{1,0:T(8,128)S(1)} %add.113.coef_ref, f32[256,16384]{1,0:T(8,128)} %locked_ref.23, f32[64,2048]{1,0:T(8,128)S(1)} %collective-permute-done.5.refs_0_, f32[64,2048]{1,0:T(8,128)S(1)} %collective-permute-done.6.refs_1_), custom_call_target="tpu_custom_call" | custom-call | flops 805306368 | bytes 6291456 | tf_op jit(solution)/shard_map/pallas_call | solution.py:146
  54.5 3.4 %collective-permute-done.3.refs_1_ = f32[64,2048]{1,0:T(8,128)S(1)} collective-permute-done((f32[64,2048]{1,0:T(8,128)}, f32[64,2048]{1,0:T(8,128)S(1)}, u32[]{:S(2)}, u32[]{:S(2)}) %collective-permute-start.3) | collective-permute-done | bytes 524320 | tf_op jit(solution)/shard_map/ppermute | solution.py:257
  59.4 3.7 %shard_map.52 = (f32[64,2048]{1,0:T(8,128)S(1)}, f32[64,2048]{1,0:T(8,128)S(1)}) custom-call(s32[2]{0:T(128)S(1)} %pad_add_fusion.ids_ref, f32[64,256]{1,0:T(8,128)S(1)} %add.113.coef_ref, f32[256,16384]{1,0:T(8,128)} %locked_ref.23, f32[64,16384]{1,0:T(8,128)} %refs_0_.3, f32[64,2048]{1,0:T(8,128)S(1)} %collective-permute-done.3.refs_1_, ...), custom_call_target="tpu_custom_call" | custom-call | flops 805306368 | bytes 6291456 | tf_op jit(solution)/shard_map/pallas_call | solution.py:146
  63.1 3.5 %collective-permute-done.8 = f32[64,2048]{1,0:T(8,128)S(1)} collective-permute-done((f32[64,2048]{1,0:T(8,128)}, f32[64,2048]{1,0:T(8,128)S(1)}, u32[]{:S(2)}, u32[]{:S(2)}) %collective-permute-start.8) | collective-permute-done | bytes 524320 | tf_op jit(solution)/shard_map/ppermute | solution.py:257
  70.9 10.7 %collective-permute-done.10.refs_1_ = f32[64,2048]{1,0:T(8,128)S(1)} collective-permute-done((f32[64,2048]{1,0:T(8,128)S(1)}, f32[64,2048]{1,0:T(8,128)S(1)}, u32[]{:S(2)}, u32[]{:S(2)}) %collective-permute-start.10) | collective-permute-done | bytes 524320 | tf_op jit(solution)/shard_map/ppermute | solution.py:257
  84.5 3.9 %shard_map.55 = f32[64,256]{1,0:T(8,128)S(1)} custom-call(s32[2]{0:T(128)S(1)} %pad_add_fusion.ids_ref, f32[256,16384]{1,0:T(8,128)} %locked_ref.23, f32[1,16384]{1,0:T(1,128)S(1)} %bitcast.10, f32[64,2048]{1,0:T(8,128)S(1)} %sub.19.refs_0_, f32[64,2048]{1,0:T(8,128)S(1)} %sub.20.refs_1_), custom_call_target="tpu_custom_call" | custom-call | flops 805306368 | bytes 5242880 | tf_op jit(solution)/shard_map/pallas_call | solution.py:92
  88.4 5.9 %collective-permute-done.12.refs_3_ = f32[64,2048]{1,0:T(8,128)S(1)} collective-permute-done((f32[64,2048]{1,0:T(8,128)S(1)}, f32[64,2048]{1,0:T(8,128)S(1)}, u32[]{:S(2)}, u32[]{:S(2)}) %collective-permute-start.12) | collective-permute-done | bytes 524320 | tf_op jit(solution)/shard_map/ppermute | solution.py:257
  94.3 6.4 %shard_map.56 = f32[64,256]{1,0:T(8,128)S(1)} custom-call(s32[4]{0:T(128)S(1)} %pad_add_fusion.4.ids_ref, f32[256,16384]{1,0:T(8,128)} %locked_ref.23, f32[1,16384]{1,0:T(1,128)S(1)} %bitcast.11, f32[64,2048]{1,0:T(8,128)S(1)} %collective-permute-done.9.refs_0_, f32[64,2048]{1,0:T(8,128)S(1)} %collective-permute-done.10.refs_1_, ...), custom_call_target="tpu_custom_call" | custom-call | flops 1610612736 | bytes 10485760 | tf_op jit(solution)/shard_map/pallas_call | solution.py:92
  100.9 3.9 %shard_map.57 = f32[64,256]{1,0:T(8,128)S(1)} custom-call(s32[2]{0:T(128)S(1)} %pad_add_fusion.3.ids_ref, f32[256,16384]{1,0:T(8,128)} %locked_ref.23, f32[1,16384]{1,0:T(1,128)S(1)} %bitcast.12, f32[64,2048]{1,0:T(8,128)S(1)} %collective-permute-done.13.refs_0_, f32[64,2048]{1,0:T(8,128)S(1)} %collective-permute-done.14.refs_1_), custom_call_target="tpu_custom_call" | custom-call | flops 805306368 | bytes 5242880 | tf_op jit(solution)/shard_map/pallas_call | solution.py:92
  110.5 3.0 %collective-permute-start.17 = (f32[64,256]{1,0:T(8,128)S(1)}, f32[64,256]{1,0:T(8,128)S(1)}, u32[]{:S(2)}, u32[]{:S(2)}) collective-permute-start(f32[64,256]{1,0:T(8,128)S(1)} %add.117), channel_id=1, source_target_pairs={{0,4},{1,5},{2,6},{3,7},{4,0},{5,1},{6,2},{7,3},{8,12},{9,13},{10,... | collective-permute-start | bytes 196616 | tf_op jit(solution)/shard_map/ppermute | solution.py:257
  116.1 3.6 %shard_map.60 = (f32[64,2048]{1,0:T(8,128)S(1)}, f32[64,2048]{1,0:T(8,128)S(1)}) custom-call(s32[2]{0:T(128)S(1)} %pad_add_fusion.3.ids_ref, f32[64,256]{1,0:T(8,128)S(1)} %add.118.coef_ref, f32[256,16384]{1,0:T(8,128)} %locked_ref.23), custom_call_target="tpu_custom_call" | custom-call | flops 805306368 | bytes 6291456 | tf_op jit(solution)/shard_map/pallas_call | solution.py:146
  121.8 3.4 %shard_map.58 = (f32[64,2048]{1,0:T(8,128)S(1)}, f32[64,2048]{1,0:T(8,128)S(1)}) custom-call(s32[2]{0:T(128)S(1)} %pad_add_fusion.1.ids_ref, f32[64,256]{1,0:T(8,128)S(1)} %add.118.coef_ref, f32[256,16384]{1,0:T(8,128)} %locked_ref.23), custom_call_target="tpu_custom_call" | custom-call | flops 805306368 | bytes 6291456 | tf_op jit(solution)/shard_map/pallas_call | solution.py:146
  127.2 7.3 %collective-permute-done.20.refs_0_ = f32[64,2048]{1,0:T(8,128)S(1)} collective-permute-done((f32[64,2048]{1,0:T(8,128)S(1)}, f32[64,2048]{1,0:T(8,128)S(1)}, u32[]{:S(2)}, u32[]{:S(2)}) %collective-permute-start.20) | collective-permute-done | bytes 524320 | tf_op jit(solution)/shard_map/ppermute | solution.py:257
  136.4 3.4 %shard_map.61 = (f32[64,2048]{1,0:T(8,128)S(1)}, f32[64,2048]{1,0:T(8,128)S(1)}) custom-call(s32[2]{0:T(128)S(1)} %pad_add_fusion.2.ids_ref, f32[64,256]{1,0:T(8,128)S(1)} %add.118.coef_ref, f32[256,16384]{1,0:T(8,128)} %locked_ref.23, f32[64,2048]{1,0:T(8,128)S(1)} %collective-permute-done.20.refs_0_, f32[64,2048]{1,0:T(8,128)S(1)} %collective-permute-done.21.refs_1_), custom_call_target="tpu_custom_call" | custom-call | flops 805306368 | bytes 6291456 | tf_op jit(solution)/shard_map/pallas_call | solution.py:146
  141.6 4.2 %collective-permute-done.18.refs_2_ = f32[64,2048]{1,0:T(8,128)S(1)} collective-permute-done((f32[64,2048]{1,0:T(8,128)S(1)}, f32[64,2048]{1,0:T(8,128)S(1)}, u32[]{:S(2)}, u32[]{:S(2)}) %collective-permute-start.18) | collective-permute-done | bytes 524320 | tf_op jit(solution)/shard_map/ppermute | solution.py:257
  147.7 3.5 %shard_map.59 = (f32[64,2048]{1,0:T(8,128)S(1)}, f32[64,2048]{1,0:T(8,128)S(1)}) custom-call(s32[2]{0:T(128)S(1)} %pad_add_fusion.ids_ref, f32[64,256]{1,0:T(8,128)S(1)} %add.118.coef_ref, f32[256,16384]{1,0:T(8,128)} %locked_ref.23, f32[64,2048]{1,0:T(8,128)S(1)} %sub.19.refs_0_, f32[64,2048]{1,0:T(8,128)S(1)} %sub.20.refs_1_, ...), custom_call_target="tpu_custom_call" | custom-call | flops 805306368 | bytes 6291456 | tf_op jit(solution)/shard_map/pallas_call | solution.py:146
  151.1 3.6 %collective-permute-done.22.refs_2_ = f32[64,2048]{1,0:T(8,128)S(1)} collective-permute-done((f32[64,2048]{1,0:T(8,128)S(1)}, f32[64,2048]{1,0:T(8,128)S(1)}, u32[]{:S(2)}, u32[]{:S(2)}) %collective-permute-start.22) | collective-permute-done | bytes 524320 | tf_op jit(solution)/shard_map/ppermute | solution.py:257
  160.2 10.8 %collective-permute-done.34.refs_2_ = f32[64,2048]{1,0:T(8,128)S(1)} collective-permute-done((f32[64,2048]{1,0:T(8,128)S(1)}, f32[64,2048]{1,0:T(8,128)S(1)}, u32[]{:S(2)}, u32[]{:S(2)}) %collective-permute-start.34) | collective-permute-done | bytes 524320 | tf_op jit(solution)/shard_map/ppermute | solution.py:257
  174.6 17.1 %collective-permute-done.24 = f32[64,64]{1,0:T(8,128)S(1)} collective-permute-done((f32[64,64]{1,0:T(8,128)S(1)}, f32[64,64]{1,0:T(8,128)S(1)}, u32[]{:S(2)}, u32[]{:S(2)}) %collective-permute-start.24) | collective-permute-done | bytes 16416 | tf_op jit(solution)/shard_map/ppermute | solution.py:257
  192.2 3.4 %collective-permute-done.25 = f32[64,64]{1,0:T(8,128)S(1)} collective-permute-done((f32[64,64]{1,0:T(8,128)S(1)}, f32[64,64]{1,0:T(8,128)S(1)}, u32[]{:S(2)}, u32[]{:S(2)}) %collective-permute-start.25) | collective-permute-done | bytes 16416 | tf_op jit(solution)/shard_map/ppermute | solution.py:257
  200.7 2.9 %collective-permute-start.28 = (f32[64,64]{1,0:T(8,128)S(1)}, f32[64,64]{1,0:T(8,128)S(1)}, u32[]{:S(2)}, u32[]{:S(2)}) collective-permute-start(f32[64,64]{1,0:T(8,128)S(1)} %add.122), channel_id=1, source_target_pairs={{0,4},{1,5},{2,6},{3,7},{4,0},{5,1},{6,2},{7,3},{8,12},{9,13},{10,... | collective-permute-start | bytes 49160 | tf_op jit(solution)/shard_map/ppermute | solution.py:257
  205.5 8.4 %shard_map.63 = (f32[64,64]{1,0:T(8,128)S(1)}, f32[64,64]{1,0:T(8,128)S(1)}, f32[64,64]{1,0:T(8,128)S(1)}) custom-call(s32[2]{0:T(128)S(1)} %pad_add_fusion.ids_ref, f32[1,16384]{1,0:T(1,128)S(1)} %bitcast.14, f32[64,64]{1,0:T(8,128)S(1)} %add.123.gram_ref, f32[64,2048]{1,0:T(8,128)S(1)} %get-tuple-element.43.a_ref.refs_0_, ...), custom_call_target="tpu_custom_call" | custom-call | flops 603979776 | bytes 1048576 | tf_op jit(solution)/shard_map/pallas_call | solution.py:327
  218.4 3.4 %collective-permute-done.30 = f32[64,64]{1,0:T(8,128)S(1)} collective-permute-done((f32[64,64]{1,0:T(8,128)S(1)}, f32[64,64]{1,0:T(8,128)S(1)}, u32[]{:S(2)}, u32[]{:S(2)}) %collective-permute-start.30) | collective-permute-done | bytes 16416 | tf_op jit(solution)/shard_map/ppermute | solution.py:257
  226.9 2.9 %collective-permute-start.33 = (f32[64,64]{1,0:T(8,128)S(1)}, f32[64,64]{1,0:T(8,128)S(1)}, u32[]{:S(2)}, u32[]{:S(2)}) collective-permute-start(f32[64,64]{1,0:T(8,128)S(1)} %add.127), channel_id=1, source_target_pairs={{0,4},{1,5},{2,6},{3,7},{4,0},{5,1},{6,2},{7,3},{8,12},{9,13},{10,... | collective-permute-start | bytes 49160 | tf_op jit(solution)/shard_map/ppermute | solution.py:257
  231.8 7.0 %shard_map.64 = (f32[64,64]{1,0:T(8,128)}, f32[64,64]{1,0:T(8,128)S(1)}) custom-call(f32[64,64]{1,0:T(8,128)S(1)} %add.128.gram_ref, f32[64,64]{1,0:T(8,128)S(1)} %get-tuple-element.46.upper_ref, f32[64,64]{1,0:T(8,128)S(1)} %get-tuple-element.47.inverse_ref), custom_call_target="tpu_custom_call" | custom-call | flops 1000000 | bytes 100000 | tf_op jit(solution)/shard_map/pallas_call | solution.py:336
  238.7 7.3 %shard_map.65 = f32[64,16384]{1,0:T(8,128)} custom-call(s32[8]{0:T(128)S(1)} %concatenate.4.ids_ref, f32[64,64]{1,0:T(8,128)S(1)} %get-tuple-element.48.both_ref, f32[64,2048]{1,0:T(8,128)S(1)} %get-tuple-element.43.a_ref.refs_0_, f32[64,2048]{1,0:T(8,128)S(1)} %get-tuple-element.44.b_ref.refs_1_, f32[64,2048]{1,0:T(8,128)S(1)} %collective-permute-done.34.refs_2_, ...), custom_call_target="tpu_custom_call" | custom-call | flops 1207959552 | bytes 8388608 | tf_op jit(solution)/shard_map/pallas_call | solution.py:345
  (96 shorter events, 72.1 us)
Async XLA Ops:
  16.7 5.4 %collective-permute-start.1 = (f32[64,256]{1,0:T(8,128)S(1)}, f32[64,256]{1,0:T(8,128)S(1)}, u32[]{:S(2)}, u32[]{:S(2)}) collective-permute-start(f32[64,256]{1,0:T(8,128)S(1)} %add.111), channel_id=1, source_target_pairs={{0,2},{1,3},{2,0},{3,1},{4,6},{5,7},{6,4},{7,5},{8,10},{9,11},{10,... | collective-permute-start | bytes 196616 | tf_op jit(solution)/shard_map/ppermute | solution.py:257
  22.1 5.3 %collective-permute-start.2 = (f32[64,256]{1,0:T(8,128)S(1)}, f32[64,256]{1,0:T(8,128)S(1)}, u32[]{:S(2)}, u32[]{:S(2)}) collective-permute-start(f32[64,256]{1,0:T(8,128)S(1)} %add.112), channel_id=1, source_target_pairs={{0,4},{1,5},{2,6},{3,7},{4,0},{5,1},{6,2},{7,3},{8,12},{9,13},{10,... | collective-permute-start | bytes 196616 | tf_op jit(solution)/shard_map/ppermute | solution.py:257
  31.6 15.1 %collective-permute-start.5 = (f32[64,2048]{1,0:T(8,128)}, f32[64,2048]{1,0:T(8,128)S(1)}, u32[]{:S(2)}, u32[]{:S(2)}) collective-permute-start(f32[64,2048]{1,0:T(8,128)} %get-tuple-element.29), channel_id=1, source_target_pairs={{0,8},{8,0},{16,24},{24,16},{1,9},{9,1},{17,25},{25,17},{2,10},{10... | collective-permute-start | bytes 1572872 | tf_op jit(solution)/shard_map/ppermute | solution.py:257
  33.3 14.9 %collective-permute-start.6 = (f32[64,2048]{1,0:T(8,128)S(1)}, f32[64,2048]{1,0:T(8,128)S(1)}, u32[]{:S(2)}, u32[]{:S(2)}) collective-permute-start(f32[64,2048]{1,0:T(8,128)S(1)} %get-tuple-element.30), channel_id=1, source_target_pairs={{0,16},{8,24},{16,0},{24,8},{1,17},{9,25},{17,1},{25,9},{2,18},{10... | collective-permute-start | bytes 1572872 | tf_op jit(solution)/shard_map/ppermute | solution.py:257
  39.1 18.8 %collective-permute-start.3 = (f32[64,2048]{1,0:T(8,128)}, f32[64,2048]{1,0:T(8,128)S(1)}, u32[]{:S(2)}, u32[]{:S(2)}) collective-permute-start(f32[64,2048]{1,0:T(8,128)} %get-tuple-element.26), channel_id=1, source_target_pairs={{0,8},{8,0},{16,24},{24,16},{1,9},{9,1},{17,25},{25,17},{2,10},{10... | collective-permute-start | bytes 1572872 | tf_op jit(solution)/shard_map/ppermute | solution.py:257
  39.7 19.7 %collective-permute-start.4 = (f32[64,2048]{1,0:T(8,128)S(1)}, f32[64,2048]{1,0:T(8,128)S(1)}, u32[]{:S(2)}, u32[]{:S(2)}) collective-permute-start(f32[64,2048]{1,0:T(8,128)S(1)} %get-tuple-element.27), channel_id=1, source_target_pairs={{0,16},{8,24},{16,0},{24,8},{1,17},{9,25},{17,1},{25,9},{2,18},{10... | collective-permute-start | bytes 1572872 | tf_op jit(solution)/shard_map/ppermute | solution.py:257
  52.3 14.2 %collective-permute-start.8 = (f32[64,2048]{1,0:T(8,128)}, f32[64,2048]{1,0:T(8,128)S(1)}, u32[]{:S(2)}, u32[]{:S(2)}) collective-permute-start(f32[64,2048]{1,0:T(8,128)} %get-tuple-element.33), channel_id=1, source_target_pairs={{0,8},{8,0},{16,24},{24,16},{1,9},{9,1},{17,25},{25,17},{2,10},{10... | collective-permute-start | bytes 1572872 | tf_op jit(solution)/shard_map/ppermute | solution.py:257
  52.7 15.4 %collective-permute-start.7 = (f32[64,2048]{1,0:T(8,128)S(1)}, f32[64,2048]{1,0:T(8,128)S(1)}, u32[]{:S(2)}, u32[]{:S(2)}) collective-permute-start(f32[64,2048]{1,0:T(8,128)S(1)} %get-tuple-element.31), channel_id=1, source_target_pairs={{0,16},{8,24},{16,0},{24,8},{1,17},{9,25},{17,1},{25,9},{2,18},{10... | collective-permute-start | bytes 1572872 | tf_op jit(solution)/shard_map/ppermute | solution.py:257
  66.6 14.9 %collective-permute-start.10 = (f32[64,2048]{1,0:T(8,128)S(1)}, f32[64,2048]{1,0:T(8,128)S(1)}, u32[]{:S(2)}, u32[]{:S(2)}) collective-permute-start(f32[64,2048]{1,0:T(8,128)S(1)} %sub.20.refs_1_), channel_id=1, source_target_pairs={{0,8},{8,0},{16,24},{24,16},{1,9},{9,1},{17,25},{25,17},{2,10},{10... | collective-permute-start | bytes 1572872 | tf_op jit(solution)/shard_map/ppermute | solution.py:257
  68.1 14.9 %collective-permute-start.9 = (f32[64,2048]{1,0:T(8,128)S(1)}, f32[64,2048]{1,0:T(8,128)S(1)}, u32[]{:S(2)}, u32[]{:S(2)}) collective-permute-start(f32[64,2048]{1,0:T(8,128)S(1)} %sub.19.refs_0_), channel_id=1, source_target_pairs={{0,16},{8,24},{16,0},{24,8},{1,17},{9,25},{17,1},{25,9},{2,18},{10... | collective-permute-start | bytes 1572872 | tf_op jit(solution)/shard_map/ppermute | solution.py:257
  69.7 24.6 %collective-permute-start.12 = (f32[64,2048]{1,0:T(8,128)S(1)}, f32[64,2048]{1,0:T(8,128)S(1)}, u32[]{:S(2)}, u32[]{:S(2)}) collective-permute-start(f32[64,2048]{1,0:T(8,128)S(1)} %sub.20.refs_1_), channel_id=1, source_target_pairs={{0,16},{8,24},{16,0},{24,8},{1,17},{9,25},{17,1},{25,9},{2,18},{10... | collective-permute-start | bytes 1572872 | tf_op jit(solution)/shard_map/ppermute | solution.py:257
  70.2 24.1 %collective-permute-start.11 = (f32[64,2048]{1,0:T(8,128)S(1)}, f32[64,2048]{1,0:T(8,128)S(1)}, u32[]{:S(2)}, u32[]{:S(2)}) collective-permute-start(f32[64,2048]{1,0:T(8,128)S(1)} %sub.19.refs_0_), channel_id=1, source_target_pairs={{0,8},{8,0},{16,24},{24,16},{1,9},{9,1},{17,25},{25,17},{2,10},{10... | collective-permute-start | bytes 1572872 | tf_op jit(solution)/shard_map/ppermute | solution.py:257
  81.6 19.3 %collective-permute-start.14 = (f32[64,2048]{1,0:T(8,128)S(1)}, f32[64,2048]{1,0:T(8,128)S(1)}, u32[]{:S(2)}, u32[]{:S(2)}) collective-permute-start(f32[64,2048]{1,0:T(8,128)S(1)} %collective-permute-done.10.refs_1_), channel_id=1, source_target_pairs={{0,16},{8,24},{16,0},{24,8},{1,17},{9,25},{17,1},{25,9},{2,18},{10... | collective-permute-start | bytes 1572872 | tf_op jit(solution)/shard_map/ppermute | solution.py:257
  83.1 17.8 %collective-permute-start.13 = (f32[64,2048]{1,0:T(8,128)S(1)}, f32[64,2048]{1,0:T(8,128)S(1)}, u32[]{:S(2)}, u32[]{:S(2)}) collective-permute-start(f32[64,2048]{1,0:T(8,128)S(1)} %collective-permute-done.9.refs_0_), channel_id=1, source_target_pairs={{0,8},{8,0},{16,24},{24,16},{1,9},{9,1},{17,25},{25,17},{2,10},{10... | collective-permute-start | bytes 1572872 | tf_op jit(solution)/shard_map/ppermute | solution.py:257
  106.1 4.3 %collective-permute-start.16 = (f32[64,256]{1,0:T(8,128)S(1)}, f32[64,256]{1,0:T(8,128)S(1)}, u32[]{:S(2)}, u32[]{:S(2)}) collective-permute-start(f32[64,256]{1,0:T(8,128)S(1)} %add.116), channel_id=1, source_target_pairs={{0,2},{1,3},{2,0},{3,1},{4,6},{5,7},{6,4},{7,5},{8,10},{9,11},{10,... | collective-permute-start | bytes 196616 | tf_op jit(solution)/shard_map/ppermute | solution.py:257
  110.5 5.6 %collective-permute-start.17 = (f32[64,256]{1,0:T(8,128)S(1)}, f32[64,256]{1,0:T(8,128)S(1)}, u32[]{:S(2)}, u32[]{:S(2)}) collective-permute-start(f32[64,256]{1,0:T(8,128)S(1)} %add.117), channel_id=1, source_target_pairs={{0,4},{1,5},{2,6},{3,7},{4,0},{5,1},{6,2},{7,3},{8,12},{9,13},{10,... | collective-permute-start | bytes 196616 | tf_op jit(solution)/shard_map/ppermute | solution.py:257
  119.7 14.9 %collective-permute-start.20 = (f32[64,2048]{1,0:T(8,128)S(1)}, f32[64,2048]{1,0:T(8,128)S(1)}, u32[]{:S(2)}, u32[]{:S(2)}) collective-permute-start(f32[64,2048]{1,0:T(8,128)S(1)} %get-tuple-element.38), channel_id=1, source_target_pairs={{0,8},{8,0},{16,24},{24,16},{1,9},{9,1},{17,25},{25,17},{2,10},{10... | collective-permute-start | bytes 1572872 | tf_op jit(solution)/shard_map/ppermute | solution.py:257
  121.6 14.9 %collective-permute-start.21 = (f32[64,2048]{1,0:T(8,128)S(1)}, f32[64,2048]{1,0:T(8,128)S(1)}, u32[]{:S(2)}, u32[]{:S(2)}) collective-permute-start(f32[64,2048]{1,0:T(8,128)S(1)} %get-tuple-element.39), channel_id=1, source_target_pairs={{0,16},{8,24},{16,0},{24,8},{1,17},{9,25},{17,1},{25,9},{2,18},{10... | collective-permute-start | bytes 1572872 | tf_op jit(solution)/shard_map/ppermute | solution.py:257
  125.2 20.6 %collective-permute-start.18 = (f32[64,2048]{1,0:T(8,128)S(1)}, f32[64,2048]{1,0:T(8,128)S(1)}, u32[]{:S(2)}, u32[]{:S(2)}) collective-permute-start(f32[64,2048]{1,0:T(8,128)S(1)} %get-tuple-element.34), channel_id=1, source_target_pairs={{0,8},{8,0},{16,24},{24,16},{1,9},{9,1},{17,25},{25,17},{2,10},{10... | collective-permute-start | bytes 1572872 | tf_op jit(solution)/shard_map/ppermute | solution.py:257
  126.7 20.9 %collective-permute-start.19 = (f32[64,2048]{1,0:T(8,128)S(1)}, f32[64,2048]{1,0:T(8,128)S(1)}, u32[]{:S(2)}, u32[]{:S(2)}) collective-permute-start(f32[64,2048]{1,0:T(8,128)S(1)} %get-tuple-element.35), channel_id=1, source_target_pairs={{0,16},{8,24},{16,0},{24,8},{1,17},{9,25},{17,1},{25,9},{2,18},{10... | collective-permute-start | bytes 1572872 | tf_op jit(solution)/shard_map/ppermute | solution.py:257
  139.8 14.9 %collective-permute-start.22 = (f32[64,2048]{1,0:T(8,128)S(1)}, f32[64,2048]{1,0:T(8,128)S(1)}, u32[]{:S(2)}, u32[]{:S(2)}) collective-permute-start(f32[64,2048]{1,0:T(8,128)S(1)} %get-tuple-element.40), channel_id=1, source_target_pairs={{0,16},{8,24},{16,0},{24,8},{1,17},{9,25},{17,1},{25,9},{2,18},{10... | collective-permute-start | bytes 1572872 | tf_op jit(solution)/shard_map/ppermute | solution.py:257
  140.1 14.6 %collective-permute-start.23 = (f32[64,2048]{1,0:T(8,128)S(1)}, f32[64,2048]{1,0:T(8,128)S(1)}, u32[]{:S(2)}, u32[]{:S(2)}) collective-permute-start(f32[64,2048]{1,0:T(8,128)S(1)} %get-tuple-element.41), channel_id=1, source_target_pairs={{0,8},{8,0},{16,24},{24,16},{1,9},{9,1},{17,25},{25,17},{2,10},{10... | collective-permute-start | bytes 1572872 | tf_op jit(solution)/shard_map/ppermute | solution.py:257
  156.1 14.9 %collective-permute-start.34 = (f32[64,2048]{1,0:T(8,128)S(1)}, f32[64,2048]{1,0:T(8,128)S(1)}, u32[]{:S(2)}, u32[]{:S(2)}) collective-permute-start(f32[64,2048]{1,0:T(8,128)S(1)} %get-tuple-element.43.a_ref.refs_0_), channel_id=1, source_target_pairs={{0,16},{8,24},{16,0},{24,8},{1,17},{9,25},{17,1},{25,9},{2,18},{10... | collective-permute-start | bytes 1572872 | tf_op jit(solution)/shard_map/ppermute | solution.py:257
  157.7 14.9 %collective-permute-start.35 = (f32[64,2048]{1,0:T(8,128)S(1)}, f32[64,2048]{1,0:T(8,128)S(1)}, u32[]{:S(2)}, u32[]{:S(2)}) collective-permute-start(f32[64,2048]{1,0:T(8,128)S(1)} %get-tuple-element.44.b_ref.refs_1_), channel_id=1, source_target_pairs={{0,8},{8,0},{16,24},{24,16},{1,9},{9,1},{17,25},{25,17},{2,10},{10... | collective-permute-start | bytes 1572872 | tf_op jit(solution)/shard_map/ppermute | solution.py:257
  159.2 79.5 %collective-permute-start.36 = (f32[64,2048]{1,0:T(8,128)S(1)}, f32[64,2048]{1,0:T(8,128)S(1)}, u32[]{:S(2)}, u32[]{:S(2)}) collective-permute-start(f32[64,2048]{1,0:T(8,128)S(1)} %get-tuple-element.43.a_ref.refs_0_), channel_id=1, source_target_pairs={{0,8},{8,0},{16,24},{24,16},{1,9},{9,1},{17,25},{25,17},{2,10},{10... | collective-permute-start | bytes 1572872 | tf_op jit(solution)/shard_map/ppermute | solution.py:257
  159.7 79.0 %collective-permute-start.37 = (f32[64,2048]{1,0:T(8,128)S(1)}, f32[64,2048]{1,0:T(8,128)S(1)}, u32[]{:S(2)}, u32[]{:S(2)}) collective-permute-start(f32[64,2048]{1,0:T(8,128)S(1)} %get-tuple-element.44.b_ref.refs_1_), channel_id=1, source_target_pairs={{0,16},{8,24},{16,0},{24,8},{1,17},{9,25},{17,1},{25,9},{2,18},{10... | collective-permute-start | bytes 1572872 | tf_op jit(solution)/shard_map/ppermute | solution.py:257
  171.1 67.7 %collective-permute-start.38 = (f32[64,2048]{1,0:T(8,128)S(1)}, f32[64,2048]{1,0:T(8,128)}, u32[]{:S(2)}, u32[]{:S(2)}) collective-permute-start(f32[64,2048]{1,0:T(8,128)S(1)} %collective-permute-done.34.refs_2_), channel_id=1, source_target_pairs={{0,8},{8,0},{16,24},{24,16},{1,9},{9,1},{17,25},{25,17},{2,10},{10... | collective-permute-start | bytes 1572872 | tf_op jit(solution)/shard_map/ppermute | solution.py:257
  172.5 66.2 %collective-permute-start.39 = (f32[64,2048]{1,0:T(8,128)S(1)}, f32[64,2048]{1,0:T(8,128)}, u32[]{:S(2)}, u32[]{:S(2)}) collective-permute-start(f32[64,2048]{1,0:T(8,128)S(1)} %collective-permute-done.35.refs_3_), channel_id=1, source_target_pairs={{0,16},{8,24},{16,0},{24,8},{1,17},{9,25},{17,1},{25,9},{2,18},{10... | collective-permute-start | bytes 1572872 | tf_op jit(solution)/shard_map/ppermute | solution.py:257
  174.0 17.6 %collective-permute-start.24 = (f32[64,64]{1,0:T(8,128)S(1)}, f32[64,64]{1,0:T(8,128)S(1)}, u32[]{:S(2)}, u32[]{:S(2)}) collective-permute-start(f32[64,64]{1,0:T(8,128)S(1)} %get-tuple-element.42), channel_id=1, source_target_pairs={{0,8},{8,0},{16,24},{24,16},{1,9},{9,1},{17,25},{25,17},{2,10},{10... | collective-permute-start | bytes 49160 | tf_op jit(solution)/shard_map/ppermute | solution.py:257
  200.7 4.8 %collective-permute-start.28 = (f32[64,64]{1,0:T(8,128)S(1)}, f32[64,64]{1,0:T(8,128)S(1)}, u32[]{:S(2)}, u32[]{:S(2)}) collective-permute-start(f32[64,64]{1,0:T(8,128)S(1)} %add.122), channel_id=1, source_target_pairs={{0,4},{1,5},{2,6},{3,7},{4,0},{5,1},{6,2},{7,3},{8,12},{9,13},{10,... | collective-permute-start | bytes 49160 | tf_op jit(solution)/shard_map/ppermute | solution.py:257
  213.9 4.0 %collective-permute-start.29 = (f32[64,64]{1,0:T(8,128)S(1)}, f32[64,64]{1,0:T(8,128)S(1)}, u32[]{:S(2)}, u32[]{:S(2)}) collective-permute-start(f32[64,64]{1,0:T(8,128)S(1)} %get-tuple-element.45), channel_id=1, source_target_pairs={{0,8},{8,0},{16,24},{24,16},{1,9},{9,1},{17,25},{25,17},{2,10},{10... | collective-permute-start | bytes 49160 | tf_op jit(solution)/shard_map/ppermute | solution.py:257
  226.9 4.8 %collective-permute-start.33 = (f32[64,64]{1,0:T(8,128)S(1)}, f32[64,64]{1,0:T(8,128)S(1)}, u32[]{:S(2)}, u32[]{:S(2)}) collective-permute-start(f32[64,64]{1,0:T(8,128)S(1)} %add.127), channel_id=1, source_target_pairs={{0,4},{1,5},{2,6},{3,7},{4,0},{5,1},{6,2},{7,3},{8,12},{9,13},{10,... | collective-permute-start | bytes 49160 | tf_op jit(solution)/shard_map/ppermute | solution.py:257
  (11 other events, 53.9 us)

commit v2 on v0

v2 whole, which is shorter than its diff:
```python
import functools

import jax
import jax.numpy as jnp
from jax import lax
from jax.experimental import pallas as pl
from jax.experimental.pallas import tpu as pltpu
from jax.sharding import PartitionSpec as P

F32 = jnp.float32
BF16 = jnp.bfloat16
STEP = 512
CHUNK = 1024
SLOTS = 4
VMEM_LIMIT = 30 * 1024 * 1024
FIRST_LIMIT = VMEM_LIMIT
SMEM = pl.BlockSpec(memory_space=pltpu.SMEM)
VMEM = pl.BlockSpec(memory_space=pltpu.VMEM)
HBM = pl.BlockSpec(memory_space=pltpu.HBM)
PARAMS = pltpu.CompilerParams(vmem_limit_bytes=VMEM_LIMIT)


def halves(x):
    high = x.astype(BF16)
    return high, (x - high.astype(F32)).astype(BF16)


def thirds(x):
    high = x.astype(BF16)
    rest = x - high.astype(F32)
    middle = rest.astype(BF16)
    low = (rest - middle.astype(F32)).astype(BF16)
    return jnp.concatenate([high, middle, low], axis=0)


def dot_nt(a, b):
    return lax.dot_general(a, b, (((1,), (1,)), ((), ())), preferred_element_type=F32)


def dot_nn(a, b):
    return lax.dot_general(a, b, (((1,), (0,)), ((), ())), preferred_element_type=F32)


def fold_rows(x, size):
    return (x[2 * size :] + x[size : 2 * size]) + x[:size]


def cost(flops, nbytes):
    return pl.CostEstimate(flops=int(flops), bytes_accessed=int(nbytes), transcendentals=0)


def array(*shape, dtype=F32):
    return jax.ShapeDtypeStruct(shape, dtype)


def columns(place, unit, start=0, width=None):
    return pl.ds(pl.multiple_of(place * unit + start, STEP), unit if width is None else width)


def first_kernel(total, locked, vectors, mass, out, high, low, mass_out, held_buf, new_buf, acc, sems, mass_sem):
    rows = locked.shape[1]
    count = rows // CHUNK

    def copies(index):
        span, slot = pl.ds(index * CHUNK, CHUNK), index % SLOTS
        return (
            pltpu.make_async_copy(vectors.at[:, span], new_buf.at[slot], sems.at[0, slot]),
            pltpu.make_async_copy(locked.at[:, span], held_buf.at[slot], sems.at[1, slot]),
        )

    mass_copy = pltpu.make_async_copy(mass, mass_out, mass_sem)
    mass_copy.start()
    for index in range(SLOTS - 1):
        for copy in copies(index):
            copy.start()
    mass_copy.wait()
    for index in range(count):
        if index + SLOTS - 1 < count:
            for copy in copies(index + SLOTS - 1):
                copy.start()
        for copy in copies(index):
            copy.wait()
        span, slot = pl.ds(index * CHUNK, CHUNK), index % SLOTS
        pieces = thirds(new_buf[slot] * mass_out[:, span])
        top, rest = halves(held_buf[slot])
        high[:, span] = top
        low[:, span] = rest
        term = dot_nt(jnp.concatenate([top, rest], axis=0), pieces)
        if index == 0:
            acc[...] = term
        else:
            acc[...] += term
    held = locked.shape[0]
    out[...] = fold_rows((acc[:held] + acc[held:]).T, out.shape[0]) * (1.0 / total)


def first_coefficients(locked, vectors, mass, total):
    (held, rows), new = locked.shape, vectors.shape[0]
    return pl.pallas_call(
        functools.partial(first_kernel, total),
        out_shape=[
            array(new, held),
            array(held, rows, dtype=BF16),
            array(held, rows, dtype=BF16),
            array(1, rows),
        ],
        in_specs=[HBM] * 3,
        out_specs=[VMEM] * 4,
        scratch_shapes=[
            pltpu.VMEM((SLOTS, held, CHUNK), F32),
            pltpu.VMEM((SLOTS, new, CHUNK), F32),
            pltpu.VMEM((2 * held, 3 * new), F32),
            pltpu.SemaphoreType.DMA((2, SLOTS)),
            pltpu.SemaphoreType.DMA,
        ],
        compiler_params=pltpu.CompilerParams(vmem_limit_bytes=FIRST_LIMIT),
        cost_estimate=cost(12 * held * new * rows, 8 * held * rows),
    )(locked, vectors, mass)


def fold_gram(x, size):
    part = fold_rows(x, size)
    return (part[:, 2 * size :] + part[:, size : 2 * size]) + part[:, :size]


def second_kernel(count, total, mode, ids, high, low, mass, *refs):
    blocks, rest = refs[:count], refs[count:]
    new, unit = blocks[0].shape
    held = high.shape[0]
    if mode == "own":
        out, grams, acc = rest
    elif mode == "near":
        base, out, grams, acc = rest
    else:
        base, own_grams, near_grams, out, acc, grams = rest
    for place in range(count):
        span = columns(ids[place], unit)
        block = blocks[place][...]
        pieces = thirds(block * mass[:, span])
        left = jnp.concatenate([high[:, span], low[:, span], thirds(block)], axis=0)
        term = dot_nt(left, pieces)
        grams[ids[place] if mode == "far" else place] = fold_gram(term[2 * held :], new)
        if place == 0:
            acc[...] = term[: 2 * held]
        else:
            acc[...] += term[: 2 * held]
    second = fold_rows((acc[:held] + acc[held:]).T, new)
    if mode != "own":
        second = second + base[...]
    if mode != "far":
        out[...] = second
        return
    for place in range(2):
        grams[ids[2 + place]] = own_grams[place]
    for place in range(4):
        grams[ids[4 + place]] = near_grams[place]
    gram = grams[0]
    for place in range(1, 8):
        gram = gram + grams[place]
    out[...] = jnp.concatenate([second, gram, jnp.zeros_like(gram)], axis=1) * (1.0 / total)


def second_coefficients(mode, ids, high, low, mass, blocks, total, *others):
    new, unit = blocks[0].shape
    held, count = high.shape[0], len(blocks)
    scratch = [pltpu.VMEM((2 * held, 3 * new), F32)]
    if mode == "far":
        shapes = [array(new, held + 2 * new)]
        scratch.append(pltpu.VMEM((8, new, new), F32))
    else:
        shapes = [array(new, held), array(count, new, new)]
    return pl.pallas_call(
        functools.partial(second_kernel, count, total, mode),
        out_shape=shapes,
        in_specs=[SMEM] + [VMEM] * (3 + count + len(others)),
        out_specs=[VMEM] * len(shapes),
        scratch_shapes=scratch,
        compiler_params=PARAMS,
        cost_estimate=cost(14 * held * new * count * unit, 4 * (held + new) * count * unit),
    )(ids, high, low, mass, *blocks, *others)


def corrections_kernel(count, ids, coef, high, low, *outs):
    new, unit = outs[0].shape
    held = high.shape[0]
    pieces = thirds(coef[:, :held])
    pieces = jnp.concatenate([pieces, pieces], axis=1)
    for place in range(count):
        for start in range(0, unit, STEP):
            span = columns(ids[place], unit, start, STEP)
            term = dot_nn(pieces, jnp.concatenate([high[:, span], low[:, span]], axis=0))
            outs[place][:, pl.ds(start, STEP)] = fold_rows(term, new)


def corrections(ids, coef, high, low, unit):
    new, held, count = coef.shape[0], high.shape[0], ids.shape[0]
    return pl.pallas_call(
        functools.partial(corrections_kernel, count),
        out_shape=[array(new, unit)] * count,
        in_specs=[SMEM] + [VMEM] * 3,
        out_specs=[VMEM] * count,
        compiler_params=PARAMS,
        cost_estimate=cost(12 * held * new * count * unit, 4 * (held + new) * count * unit),
    )(ids, coef, high, low)


def eliminate(gram):
    size = gram.shape[0]
    rows = lax.broadcasted_iota(jnp.int32, (size, 2 * size), 0)
    lanes = lax.broadcasted_iota(jnp.int32, (size, 2 * size), 1)
    places = lax.broadcasted_iota(jnp.int32, (size, 1), 0)
    eye = (rows[:, :size] == lanes[:, :size]).astype(F32)
    work = jnp.concatenate([gram, eye], axis=1)
    scales = jnp.zeros((size, 1), F32)
    for index in range(size):
        line = work[index : index + 1, :]
        pivot = line[:, index : index + 1]
        scale = lax.rsqrt(pivot)
        scale = scale * (1.5 - 0.5 * pivot * scale * scale)
        line = line * scale
        column = jnp.where(places > index, work[:, index : index + 1] * scale, 0.0)
        scales = jnp.where(places == index, scale, scales)
        work = work - column * line
    work = work * scales
    upper = jnp.where(lanes >= rows, work, 0.0)[:, :size]
    return upper, work[:, size:]


def spread(matrix):
    pieces = thirds(matrix)
    return jnp.concatenate([pieces, pieces, pieces], axis=1)


def apply_left(spread_matrix, block):
    return fold_rows(dot_nn(spread_matrix, thirds(block)), block.shape[0])


def gram_of(block, mass):
    size = block.shape[0]
    return fold_gram(dot_nt(thirds(block * mass), thirds(block)), size)


def factor_kernel(both, upper_out, inverse_out):
    size = upper_out.shape[0]
    held = both.shape[1] - 2 * size
    upper_out[...], inverse_out[...] = eliminate(both[:, held : held + size])


def middle_kernel(total, ids, mass, inverse, *refs):
    ins, outs = refs[:4], refs[4:]
    new, unit = outs[0].shape
    left = spread(inverse[...])
    acc = jnp.zeros((new, new), F32)
    for place in range(2):
        for start in range(0, unit, STEP):
            span = pl.ds(start, STEP)
            middle = apply_left(left, ins[place][:, span] - ins[2 + place][:, span])
            outs[place][:, span] = middle
            acc = acc + gram_of(middle, mass[:, columns(ids[place], unit, start, STEP)])
    outs[2][...] = acc * (1.0 / total)


def last_kernel(gram, upper_one, factor_out, inverse_out):
    upper, inverse = eliminate(gram[...])
    factor_out[...] = jnp.dot(
        upper, upper_one[...], precision=lax.Precision.HIGHEST, preferred_element_type=F32
    )
    inverse_out[...] = inverse


def finish_kernel(count, ids, inverse, *refs):
    blocks, out = refs[:count], refs[-1]
    left = spread(inverse[...])
    step = pl.program_id(0)
    for place in range(count):

        @pl.when(step == place)
        def _():
            for start in range(0, out.shape[1], STEP):
                span = pl.ds(start, STEP)
                out[:, span] = apply_left(left, blocks[place][:, span])


def finish(ids, inverse, blocks, rows, target=None):
    new, unit = blocks[0].shape
    count = len(blocks)
    extra = [] if target is None else [target]
    whole = lambda shape: pl.BlockSpec(shape, lambda i, ids: (0, 0))
    return pl.pallas_call(
        functools.partial(finish_kernel, count),
        out_shape=array(new, rows),
        grid_spec=pltpu.PrefetchScalarGridSpec(
            num_scalar_prefetch=1,
            grid=(count,),
            in_specs=[whole((new, new))]
            + [whole((new, unit))] * count
            + [pl.BlockSpec(memory_space=pl.ANY)] * len(extra),
            out_specs=pl.BlockSpec((new, unit), lambda i, ids: (0, ids[i])),
        ),
        input_output_aliases={} if target is None else {2 + count: 0},
        compiler_params=PARAMS,
        cost_estimate=cost(18 * new * new * count * unit, 8 * new * count * unit),
    )(ids, inverse, *blocks, *extra)


def flip(x, axis, bit):
    size = lax.axis_size(axis)
    return lax.ppermute(x, axis, [(i, i ^ bit) for i in range(size)])


def sum_over(x, axis):
    size = lax.axis_size(axis)
    bit = 1
    while bit < size:
        x = x + flip(x, axis, bit)
        bit *= 2
    return x


def sum_of_four(x, axis):
    one, two, three = flip(x, axis, 1), flip(x, axis, 2), flip(x, axis, 3)
    return (x + one) + (two + three)


def local(locked, vectors, mass):
    new, rows = vectors.shape
    total = rows * lax.axis_size("row")
    unit = rows // 8
    col = lax.axis_index("col")
    i, j = col % 2, col // 2
    k, m = 1 - i, 1 - j
    ids = lambda *xs: jnp.stack([jnp.asarray(x, jnp.int32) for x in xs])
    own = (2 * i + j, 4 + 2 * j + i)
    pass_on = (2 * i + m, 4 + 2 * j + k)
    away_first = (2 * k + m, 4 + 2 * m + k)
    away_second = (2 * k + j, 4 + 2 * m + i)
    near = ids(*pass_on, *away_second)
    far = ids(*away_first)

    first, high, low, mass = first_coefficients(locked, vectors, mass.reshape(1, rows), total)

    def scatter_sum(coef, base):
        a1, b1 = corrections(ids(*away_first), coef, high, low, unit)
        ra1, rb1 = flip(a1, "col", 1), flip(b1, "col", 2)
        a2, b2 = corrections(ids(*away_second), coef, high, low, unit)
        ra2, rb2 = flip(a2, "col", 1), flip(b2, "col", 2)
        a3, b3, a4, b4 = corrections(ids(*pass_on, *own), coef, high, low, unit)
        ra3, rb3 = flip(a3 + ra1, "col", 2), flip(b3 + rb1, "col", 1)
        return (base[0] - (a4 + ra2), base[1] - (b4 + rb2)), (ra3, rb3)

    def spread_out(a, b):
        ay, bx = flip(a, "col", 2), flip(b, "col", 1)
        ax, by = flip(a, "col", 1), flip(b, "col", 2)
        return (ay, bx, ax, by), (flip(ay, "col", 1), flip(bx, "col", 2))

    first = sum_over(first, "row")
    here = [lax.dynamic_slice_in_dim(vectors, place * unit, unit, 1) for place in own]
    (a, b), (ra, rb) = scatter_sum(first, here)
    once = (a - ra, b - rb)
    near_units, far_units = spread_out(*once)
    order = jnp.concatenate([far, ids(*own), near])
    second, grams = second_coefficients("own", ids(*own), high, low, mass, once, total)
    second, more = second_coefficients("near", near, high, low, mass, near_units, total, second)
    (second,) = second_coefficients("far", order, high, low, mass, far_units, total, second, grams, more)
    second = sum_over(second, "row")
    (a, b), (ra, rb) = scatter_sum(second, once)

    upper, inverse = pl.pallas_call(
        factor_kernel,
        out_shape=[array(new, new)] * 2,
        in_specs=[VMEM],
        out_specs=[VMEM] * 2,
        compiler_params=PARAMS,
        cost_estimate=cost(1e6, 1e5),
    )(second)
    a, b, gram = pl.pallas_call(
        functools.partial(middle_kernel, total),
        out_shape=[array(new, unit)] * 2 + [array(new, new)],
        in_specs=[SMEM] + [VMEM] * 6,
        out_specs=[VMEM] * 3,
        compiler_params=PARAMS,
        cost_estimate=cost(36 * new * new * 2 * unit, 24 * new * unit),
    )(ids(*own), mass, inverse, a, b, ra, rb)
    ay, bx = flip(a, "col", 2), flip(b, "col", 1)
    gram = sum_of_four(gram, "col")
    gram, late_a, late_b, ay, bx = lax.optimization_barrier((gram, a, b, ay, bx))
    ax, by = flip(late_a, "col", 1), flip(late_b, "col", 2)
    near_units, far_units = (ay, bx, ax, by), (flip(ay, "col", 1), flip(bx, "col", 2))
    gram = sum_over(gram, "row")
    factor, inverse = pl.pallas_call(
        last_kernel,
        out_shape=[array(new, new)] * 2,
        in_specs=[VMEM] * 2,
        out_specs=[VMEM] * 2,
        compiler_params=PARAMS,
        cost_estimate=cost(1e6, 1e5),
    )(gram, upper)
    appended = finish(jnp.concatenate([ids(*own), near]), inverse, (a, b, *near_units), rows)
    appended = finish(far, inverse, far_units, rows, appended)
    return (appended, factor)


def solution(mesh):
    return jax.shard_map(
        local,
        mesh=mesh,
        in_specs=(P("col", "row"), P(None, "row"), P("row")),
        out_specs=(P(None, "row"), P()),
        check_vma=False,
    )
```

time: 851 us -> 220 us (0.26)
  waiting for transfers between devices: 317 us -> 77 us
  matrix products: 180 us -> 0 us
  other arithmetic: 111 us -> 5.96 us
  loops' own time: 90.1 us -> 0 us
  Pallas kernels: 0 us -> 57.7 us
  blocking collectives: 54.5 us -> 0 us
  local copies, waits for them, and re-layouts: 81.1 us -> 30.8 us
  starting transfers between devices: 0.34 us -> 47.5 us
  between operations: 13.9 us -> 0.85 us
    psum x4 -> x0, waiting for transfers between devices: 317 us -> none  [the longest x1 103 us: local(): projected = once - lax.psum(term, 'col')]
    dot_general x137 -> x0, matrix products: 180 us -> none  [the longest x128 94.7 us: invert_step(): jnp.dot(line, inverse, precision=lax.Precision.HIGHEST)]
    another operation x4 -> x0, loops' own time: 90.1 us -> none  [the longest x2 89.9 us: factorize(): lax.fori_loop(0, size, factorize_step, (gram, jnp.zeros_like(gram)))]
    reduce_sum x128 -> x0, other arithmetic: 78.2 us -> none  [invert_step(): pivot = jnp.sum(line * pick)]
    ppermute x0 -> x36, waiting for transfers between devices: none -> 77 us  [flip(): return lax.ppermute(x, axis, [(i, i ^ bit) for i in range(size)])]
    dynamic_slice x128 -> x0, local copies, waits for them, and re-layouts: 74.9 us -> none  [factorize_step(): pivot = jnp.sqrt(lax.dynamic_slice_in_dim(column, index, 1, 0)[0])]
    pallas_call x0 -> x15, Pallas kernels: none -> 57.7 us  [the longest x1 13.4 us: first_coefficients(): pl.pallas_call(functools.partial(first_kernel, total), out_shape=[array(n...]
    psum x2 -> x0, blocking collectives: 54.5 us -> none  [row_gram(): return lax.psum(weighted(block, block, weights, total), 'row')]
  transfers between devices with their start and end apart: 4 -> 36, of which waited for: 4 -> 21; matrix products, arithmetic and copies ran while one was open for 0% -> 2% of each run, Pallas kernels for 0% -> 15%
where the time goes in v2:
time: 220 us
  waiting for transfers between devices  77 us (35%)
  Pallas kernels  57.7 us (26%)
  starting transfers between devices  47.5 us (22%)
  local copies, waits for them, and re-layouts  30.8 us (14%)
  other arithmetic  5.96 us (3%)
    ppermute x36, waiting for transfers between devices, flip(): return lax.ppermute(x, axis, [(i, i ^ bit) for i in range(size)])  77 us
    ppermute x36, starting transfers between devices, flip(): return lax.ppermute(x, axis, [(i, i ^ bit) for i in range(size)])  47.5 us
    unnamed x22, local copies, waits for them, and re-layouts  30.7 us
    pallas_call x1, Pallas kernels, first_coefficients(): pl.pallas_call(functools.partial(first_kernel, total), out_shape=[array(n...  13.4 us
    pallas_call x6, Pallas kernels, corrections(): pl.pallas_call(functools.partial(corrections_kernel, count), out_shape=[a...  11.2 us
    pallas_call x3, Pallas kernels, second_coefficients(): pl.pallas_call(functools.partial(second_kernel, count, total, mode), out_...  9.65 us
    pallas_call x2, Pallas kernels, finish(): pl.pallas_call(functools.partial(finish_kernel, count), out_shape=array(n...  8.28 us
    pallas_call x1, Pallas kernels, local(): pl.pallas_call(last_kernel, out_shape=[array(new, new)] * 2, in_specs=[VM...  6.91 us
  transfers between devices with their start and end apart: 36, of which 21 were waited for; matrix products, arithmetic and copies ran while one was open for 2% of the time, Pallas kernels for 15%

profile of v2, /device:TPU:0, one launch (start us, length us, event | category | flops | bytes accessed | tf_op | source)
XLA Modules:
  0.0 219.9 jit_solution(10191474649241048547)
XLA Ops:
  3.7 13.4 %shard_map.50 = (f32[64,256]{1,0:T(8,128)S(1)}, bf16[256,16384]{1,0:T(8,128)(2,1)S(1)}, bf16[256,16384]{1,0:T(8,128)(2,1)S(1)}, f32[1,16384]{1,0:T(1,128)S(1)}) custom-call(f32[256,16384]{1,0:T(8,128)} %locked.1, f32[64,16384]{1,0:T(8,128)S(1)} %copy-done.8, f32[1,16384]{1,0:T(1,128)S(1)} %bitcast.9), custom_call_target="tpu_custom_call" | custom-call | flops 3221225472 | bytes 33554432 | tf_op jit(solution)/shard_map/pallas_call | solution.py:99
  17.0 3.3 %copy-done = bf16[256,16384]{1,0:T(8,128)(2,1)} copy-done((bf16[256,16384]{1,0:T(8,128)(2,1)}, bf16[256,16384]{1,0:T(8,128)(2,1)S(1)}, u32[]{:S(2)}) %copy-start) | copy-done | bytes 8388632
  20.3 3.3 %copy-done.4 = bf16[256,16384]{1,0:T(8,128)(2,1)} copy-done((bf16[256,16384]{1,0:T(8,128)(2,1)}, bf16[256,16384]{1,0:T(8,128)(2,1)S(1)}, u32[]{:S(2)}) %copy-start.4) | copy-done | bytes 8388632
  25.0 3.0 %collective-permute-start.1 = (f32[64,256]{1,0:T(8,128)S(1)}, f32[64,256]{1,0:T(8,128)S(1)}, u32[]{:S(2)}, u32[]{:S(2)}) collective-permute-start(f32[64,256]{1,0:T(8,128)S(1)} %add.115), channel_id=1, source_target_pairs={{0,2},{1,3},{2,0},{3,1},{4,6},{5,7},{6,4},{7,5},{8,10},{9,11},{10,... | collective-permute-start | bytes 196616 | tf_op jit(solution)/shard_map/ppermute | solution.py:308
  28.0 2.4 %collective-permute-done.1 = f32[64,256]{1,0:T(8,128)S(1)} collective-permute-done((f32[64,256]{1,0:T(8,128)S(1)}, f32[64,256]{1,0:T(8,128)S(1)}, u32[]{:S(2)}, u32[]{:S(2)}) %collective-permute-start.1) | collective-permute-done | bytes 65568 | tf_op jit(solution)/shard_map/ppermute | solution.py:308
  30.4 2.9 %collective-permute-start.2 = (f32[64,256]{1,0:T(8,128)S(1)}, f32[64,256]{1,0:T(8,128)S(1)}, u32[]{:S(2)}, u32[]{:S(2)}) collective-permute-start(f32[64,256]{1,0:T(8,128)S(1)} %add.116), channel_id=1, source_target_pairs={{0,4},{1,5},{2,6},{3,7},{4,0},{5,1},{6,2},{7,3},{8,12},{9,13},{10,... | collective-permute-start | bytes 196616 | tf_op jit(solution)/shard_map/ppermute | solution.py:308
  35.7 3.4 %copy-done.1 = bf16[256,16384]{1,0:T(8,128)(2,1)S(1)} copy-done((bf16[256,16384]{1,0:T(8,128)(2,1)S(1)}, bf16[256,16384]{1,0:T(8,128)(2,1)}, u32[]{:S(2)}) %copy-start.1) | copy-done | bytes 8388632
  39.1 3.4 %copy-done.5 = bf16[256,16384]{1,0:T(8,128)(2,1)S(1)} copy-done((bf16[256,16384]{1,0:T(8,128)(2,1)S(1)}, bf16[256,16384]{1,0:T(8,128)(2,1)}, u32[]{:S(2)}) %copy-start.5) | copy-done | bytes 8388632
  47.8 3.4 %copy-done.2 = bf16[256,16384]{1,0:T(8,128)(2,1)S(1)} copy-done((bf16[256,16384]{1,0:T(8,128)(2,1)S(1)}, bf16[256,16384]{1,0:T(8,128)(2,1)}, u32[]{:S(2)}) %copy-start.2) | copy-done | bytes 8388632
  51.2 3.4 %copy-done.6 = bf16[256,16384]{1,0:T(8,128)(2,1)S(1)} copy-done((bf16[256,16384]{1,0:T(8,128)(2,1)S(1)}, bf16[256,16384]{1,0:T(8,128)(2,1)}, u32[]{:S(2)}) %copy-start.6) | copy-done | bytes 8388632
  57.0 2.4 %shard_map.51 = (f32[64,2048]{1,0:T(8,128)S(1)}, f32[64,2048]{1,0:T(8,128)S(1)}, f32[64,2048]{1,0:T(8,128)S(1)}, f32[64,2048]{1,0:T(8,128)S(1)}) custom-call(s32[4]{0:T(128)S(1)} %pad_add_fusion.2.ids, f32[64,256]{1,0:T(8,128)S(1)} %add.117.coef, bf16[256,16384]{1,0:T(8,128)(2,1)S(1)} %copy-done.2, bf16[256,16384]{1,0:T(8,128)(2,1)S(1)} %copy-done.6), custom_call_target="tpu_custom_call" | custom-call | flops 1610612736 | bytes 10485760 | tf_op jit(solution)/shard_map/pallas_call | solution.py:197
  65.6 5.5 %collective-permute-done.3 = f32[64,2048]{1,0:T(8,128)} collective-permute-done((f32[64,2048]{1,0:T(8,128)S(1)}, f32[64,2048]{1,0:T(8,128)}, u32[]{:S(2)}, u32[]{:S(2)}) %collective-permute-start.3) | collective-permute-done | bytes 524320 | tf_op jit(solution)/shard_map/ppermute | solution.py:308
  71.7 8.4 %collective-permute-done.5 = f32[64,2048]{1,0:T(8,128)} collective-permute-done((f32[64,2048]{1,0:T(8,128)}, f32[64,2048]{1,0:T(8,128)}, u32[]{:S(2)}, u32[]{:S(2)}) %collective-permute-start.5) | collective-permute-done | bytes 524320 | tf_op jit(solution)/shard_map/ppermute | solution.py:308
  87.2 10.8 %collective-permute-done.11.refs_1_ = f32[64,2048]{1,0:T(8,128)S(1)} collective-permute-done((f32[64,2048]{1,0:T(8,128)S(1)}, f32[64,2048]{1,0:T(8,128)S(1)}, u32[]{:S(2)}, u32[]{:S(2)}) %collective-permute-start.11) | collective-permute-done | bytes 524320 | tf_op jit(solution)/shard_map/ppermute | solution.py:308
  100.3 3.4 %copy-done.3 = bf16[256,16384]{1,0:T(8,128)(2,1)S(1)} copy-done((bf16[256,16384]{1,0:T(8,128)(2,1)S(1)}, bf16[256,16384]{1,0:T(8,128)(2,1)}, u32[]{:S(2)}) %copy-start.3) | copy-done | bytes 8388632
  103.7 3.4 %copy-done.7 = bf16[256,16384]{1,0:T(8,128)(2,1)S(1)} copy-done((bf16[256,16384]{1,0:T(8,128)(2,1)S(1)}, bf16[256,16384]{1,0:T(8,128)(2,1)}, u32[]{:S(2)}) %copy-start.7) | copy-done | bytes 8388632
  107.1 2.4 %shard_map.54 = (f32[64,256]{1,0:T(8,128)S(1)}, f32[2,64,64]{2,1,0:T(8,128)S(1)}) custom-call(s32[2]{0:T(128)S(1)} %pad_add_fusion.1.ids, bf16[256,16384]{1,0:T(8,128)(2,1)S(1)} %copy-done.3, bf16[256,16384]{1,0:T(8,128)(2,1)S(1)} %copy-done.7, f32[1,16384]{1,0:T(1,128)S(1)} %get-tuple-element.38.mass, f32[64,2048]{1,0:T(8,128)S(1)} %get-tuple-element.75.refs_0_, ...), custom_call_target="tpu_custom_call" | custom-call | flops 939524096 | bytes 5242880 | tf_op jit(solution)/shard_map/pallas_call | solution.py:172
  110.1 4.0 %shard_map.55 = (f32[64,256]{1,0:T(8,128)S(1)}, f32[4,64,64]{2,1,0:T(8,128)S(1)}) custom-call(s32[4]{0:T(128)S(1)} %pad_add_fusion.5.ids, bf16[256,16384]{1,0:T(8,128)(2,1)S(1)} %copy-done.3, bf16[256,16384]{1,0:T(8,128)(2,1)S(1)} %copy-done.7, f32[1,16384]{1,0:T(1,128)S(1)} %get-tuple-element.38.mass, f32[64,2048]{1,0:T(8,128)S(1)} %collective-permute-done.6.refs_0_, ...), custom_call_target="tpu_custom_call" | custom-call | flops 1879048192 | bytes 10485760 | tf_op jit(solution)/shard_map/pallas_call | solution.py:172
  114.1 3.6 %collective-permute-done.12.refs_1_ = f32[64,2048]{1,0:T(8,128)} collective-permute-done((f32[64,2048]{1,0:T(8,128)S(1)}, f32[64,2048]{1,0:T(8,128)}, u32[]{:S(2)}, u32[]{:S(2)}) %collective-permute-start.12) | collective-permute-done | bytes 524320 | tf_op jit(solution)/shard_map/ppermute | solution.py:308
  117.7 3.3 %shard_map.56 = f32[64,384]{1,0:T(8,128)S(1)} custom-call(s32[8]{0:T(128)S(1)} %concatenate.8.ids, bf16[256,16384]{1,0:T(8,128)(2,1)S(1)} %copy-done.3, bf16[256,16384]{1,0:T(8,128)(2,1)S(1)} %copy-done.7, f32[1,16384]{1,0:T(1,128)S(1)} %get-tuple-element.38.mass, f32[64,2048]{1,0:T(8,128)} %collective-permute-done.7.refs_0_, ...), custom_call_target="tpu_custom_call" | custom-call | flops 939524096 | bytes 5242880 | tf_op jit(solution)/shard_map/pallas_call | solution.py:172
  124.1 3.3 %collective-permute-done.16 = f32[64,384]{1,0:T(8,128)S(1)} collective-permute-done((f32[64,384]{1,0:T(8,128)S(1)}, f32[64,384]{1,0:T(8,128)S(1)}, u32[]{:S(2)}, u32[]{:S(2)}) %collective-permute-start.16) | collective-permute-done | bytes 98336 | tf_op jit(solution)/shard_map/ppermute | solution.py:308
  127.4 2.9 %collective-permute-start.17 = (f32[64,384]{1,0:T(8,128)S(1)}, f32[64,384]{1,0:T(8,128)S(1)}, u32[]{:S(2)}, u32[]{:S(2)}) collective-permute-start(f32[64,384]{1,0:T(8,128)S(1)} %add.124), channel_id=1, source_target_pairs={{0,4},{1,5},{2,6},{3,7},{4,0},{5,1},{6,2},{7,3},{8,12},{9,13},{10,... | collective-permute-start | bytes 294920 | tf_op jit(solution)/shard_map/ppermute | solution.py:308
  130.2 4.7 %collective-permute-done.17 = f32[64,384]{1,0:T(8,128)S(1)} collective-permute-done((f32[64,384]{1,0:T(8,128)S(1)}, f32[64,384]{1,0:T(8,128)S(1)}, u32[]{:S(2)}, u32[]{:S(2)}) %collective-permute-start.17) | collective-permute-done | bytes 98336 | tf_op jit(solution)/shard_map/ppermute | solution.py:308
  144.6 6.2 %shard_map.57 = (f32[64,64]{1,0:T(8,128)S(1)}, f32[64,64]{1,0:T(8,128)S(1)}) custom-call(f32[64,384]{1,0:T(8,128)S(1)} %add.125.both.coef), custom_call_target="tpu_custom_call" | custom-call | flops 1000000 | bytes 100000 | tf_op jit(solution)/shard_map/pallas_call | solution.py:368
  154.9 7.8 %collective-permute-done.19 = f32[64,2048]{1,0:T(8,128)S(1)} collective-permute-done((f32[64,2048]{1,0:T(8,128)S(1)}, f32[64,2048]{1,0:T(8,128)S(1)}, u32[]{:S(2)}, u32[]{:S(2)}) %collective-permute-start.19) | collective-permute-done | bytes 524320 | tf_op jit(solution)/shard_map/ppermute | solution.py:308
  164.4 7.9 %collective-permute-done.23.refs_3_ = f32[64,2048]{1,0:T(8,128)S(1)} collective-permute-done((f32[64,2048]{1,0:T(8,128)S(1)}, f32[64,2048]{1,0:T(8,128)S(1)}, u32[]{:S(2)}, u32[]{:S(2)}) %collective-permute-start.23) | collective-permute-done | bytes 524320 | tf_op jit(solution)/shard_map/ppermute | solution.py:308
  179.9 7.1 %collective-permute-done.24 = f32[64,64]{1,0:T(8,128)S(1)} collective-permute-done((f32[64,64]{1,0:T(8,128)S(1)}, f32[64,64]{1,0:T(8,128)S(1)}, u32[]{:S(2)}, u32[]{:S(2)}) %collective-permute-start.24) | collective-permute-done | bytes 16416 | tf_op jit(solution)/shard_map/ppermute | solution.py:308
  187.0 2.4 %collective-permute-done.26 = f32[64,64]{1,0:T(8,128)S(1)} collective-permute-done((f32[64,64]{1,0:T(8,128)S(1)}, f32[64,64]{1,0:T(8,128)S(1)}, u32[]{:S(2)}, u32[]{:S(2)}) %collective-permute-start.26) | collective-permute-done | bytes 16416 | tf_op jit(solution)/shard_map/ppermute | solution.py:308
  194.7 2.4 %collective-permute-start.30 = (f32[64,64]{1,0:T(8,128)S(1)}, f32[64,64]{1,0:T(8,128)S(1)}, u32[]{:S(2)}, u32[]{:S(2)}) collective-permute-start(f32[64,64]{1,0:T(8,128)S(1)} %add.133), channel_id=1, source_target_pairs={{0,2},{1,3},{2,0},{3,1},{4,6},{5,7},{6,4},{7,5},{8,10},{9,11},{10,... | collective-permute-start | bytes 49160 | tf_op jit(solution)/shard_map/ppermute | solution.py:308
  199.1 3.4 %collective-permute-start.31 = (f32[64,64]{1,0:T(8,128)S(1)}, f32[64,64]{1,0:T(8,128)S(1)}, u32[]{:S(2)}, u32[]{:S(2)}) collective-permute-start(f32[64,64]{1,0:T(8,128)S(1)} %add.134), channel_id=1, source_target_pairs={{0,4},{1,5},{2,6},{3,7},{4,0},{5,1},{6,2},{7,3},{8,12},{9,13},{10,... | collective-permute-start | bytes 49160 | tf_op jit(solution)/shard_map/ppermute | solution.py:308
  204.7 6.9 %shard_map.62 = (f32[64,64]{1,0:T(8,128)}, f32[64,64]{1,0:T(8,128)S(1)}) custom-call(f32[64,64]{1,0:T(8,128)S(1)} %add.135.gram, f32[64,64]{1,0:T(8,128)S(1)} %get-tuple-element.67.upper_one), custom_call_target="tpu_custom_call" | custom-call | flops 1000000 | bytes 100000 | tf_op jit(solution)/shard_map/pallas_call | solution.py:390
  211.6 6.0 %shard_map.63.refs_2_ = f32[64,16384]{1,0:T(8,128)} custom-call(s32[6]{0:T(128)S(1)} %concatenate.9.ids, f32[64,64]{1,0:T(8,128)S(1)} %get-tuple-element.68.inverse, f32[64,2048]{1,0:T(8,128)S(1)} %get-tuple-element.71.refs_0_, f32[64,2048]{1,0:T(8,128)S(1)} %get-tuple-element.72.refs_1_, f32[64,2048]{1,0:T(8,128)S(1)} %collective-permute-done.27.refs_2_, ...), custom_call_target="tpu_custom_call" | custom-call | flops 905969664 | bytes 6291456 | tf_op jit(solution)/shard_map/pallas_call | solution.py:289
  (101 shorter events, 69.3 us)
Async XLA Ops:
  25.0 5.4 %collective-permute-start.1 = (f32[64,256]{1,0:T(8,128)S(1)}, f32[64,256]{1,0:T(8,128)S(1)}, u32[]{:S(2)}, u32[]{:S(2)}) collective-permute-start(f32[64,256]{1,0:T(8,128)S(1)} %add.115), channel_id=1, source_target_pairs={{0,2},{1,3},{2,0},{3,1},{4,6},{5,7},{6,4},{7,5},{8,10},{9,11},{10,... | collective-permute-start | bytes 196616 | tf_op jit(solution)/shard_map/ppermute | solution.py:308
  30.4 5.3 %collective-permute-start.2 = (f32[64,256]{1,0:T(8,128)S(1)}, f32[64,256]{1,0:T(8,128)S(1)}, u32[]{:S(2)}, u32[]{:S(2)}) collective-permute-start(f32[64,256]{1,0:T(8,128)S(1)} %add.116), channel_id=1, source_target_pairs={{0,4},{1,5},{2,6},{3,7},{4,0},{5,1},{6,2},{7,3},{8,12},{9,13},{10,... | collective-permute-start | bytes 196616 | tf_op jit(solution)/shard_map/ppermute | solution.py:308
  44.4 14.9 %collective-permute-start.4 = (f32[64,2048]{1,0:T(8,128)}, f32[64,2048]{1,0:T(8,128)}, u32[]{:S(2)}, u32[]{:S(2)}) collective-permute-start(f32[64,2048]{1,0:T(8,128)} %get-tuple-element.45), channel_id=1, source_target_pairs={{0,8},{8,0},{16,24},{24,16},{1,9},{9,1},{17,25},{25,17},{2,10},{10... | collective-permute-start | bytes 1572872 | tf_op jit(solution)/shard_map/ppermute | solution.py:308
  46.1 16.9 %collective-permute-start.9 = (f32[64,2048]{1,0:T(8,128)S(1)}, f32[64,2048]{1,0:T(8,128)}, u32[]{:S(2)}, u32[]{:S(2)}) collective-permute-start(f32[64,2048]{1,0:T(8,128)S(1)} %get-tuple-element.49), channel_id=1, source_target_pairs={{0,16},{8,24},{16,0},{24,8},{1,17},{9,25},{17,1},{25,9},{2,18},{10... | collective-permute-start | bytes 1572872 | tf_op jit(solution)/shard_map/ppermute | solution.py:308
  56.1 15.0 %collective-permute-start.3 = (f32[64,2048]{1,0:T(8,128)S(1)}, f32[64,2048]{1,0:T(8,128)}, u32[]{:S(2)}, u32[]{:S(2)}) collective-permute-start(f32[64,2048]{1,0:T(8,128)S(1)} %get-tuple-element.43), channel_id=1, source_target_pairs={{0,8},{8,0},{16,24},{24,16},{1,9},{9,1},{17,25},{25,17},{2,10},{10... | collective-permute-start | bytes 1572872 | tf_op jit(solution)/shard_map/ppermute | solution.py:308
  56.7 15.0 %collective-permute-start.8 = (f32[64,2048]{1,0:T(8,128)S(1)}, f32[64,2048]{1,0:T(8,128)}, u32[]{:S(2)}, u32[]{:S(2)}) collective-permute-start(f32[64,2048]{1,0:T(8,128)S(1)} %get-tuple-element.47), channel_id=1, source_target_pairs={{0,16},{8,24},{16,0},{24,8},{1,17},{9,25},{17,1},{25,9},{2,18},{10... | collective-permute-start | bytes 1572872 | tf_op jit(solution)/shard_map/ppermute | solution.py:308
  61.3 18.8 %collective-permute-start.5 = (f32[64,2048]{1,0:T(8,128)}, f32[64,2048]{1,0:T(8,128)}, u32[]{:S(2)}, u32[]{:S(2)}) collective-permute-start(f32[64,2048]{1,0:T(8,128)} %add.119), channel_id=1, source_target_pairs={{0,16},{8,24},{16,0},{24,8},{1,17},{9,25},{17,1},{25,9},{2,18},{10... | collective-permute-start | bytes 1572872 | tf_op jit(solution)/shard_map/ppermute | solution.py:308
  64.1 16.0 %collective-permute-start.10 = (f32[64,2048]{1,0:T(8,128)S(1)}, f32[64,2048]{1,0:T(8,128)S(1)}, u32[]{:S(2)}, u32[]{:S(2)}) collective-permute-start(f32[64,2048]{1,0:T(8,128)S(1)} %add.122), channel_id=1, source_target_pairs={{0,8},{8,0},{16,24},{24,16},{1,9},{9,1},{17,25},{25,17},{2,10},{10... | collective-permute-start | bytes 1572872 | tf_op jit(solution)/shard_map/ppermute | solution.py:308
  83.1 14.9 %collective-permute-start.11 = (f32[64,2048]{1,0:T(8,128)S(1)}, f32[64,2048]{1,0:T(8,128)S(1)}, u32[]{:S(2)}, u32[]{:S(2)}) collective-permute-start(f32[64,2048]{1,0:T(8,128)S(1)} %get-tuple-element.74.refs_1_), channel_id=1, source_target_pairs={{0,8},{8,0},{16,24},{24,16},{1,9},{9,1},{17,25},{25,17},{2,10},{10... | collective-permute-start | bytes 1572872 | tf_op jit(solution)/shard_map/ppermute | solution.py:308
  84.0 15.5 %collective-permute-start.6 = (f32[64,2048]{1,0:T(8,128)S(1)}, f32[64,2048]{1,0:T(8,128)S(1)}, u32[]{:S(2)}, u32[]{:S(2)}) collective-permute-start(f32[64,2048]{1,0:T(8,128)S(1)} %get-tuple-element.75.refs_0_), channel_id=1, source_target_pairs={{0,16},{8,24},{16,0},{24,8},{1,17},{9,25},{17,1},{25,9},{2,18},{10... | collective-permute-start | bytes 1572872 | tf_op jit(solution)/shard_map/ppermute | solution.py:308
  85.2 24.3 %collective-permute-start.13 = (f32[64,2048]{1,0:T(8,128)S(1)}, f32[64,2048]{1,0:T(8,128)S(1)}, u32[]{:S(2)}, u32[]{:S(2)}) collective-permute-start(f32[64,2048]{1,0:T(8,128)S(1)} %get-tuple-element.75.refs_0_), channel_id=1, source_target_pairs={{0,8},{8,0},{16,24},{24,16},{1,9},{9,1},{17,25},{25,17},{2,10},{10... | collective-permute-start | bytes 1572872 | tf_op jit(solution)/shard_map/ppermute | solution.py:308
  86.7 23.5 %collective-permute-start.14 = (f32[64,2048]{1,0:T(8,128)S(1)}, f32[64,2048]{1,0:T(8,128)S(1)}, u32[]{:S(2)}, u32[]{:S(2)}) collective-permute-start(f32[64,2048]{1,0:T(8,128)S(1)} %get-tuple-element.74.refs_1_), channel_id=1, source_target_pairs={{0,16},{8,24},{16,0},{24,8},{1,17},{9,25},{17,1},{25,9},{2,18},{10... | collective-permute-start | bytes 1572872 | tf_op jit(solution)/shard_map/ppermute | solution.py:308
  98.0 19.7 %collective-permute-start.12 = (f32[64,2048]{1,0:T(8,128)S(1)}, f32[64,2048]{1,0:T(8,128)}, u32[]{:S(2)}, u32[]{:S(2)}) collective-permute-start(f32[64,2048]{1,0:T(8,128)S(1)} %collective-permute-done.11.refs_1_), channel_id=1, source_target_pairs={{0,16},{8,24},{16,0},{24,8},{1,17},{9,25},{17,1},{25,9},{2,18},{10... | collective-permute-start | bytes 1572872 | tf_op jit(solution)/shard_map/ppermute | solution.py:308
  99.5 18.2 %collective-permute-start.7 = (f32[64,2048]{1,0:T(8,128)S(1)}, f32[64,2048]{1,0:T(8,128)}, u32[]{:S(2)}, u32[]{:S(2)}) collective-permute-start(f32[64,2048]{1,0:T(8,128)S(1)} %collective-permute-done.6.refs_0_), channel_id=1, source_target_pairs={{0,8},{8,0},{16,24},{24,16},{1,9},{9,1},{17,25},{25,17},{2,10},{10... | collective-permute-start | bytes 1572872 | tf_op jit(solution)/shard_map/ppermute | solution.py:308
  122.4 4.9 %collective-permute-start.16 = (f32[64,384]{1,0:T(8,128)S(1)}, f32[64,384]{1,0:T(8,128)S(1)}, u32[]{:S(2)}, u32[]{:S(2)}) collective-permute-start(f32[64,384]{1,0:T(8,128)S(1)} %add.123), channel_id=1, source_target_pairs={{0,2},{1,3},{2,0},{3,1},{4,6},{5,7},{6,4},{7,5},{8,10},{9,11},{10,... | collective-permute-start | bytes 294920 | tf_op jit(solution)/shard_map/ppermute | solution.py:308
  127.4 7.6 %collective-permute-start.17 = (f32[64,384]{1,0:T(8,128)S(1)}, f32[64,384]{1,0:T(8,128)S(1)}, u32[]{:S(2)}, u32[]{:S(2)}) collective-permute-start(f32[64,384]{1,0:T(8,128)S(1)} %add.124), channel_id=1, source_target_pairs={{0,4},{1,5},{2,6},{3,7},{4,0},{5,1},{6,2},{7,3},{8,12},{9,13},{10,... | collective-permute-start | bytes 294920 | tf_op jit(solution)/shard_map/ppermute | solution.py:308
  136.5 14.9 %collective-permute-start.22 = (f32[64,2048]{1,0:T(8,128)S(1)}, f32[64,2048]{1,0:T(8,128)S(1)}, u32[]{:S(2)}, u32[]{:S(2)}) collective-permute-start(f32[64,2048]{1,0:T(8,128)S(1)} %get-tuple-element.62), channel_id=1, source_target_pairs={{0,16},{8,24},{16,0},{24,8},{1,17},{9,25},{17,1},{25,9},{2,18},{10... | collective-permute-start | bytes 1572872 | tf_op jit(solution)/shard_map/ppermute | solution.py:308
  138.2 14.9 %collective-permute-start.20 = (f32[64,2048]{1,0:T(8,128)S(1)}, f32[64,2048]{1,0:T(8,128)S(1)}, u32[]{:S(2)}, u32[]{:S(2)}) collective-permute-start(f32[64,2048]{1,0:T(8,128)S(1)} %get-tuple-element.60), channel_id=1, source_target_pairs={{0,8},{8,0},{16,24},{24,16},{1,9},{9,1},{17,25},{25,17},{2,10},{10... | collective-permute-start | bytes 1572872 | tf_op jit(solution)/shard_map/ppermute | solution.py:308
  141.3 21.3 %collective-permute-start.19 = (f32[64,2048]{1,0:T(8,128)S(1)}, f32[64,2048]{1,0:T(8,128)S(1)}, u32[]{:S(2)}, u32[]{:S(2)}) collective-permute-start(f32[64,2048]{1,0:T(8,128)S(1)} %get-tuple-element.58), channel_id=1, source_target_pairs={{0,16},{8,24},{16,0},{24,8},{1,17},{9,25},{17,1},{25,9},{2,18},{10... | collective-permute-start | bytes 1572872 | tf_op jit(solution)/shard_map/ppermute | solution.py:308
  141.7 22.6 %collective-permute-start.18 = (f32[64,2048]{1,0:T(8,128)S(1)}, f32[64,2048]{1,0:T(8,128)S(1)}, u32[]{:S(2)}, u32[]{:S(2)}) collective-permute-start(f32[64,2048]{1,0:T(8,128)S(1)} %get-tuple-element.56), channel_id=1, source_target_pairs={{0,8},{8,0},{16,24},{24,16},{1,9},{9,1},{17,25},{25,17},{2,10},{10... | collective-permute-start | bytes 1572872 | tf_op jit(solution)/shard_map/ppermute | solution.py:308
  151.5 20.7 %collective-permute-start.23 = (f32[64,2048]{1,0:T(8,128)S(1)}, f32[64,2048]{1,0:T(8,128)S(1)}, u32[]{:S(2)}, u32[]{:S(2)}) collective-permute-start(f32[64,2048]{1,0:T(8,128)S(1)} %add.129), channel_id=1, source_target_pairs={{0,8},{8,0},{16,24},{24,16},{1,9},{9,1},{17,25},{25,17},{2,10},{10... | collective-permute-start | bytes 1572872 | tf_op jit(solution)/shard_map/ppermute | solution.py:308
  153.1 19.1 %collective-permute-start.21 = (f32[64,2048]{1,0:T(8,128)S(1)}, f32[64,2048]{1,0:T(8,128)S(1)}, u32[]{:S(2)}, u32[]{:S(2)}) collective-permute-start(f32[64,2048]{1,0:T(8,128)S(1)} %add.128), channel_id=1, source_target_pairs={{0,16},{8,24},{16,0},{24,8},{1,17},{9,25},{17,1},{25,9},{2,18},{10... | collective-permute-start | bytes 1572872 | tf_op jit(solution)/shard_map/ppermute | solution.py:308
  174.3 15.1 %collective-permute-start.27 = (f32[64,2048]{1,0:T(8,128)S(1)}, f32[64,2048]{1,0:T(8,128)S(1)}, u32[]{:S(2)}, u32[]{:S(2)}) collective-permute-start(f32[64,2048]{1,0:T(8,128)S(1)} %get-tuple-element.71.refs_0_), channel_id=1, source_target_pairs={{0,16},{8,24},{16,0},{24,8},{1,17},{9,25},{17,1},{25,9},{2,18},{10... | collective-permute-start | bytes 1572872 | tf_op jit(solution)/shard_map/ppermute | solution.py:308
  174.8 14.6 %collective-permute-start.28 = (f32[64,2048]{1,0:T(8,128)S(1)}, f32[64,2048]{1,0:T(8,128)S(1)}, u32[]{:S(2)}, u32[]{:S(2)}) collective-permute-start(f32[64,2048]{1,0:T(8,128)S(1)} %get-tuple-element.72.refs_1_), channel_id=1, source_target_pairs={{0,8},{8,0},{16,24},{24,16},{1,9},{9,1},{17,25},{25,17},{2,10},{10... | collective-permute-start | bytes 1572872 | tf_op jit(solution)/shard_map/ppermute | solution.py:308
  176.4 10.6 %collective-permute-start.24 = (f32[64,64]{1,0:T(8,128)S(1)}, f32[64,64]{1,0:T(8,128)S(1)}, u32[]{:S(2)}, u32[]{:S(2)}) collective-permute-start(f32[64,64]{1,0:T(8,128)S(1)} %get-tuple-element.63), channel_id=1, source_target_pairs={{0,8},{8,0},{16,24},{24,16},{1,9},{9,1},{17,25},{25,17},{2,10},{10... | collective-permute-start | bytes 49160 | tf_op jit(solution)/shard_map/ppermute | solution.py:308
  176.9 10.1 %collective-permute-start.25 = (f32[64,64]{1,0:T(8,128)S(1)}, f32[64,64]{1,0:T(8,128)S(1)}, u32[]{:S(2)}, u32[]{:S(2)}) collective-permute-start(f32[64,64]{1,0:T(8,128)S(1)} %get-tuple-element.63), channel_id=1, source_target_pairs={{0,16},{8,24},{16,0},{24,8},{1,17},{9,25},{17,1},{25,9},{2,18},{10... | collective-permute-start | bytes 49160 | tf_op jit(solution)/shard_map/ppermute | solution.py:308
  178.4 11.0 %collective-permute-start.26 = (f32[64,64]{1,0:T(8,128)S(1)}, f32[64,64]{1,0:T(8,128)S(1)}, u32[]{:S(2)}, u32[]{:S(2)}) collective-permute-start(f32[64,64]{1,0:T(8,128)S(1)} %get-tuple-element.63), channel_id=1, source_target_pairs={{0,24},{8,16},{16,8},{24,0},{1,25},{9,17},{17,9},{25,1},{2,26},{10... | collective-permute-start | bytes 49160 | tf_op jit(solution)/shard_map/ppermute | solution.py:308
  189.4 22.2 %collective-permute-start.34 = (f32[64,2048]{1,0:T(8,128)S(1)}, f32[64,2048]{1,0:T(8,128)}, u32[]{:S(2)}, u32[]{:S(2)}) collective-permute-start(f32[64,2048]{1,0:T(8,128)S(1)} %get-tuple-element.71.refs_0_), channel_id=1, source_target_pairs={{0,8},{8,0},{16,24},{24,16},{1,9},{9,1},{17,25},{25,17},{2,10},{10... | collective-permute-start | bytes 1572872 | tf_op jit(solution)/shard_map/ppermute | solution.py:308
  191.1 20.5 %collective-permute-start.35 = (f32[64,2048]{1,0:T(8,128)S(1)}, f32[64,2048]{1,0:T(8,128)}, u32[]{:S(2)}, u32[]{:S(2)}) collective-permute-start(f32[64,2048]{1,0:T(8,128)S(1)} %get-tuple-element.72.refs_1_), channel_id=1, source_target_pairs={{0,16},{8,24},{16,0},{24,8},{1,17},{9,25},{17,1},{25,9},{2,18},{10... | collective-permute-start | bytes 1572872 | tf_op jit(solution)/shard_map/ppermute | solution.py:308
  191.1 26.5 %collective-permute-start.32 = (f32[64,2048]{1,0:T(8,128)S(1)}, f32[64,2048]{1,0:T(8,128)S(1)}, u32[]{:S(2)}, u32[]{:S(2)}) collective-permute-start(f32[64,2048]{1,0:T(8,128)S(1)} %collective-permute-done.27.refs_2_), channel_id=1, source_target_pairs={{0,8},{8,0},{16,24},{24,16},{1,9},{9,1},{17,25},{25,17},{2,10},{10... | collective-permute-start | bytes 1572872 | tf_op jit(solution)/shard_map/ppermute | solution.py:308
  191.5 26.1 %collective-permute-start.33 = (f32[64,2048]{1,0:T(8,128)S(1)}, f32[64,2048]{1,0:T(8,128)S(1)}, u32[]{:S(2)}, u32[]{:S(2)}) collective-permute-start(f32[64,2048]{1,0:T(8,128)S(1)} %collective-permute-done.28.refs_3_), channel_id=1, source_target_pairs={{0,16},{8,24},{16,0},{24,8},{1,17},{9,25},{17,1},{25,9},{2,18},{10... | collective-permute-start | bytes 1572872 | tf_op jit(solution)/shard_map/ppermute | solution.py:308
  199.1 5.6 %collective-permute-start.31 = (f32[64,64]{1,0:T(8,128)S(1)}, f32[64,64]{1,0:T(8,128)S(1)}, u32[]{:S(2)}, u32[]{:S(2)}) collective-permute-start(f32[64,64]{1,0:T(8,128)S(1)} %add.134), channel_id=1, source_target_pairs={{0,4},{1,5},{2,6},{3,7},{4,0},{5,1},{6,2},{7,3},{8,12},{9,13},{10,... | collective-permute-start | bytes 49160 | tf_op jit(solution)/shard_map/ppermute | solution.py:308
  (15 other events, 39.0 us)

commit v3 on v2

v3 whole, which is shorter than its diff:
```python
import functools

import jax
import jax.numpy as jnp
from jax import lax
from jax.experimental import pallas as pl
from jax.experimental.pallas import tpu as pltpu
from jax.sharding import PartitionSpec as P

F32 = jnp.float32
BF16 = jnp.bfloat16
STEP = 1024
CHUNK = 1024
SLOTS = 4
ROWS = 16
GROUP = 4
VMEM_LIMIT = 24 * 1024 * 1024
VMEM = pl.BlockSpec(memory_space=pltpu.VMEM)
HBM = pl.BlockSpec(memory_space=pltpu.HBM)
NEAR, FAR = ("pass_on", "away_second"), ("away_first",)
PARAMS = pltpu.CompilerParams(vmem_limit_bytes=VMEM_LIMIT)


def halves(x):
    high = x.astype(BF16)
    return high, (x - high.astype(F32)).astype(BF16)


def thirds(x):
    high = x.astype(BF16)
    rest = x - high.astype(F32)
    middle = rest.astype(BF16)
    low = (rest - middle.astype(F32)).astype(BF16)
    return jnp.concatenate([high, middle, low], axis=0)


def put_halves(high, low, span, source):
    for row in range(0, source.shape[0], ROWS):
        here = pl.ds(row, ROWS)
        high[here, span], low[here, span] = halves(source[here, :])


def put_thirds(target, source, weights=None):
    size = source.shape[0]
    for row in range(0, size, ROWS):
        part = source[pl.ds(row, ROWS), :]
        part = thirds(part if weights is None else part * weights)
        for third in range(3):
            target[pl.ds(third * size + row, ROWS), :] = part[third * ROWS : (third + 1) * ROWS]


def dot_nt(a, b):
    return lax.dot_general(a, b, (((1,), (1,)), ((), ())), preferred_element_type=F32)


def dot_nn(a, b):
    return lax.dot_general(a, b, (((1,), (0,)), ((), ())), preferred_element_type=F32)


def fold_rows(x, size):
    return (x[2 * size :] + x[size : 2 * size]) + x[:size]


def cost(flops, nbytes):
    return pl.CostEstimate(flops=int(flops), bytes_accessed=int(nbytes), transcendentals=0)


def array(*shape, dtype=F32):
    return jax.ShapeDtypeStruct(shape, dtype)


def columns(place, unit, start=0, width=None):
    return pl.ds(pl.multiple_of(place * unit + start, STEP), unit if width is None else width)


def unit_places():
    col = lax.axis_index("col")
    i, j = lax.rem(col, 2), lax.div(col, 2)
    k, m = 1 - i, 1 - j
    return {
        "own": (2 * i + j, 4 + 2 * j + i),
        "pass_on": (2 * i + m, 4 + 2 * j + k),
        "away_first": (2 * k + m, 4 + 2 * m + k),
        "away_second": (2 * k + j, 4 + 2 * m + i),
    }


def places_of(*names):
    places = unit_places()
    return [place for name in names for place in places[name]]


def first_kernel(
    total, locked, vectors, mass, out, high, low, mass_out, here_a, here_b, held_buf, new_buf, pieces, acc, sems, more_sems
):
    held, rows = locked.shape
    unit = here_a.shape[1]
    count = rows // CHUNK

    def copies(index):
        span, slot = pl.ds(index * CHUNK, CHUNK), index % SLOTS
        return (
            pltpu.make_async_copy(vectors.at[:, span], new_buf.at[slot], sems.at[0, slot]),
            pltpu.make_async_copy(locked.at[:, span], held_buf.at[slot], sems.at[1, slot]),
        )

    mass_copy = pltpu.make_async_copy(mass, mass_out, more_sems.at[0])
    mass_copy.start()
    for index in range(SLOTS - 1):
        for copy in copies(index):
            copy.start()
    places = places_of("own")
    own_copies = [
        pltpu.make_async_copy(vectors.at[:, columns(place, unit)], here, more_sems.at[1 + which])
        for which, (place, here) in enumerate(zip(places, (here_a, here_b)))
    ]
    mass_copy.wait()
    for index in range(count + 1):
        if index < count:
            if index + SLOTS - 1 < count:
                for copy in copies(index + SLOTS - 1):
                    copy.start()
            if index == count // 2:
                for copy in own_copies:
                    copy.start()
            for copy in copies(index):
                copy.wait()
        if index > 0:
            span = pl.ds((index - 1) * CHUNK, CHUNK)
            left = jnp.concatenate([high[:, span], low[:, span]], axis=0)
            term = dot_nt(left, pieces[(index - 1) % 2])
            if index == 1:
                acc[...] = term
            else:
                acc[...] += term
        if index < count:
            span, slot = pl.ds(index * CHUNK, CHUNK), index % SLOTS
            put_thirds(pieces.at[index % 2], new_buf.at[slot], mass_out[:, span])
            put_halves(high, low, span, held_buf.at[slot])
    for copy in own_copies:
        copy.wait()
    out[...] = fold_rows((acc[:held] + acc[held:]).T, out.shape[0]) * (1.0 / total)


def first_coefficients(locked, vectors, mass, unit, total):
    (held, rows), new = locked.shape, vectors.shape[0]
    in_hbm = [pltpu.with_memory_space_constraint(x, pltpu.HBM) for x in (locked, vectors, mass)]
    return pl.pallas_call(
        functools.partial(first_kernel, total),
        out_shape=[
            array(new, held),
            array(held, rows, dtype=BF16),
            array(held, rows, dtype=BF16),
            array(1, rows),
            array(new, unit),
            array(new, unit),
        ],
        in_specs=[HBM] * 3,
        out_specs=[VMEM] * 6,
        scratch_shapes=[
            pltpu.VMEM((SLOTS, held, CHUNK), F32),
            pltpu.VMEM((SLOTS, new, CHUNK), F32),
            pltpu.VMEM((2, 3 * new, CHUNK), BF16),
            pltpu.VMEM((2 * held, 3 * new), F32),
            pltpu.SemaphoreType.DMA((2, SLOTS)),
            pltpu.SemaphoreType.DMA((3,)),
        ],
        compiler_params=PARAMS,
        cost_estimate=cost(12 * held * new * rows, 8 * held * rows),
    )(*in_hbm)


def fold_gram(x, size):
    part = fold_rows(x, size)
    return (part[:, 2 * size :] + part[:, size : 2 * size]) + part[:, :size]


def second_kernel(count, total, mode, high, low, mass, *refs):
    blocks, rest = refs[:count], refs[count:]
    new, unit = blocks[0].shape
    held = high.shape[0]
    rest, (acc, plain, weighted) = rest[:-3], rest[-3:]
    if mode == "own":
        out, grams = rest
    elif mode == "near":
        base, out, grams = rest
    else:
        base, own_grams, near_grams, out, grams = rest
    parts = {"own": ("own",), "near": NEAR, "far": FAR + ("own",) + NEAR}[mode]
    ids = places_of(*parts)
    for place in range(count):
        span = columns(ids[place], unit)
        put_thirds(weighted.at[place], blocks[place], mass[:, span])
        put_thirds(plain.at[place], blocks[place])
        left = jnp.concatenate([high[:, span], low[:, span], plain[place]], axis=0)
        term = dot_nt(left, weighted[place])
        grams[ids[place] if mode == "far" else place] = fold_gram(term[2 * held :], new)
        if place == 0:
            acc[...] = term[: 2 * held]
        else:
            acc[...] += term[: 2 * held]
    second = fold_rows((acc[:held] + acc[held:]).T, new)
    if mode != "own":
        second = second + base[...]
    if mode != "far":
        out[...] = second
        return
    for place in range(2):
        grams[ids[2 + place]] = own_grams[place]
    for place in range(4):
        grams[ids[4 + place]] = near_grams[place]
    gram = grams[0]
    for place in range(1, 8):
        gram = gram + grams[place]
    out[...] = jnp.concatenate([second, gram, jnp.zeros_like(gram)], axis=1) * (1.0 / total)


def second_coefficients(mode, high, low, mass, blocks, total, *others):
    new, unit = blocks[0].shape
    held, count = high.shape[0], len(blocks)
    pieces = pltpu.VMEM((count, 3 * new, unit), BF16)
    scratch = [pltpu.VMEM((2 * held, 3 * new), F32), pieces, pieces]
    if mode == "far":
        shapes = [array(new, held + 2 * new)]
        scratch.insert(0, pltpu.VMEM((8, new, new), F32))
    else:
        shapes = [array(new, held), array(count, new, new)]
    return pl.pallas_call(
        functools.partial(second_kernel, count, total, mode),
        out_shape=shapes,
        in_specs=[VMEM] * (3 + count + len(others)),
        out_specs=[VMEM] * len(shapes),
        scratch_shapes=scratch,
        compiler_params=PARAMS,
        cost_estimate=cost(14 * held * new * count * unit, 4 * (held + new) * count * unit),
    )(high, low, mass, *blocks, *others)


def corrections_kernel(names, bases, coef, high, low, *refs):
    base, outs = refs[:bases], refs[bases:]
    new, unit = outs[0].shape
    held = high.shape[0]
    pieces = thirds(coef[:, :held])
    pieces = jnp.concatenate([pieces, pieces], axis=1)
    places = places_of(*names)
    for which, place in enumerate(places):
        taken_off = which - (len(places) - bases)
        for start in range(0, unit, STEP):
            span, here = columns(place, unit, start, STEP), pl.ds(start, STEP)
            term = dot_nn(pieces, jnp.concatenate([high[:, span], low[:, span]], axis=0))
            term = fold_rows(term, new)
            outs[which][:, here] = base[taken_off][:, here] - term if taken_off >= 0 else term


def corrections(names, coef, high, low, unit, base=()):
    new, held, count = coef.shape[0], high.shape[0], 2 * len(names)
    return pl.pallas_call(
        functools.partial(corrections_kernel, names, len(base)),
        out_shape=[array(new, unit)] * count,
        in_specs=[VMEM] * (3 + len(base)),
        out_specs=[VMEM] * count,
        compiler_params=PARAMS,
        cost_estimate=cost(12 * held * new * count * unit, 4 * (held + new) * count * unit),
    )(coef, high, low, *base)


def take_off_kernel(*refs):
    for place in range(2):
        refs[6 + place][...] = refs[place][...] - refs[2 + place][...] - refs[4 + place][...]


def eliminate(gram):
    size = gram.shape[0]
    shape = (size, 2 * size)
    rows = lax.broadcasted_iota(jnp.int32, shape, 0)
    lanes = lax.broadcasted_iota(jnp.int32, shape, 1)
    eye = (rows[:, :size] == lanes[:, :size]).astype(F32)
    work = jnp.concatenate([gram, eye], axis=1)
    for start in range(0, size, GROUP):
        group = range(start, start + GROUP)
        column = {k: jnp.broadcast_to(work[:, k : k + 1], shape) for k in group}
        line = {k: work[k : k + 1, :] for k in group}
        for k in group:
            inverse = 1.0 / column[k][k : k + 1, :]
            scaled = line[k] * inverse
            for later in range(k + 1, start + GROUP):
                line[later] = line[later] - column[k][later : later + 1, :] * scaled
                column[later] = column[later] - column[k] * (column[later][k : k + 1, :] * inverse)
            work = work - jnp.where(rows > k, column[k], 0.0) * scaled
    pivots = jnp.sum(jnp.where(lanes == rows, work, 0.0), axis=1, keepdims=True)
    scale = lax.rsqrt(pivots)
    work = work * (scale * (1.5 - 0.5 * pivots * scale * scale))
    upper = jnp.where(lanes >= rows, work, 0.0)[:, :size]
    return upper, work[:, size:]


def spread(matrix):
    pieces = thirds(matrix)
    return jnp.concatenate([pieces, pieces, pieces], axis=1)


def apply_left(spread_matrix, block):
    return fold_rows(dot_nn(spread_matrix, thirds(block)), block.shape[0])


def gram_of(block, mass):
    size = block.shape[0]
    return fold_gram(dot_nt(thirds(block * mass), thirds(block)), size)


def factor_kernel(both, upper_out, inverse_out):
    size = upper_out.shape[0]
    held = both.shape[1] - 2 * size
    upper_out[...], inverse_out[...] = eliminate(both[:, held : held + size])


def middle_kernel(total, mass, inverse, *refs):
    ins, outs = refs[:6], refs[6:]
    new, unit = outs[0].shape
    left = spread(inverse[...])
    places = places_of("own")
    acc = jnp.zeros((new, new), F32)
    for which, place in enumerate(places):
        for start in range(0, unit, STEP):
            span = pl.ds(start, STEP)
            projected = ins[which][:, span] - ins[2 + which][:, span] - ins[4 + which][:, span]
            middle = apply_left(left, projected)
            outs[which][:, span] = middle
            acc = acc + gram_of(middle, mass[:, columns(place, unit, start, STEP)])
    outs[2][...] = acc * (1.0 / total)


def last_kernel(gram, upper_one, factor_out, inverse_out):
    upper, inverse = eliminate(gram[...])
    factor_out[...] = jnp.dot(
        upper, upper_one[...], precision=lax.Precision.HIGHEST, preferred_element_type=F32
    )
    inverse_out[...] = inverse


def finish_kernel(names, inverse, *refs):
    count = 2 * len(names)
    blocks, (out, buf, sems) = refs[:count], refs[-3:]
    unit = blocks[0].shape[1]
    left = spread(inverse[...])
    copies = []
    for which, place in enumerate(places_of(*names)):
        for start in range(0, unit, STEP):
            span = pl.ds(start, STEP)
            buf[which, :, span] = apply_left(left, blocks[which][:, span])
        copy = pltpu.make_async_copy(buf.at[which], out.at[:, columns(place, unit)], sems.at[which])
        copy.start()
        copies.append(copy)
    for copy in copies:
        copy.wait()


def finish(names, inverse, blocks, rows, target=None):
    new, unit = blocks[0].shape
    count = len(blocks)
    extra = [] if target is None else [target]
    return pl.pallas_call(
        functools.partial(finish_kernel, names),
        out_shape=array(new, rows),
        in_specs=[VMEM] * (1 + count) + [HBM] * len(extra),
        out_specs=HBM,
        scratch_shapes=[pltpu.VMEM((count, new, unit), F32), pltpu.SemaphoreType.DMA((count,))],
        input_output_aliases={} if target is None else {1 + count: 0},
        compiler_params=PARAMS,
        cost_estimate=cost(18 * new * new * count * unit, 8 * new * count * unit),
    )(inverse, *blocks, *extra)


def flip(x, axis, bit):
    size = lax.axis_size(axis)
    return lax.ppermute(x, axis, [(i, i ^ bit) for i in range(size)])


def sum_over(x, axis):
    size = lax.axis_size(axis)
    bit = 1
    while bit < size:
        x = x + flip(x, axis, bit)
        bit *= 2
    return x


def sum_of_four(x, axis, bit=1):
    one, two, three = (flip(x, axis, n * bit) for n in (1, 2, 3))
    return (x + one) + (two + three)


def sum_by_fours(x, axis):
    size = lax.axis_size(axis)
    x = x + flip(x, axis, 1)
    bit = 2
    while bit < size:
        if 2 * bit < size:
            x = sum_of_four(x, axis, bit)
        else:
            x = x + flip(x, axis, bit)
        bit *= 4
    return x


def local(locked, vectors, mass):
    new, rows = vectors.shape
    total = rows * lax.axis_size("row")
    unit = rows // 8
    first, high, low, mass, *here = first_coefficients(locked, vectors, mass.reshape(1, rows), unit, total)

    def scatter_sum(coef, base):
        a1, b1 = corrections(("away_first",), coef, high, low, unit)
        ra1, rb1 = flip(a1, "col", 1), flip(b1, "col", 2)
        a2, b2 = corrections(("away_second",), coef, high, low, unit)
        ra2, rb2 = flip(a2, "col", 1), flip(b2, "col", 2)
        a3, b3, a4, b4 = corrections(("pass_on", "own"), coef, high, low, unit, base)
        ra3, rb3 = flip(a3 + ra1, "col", 2), flip(b3 + rb1, "col", 1)
        return a4, b4, ra2, rb2, ra3, rb3

    first = sum_over(first, "row")
    once = pl.pallas_call(
        take_off_kernel,
        out_shape=[array(new, unit)] * 2,
        in_specs=[VMEM] * 6,
        out_specs=[VMEM] * 2,
        compiler_params=PARAMS,
        cost_estimate=cost(6 * new * unit, 32 * new * unit),
    )(*scatter_sum(first, here))
    a, b = once
    ay, bx = flip(a, "col", 2), flip(b, "col", 1)
    ax, by = flip(a, "col", 1), flip(b, "col", 2)
    far = flip(ay, "col", 1), flip(bx, "col", 2)
    second, grams = second_coefficients("own", high, low, mass, once, total)
    second, more = second_coefficients("near", high, low, mass, (ay, bx, ax, by), total, second)
    (second,) = second_coefficients("far", high, low, mass, far, total, second, grams, more)
    second = sum_over(second, "row")
    parts = scatter_sum(second, once)

    upper, inverse = pl.pallas_call(
        factor_kernel,
        out_shape=[array(new, new)] * 2,
        in_specs=[VMEM],
        out_specs=[VMEM] * 2,
        compiler_params=PARAMS,
        cost_estimate=cost(1e6, 1e5),
    )(second)
    a, b, gram = pl.pallas_call(
        functools.partial(middle_kernel, total),
        out_shape=[array(new, unit)] * 2 + [array(new, new)],
        in_specs=[VMEM] * 8,
        out_specs=[VMEM] * 3,
        compiler_params=PARAMS,
        cost_estimate=cost(36 * new * new * 2 * unit, 24 * new * unit),
    )(mass, inverse, *parts)
    ay, bx = flip(a, "col", 2), flip(b, "col", 1)
    ax, by = flip(a, "col", 1), flip(b, "col", 2)
    gram = sum_of_four(sum_by_fours(gram, "row"), "col")
    gram, ay, bx = lax.optimization_barrier((gram, ay, bx))
    far = flip(ay, "col", 1), flip(bx, "col", 2)
    factor, inverse = pl.pallas_call(
        last_kernel,
        out_shape=[array(new, new)] * 2,
        in_specs=[VMEM] * 2,
        out_specs=[VMEM] * 2,
        compiler_params=PARAMS,
        cost_estimate=cost(5e9, 1e5),
    )(gram, upper)
    appended = finish(("own",) + NEAR, inverse, (a, b, ay, bx, ax, by), rows)
    appended = finish(FAR, inverse, far, rows, appended)
    return (appended, factor)


def solution(mesh):
    return jax.shard_map(
        local,
        mesh=mesh,
        in_specs=(P("col", "row"), P(None, "row"), P("row")),
        out_specs=(P(None, "row"), P()),
        check_vma=False,
    )
```

time: 220 us -> 196 us (0.89)
  waiting for transfers between devices: 77 us -> 108 us
  local copies, waits for them, and re-layouts: 30.8 us -> 0 us
  Pallas kernels: 57.7 us -> 40.1 us
  other arithmetic: 5.96 us -> 0.32 us
    unnamed x22 -> x0, local copies, waits for them, and re-layouts: 30.7 us -> none
    ppermute x36 -> x37, waiting for transfers between devices: 77 us -> 108 us  [flip(): return lax.ppermute(x, axis, [(i, i ^ bit) for i in range(size)])]
    pallas_call x8 -> x9, Pallas kernels: 19.5 us -> 11.5 us  [the longest x6 7.65 us: corrections(): pl.pallas_call(functools.partial(corrections_kernel, names, len(base)), o...]
    pallas_call x1, Pallas kernels: 6.91 us -> 3.03 us  [local(): pl.pallas_call(last_kernel, out_shape=[array(new, new)] * 2, in_specs=[VM...]
    pallas_call x1, Pallas kernels: 6.17 us -> 2.33 us  [local(): pl.pallas_call(factor_kernel, out_shape=[array(new, new)] * 2, in_specs=[...]
    add x4, other arithmetic: 3.1 us -> 0.23 us  [scatter_sum(): ra3, rb3 = (flip(a3 + ra1, 'col', 2), flip(b3 + rb1, 'col', 1))]
    pallas_call x3, Pallas kernels: 9.65 us -> 7.07 us  [second_coefficients(): pl.pallas_call(functools.partial(second_kernel, count, total, mode), out_...]
    sub x3 -> x0, other arithmetic: 2.39 us -> none  [the longest x1 2.17 us: local(): once = (a - ra, b - rb)]
  transfers between devices with their start and end apart: 36 -> 37, of which waited for: 21 -> 24; matrix products, arithmetic and copies ran while one was open for 2% -> 0% of each run, Pallas kernels for 15% -> 9%
where the time goes in v3:
time: 196 us
  waiting for transfers between devices  108 us (55%)
  starting transfers between devices  46.8 us (24%)
  Pallas kernels  40.1 us (20%)
    ppermute x37, waiting for transfers between devices, flip(): return lax.ppermute(x, axis, [(i, i ^ bit) for i in range(size)])  108 us
    ppermute x37, starting transfers between devices, flip(): return lax.ppermute(x, axis, [(i, i ^ bit) for i in range(size)])  46.8 us
    pallas_call x1, Pallas kernels, first_coefficients(): pl.pallas_call(functools.partial(first_kernel, total), out_shape=[array(n...  14.8 us
    pallas_call x6, Pallas kernels, corrections(): pl.pallas_call(functools.partial(corrections_kernel, names, len(base)), o...  7.65 us
    pallas_call x3, Pallas kernels, second_coefficients(): pl.pallas_call(functools.partial(second_kernel, count, total, mode), out_...  7.07 us
  transfers between devices with their start and end apart: 37, of which 24 were waited for; matrix products, arithmetic and copies ran while one was open for 0% of the time, Pallas kernels for 9%

profile of v3, /device:TPU:0, one launch (start us, length us, event | category | flops | bytes accessed | tf_op | source)
XLA Modules:
  0.0 195.7 jit_solution(6005547481270831644)
XLA Ops:
  0.6 14.8 %shard_map.50 = (f32[64,256]{1,0:T(8,128)S(1)}, bf16[256,16384]{1,0:T(8,128)(2,1)S(1)}, bf16[256,16384]{1,0:T(8,128)(2,1)S(1)}, f32[1,16384]{1,0:T(1,128)S(1)}, ...) custom-call(f32[256,16384]{1,0:T(8,128)} %locked.1, f32[64,16384]{1,0:T(8,128)} %vectors.1, f32[1,16384]{1,0:T(1,128)} %bitcast.1), custom_call_target="tpu_custom_call" | custom-call | flops 3221225472 | bytes 33554432 | tf_op jit(solution)/shard_map/pallas_call | solution.py:148
  16.9 3.0 %collective-permute-start.1 = (f32[64,256]{1,0:T(8,128)S(1)}, f32[64,256]{1,0:T(8,128)S(1)}, u32[]{:S(2)}, u32[]{:S(2)}) collective-permute-start(f32[64,256]{1,0:T(8,128)S(1)} %add.51), channel_id=1, source_target_pairs={{0,2},{1,3},{2,0},{3,1},{4,6},{5,7},{6,4},{7,5},{8,10},{9,11},{10,... | collective-permute-start | bytes 196616 | tf_op jit(solution)/shard_map/ppermute | solution.py:376
  19.9 2.4 %collective-permute-done.1 = f32[64,256]{1,0:T(8,128)S(1)} collective-permute-done((f32[64,256]{1,0:T(8,128)S(1)}, f32[64,256]{1,0:T(8,128)S(1)}, u32[]{:S(2)}, u32[]{:S(2)}) %collective-permute-start.1) | collective-permute-done | bytes 65568 | tf_op jit(solution)/shard_map/ppermute | solution.py:376
  22.3 2.9 %collective-permute-start.2 = (f32[64,256]{1,0:T(8,128)S(1)}, f32[64,256]{1,0:T(8,128)S(1)}, u32[]{:S(2)}, u32[]{:S(2)}) collective-permute-start(f32[64,256]{1,0:T(8,128)S(1)} %add.52), channel_id=1, source_target_pairs={{0,4},{1,5},{2,6},{3,7},{4,0},{5,1},{6,2},{7,3},{8,12},{9,13},{10,... | collective-permute-start | bytes 196616 | tf_op jit(solution)/shard_map/ppermute | solution.py:376
  25.2 2.4 %collective-permute-done.2 = f32[64,256]{1,0:T(8,128)S(1)} collective-permute-done((f32[64,256]{1,0:T(8,128)S(1)}, f32[64,256]{1,0:T(8,128)S(1)}, u32[]{:S(2)}, u32[]{:S(2)}) %collective-permute-start.2) | collective-permute-done | bytes 65568 | tf_op jit(solution)/shard_map/ppermute | solution.py:376
  28.6 1.8 collective-permute-start.7
  33.8 1.8 shard_map.51
  35.6 7.9 %collective-permute-done.7 = f32[64,2048]{1,0:T(8,128)S(1)} collective-permute-done((f32[64,2048]{1,0:T(8,128)S(1)}, f32[64,2048]{1,0:T(8,128)S(1)}, u32[]{:S(2)}, u32[]{:S(2)}) %collective-permute-start.7) | collective-permute-done | bytes 524320 | tf_op jit(solution)/shard_map/ppermute | solution.py:376
  47.0 9.5 %collective-permute-done.3.refs_2_ = f32[64,2048]{1,0:T(8,128)S(1)} collective-permute-done((f32[64,2048]{1,0:T(8,128)S(1)}, f32[64,2048]{1,0:T(8,128)S(1)}, u32[]{:S(2)}, u32[]{:S(2)}) %collective-permute-start.3) | collective-permute-done | bytes 524320 | tf_op jit(solution)/shard_map/ppermute | solution.py:376
  56.5 7.8 %collective-permute-done.8.refs_5_ = f32[64,2048]{1,0:T(8,128)S(1)} collective-permute-done((f32[64,2048]{1,0:T(8,128)S(1)}, f32[64,2048]{1,0:T(8,128)S(1)}, u32[]{:S(2)}, u32[]{:S(2)}) %collective-permute-start.8) | collective-permute-done | bytes 524320 | tf_op jit(solution)/shard_map/ppermute | solution.py:376
  68.6 10.8 %collective-permute-done.9.refs_0_ = f32[64,2048]{1,0:T(8,128)S(1)} collective-permute-done((f32[64,2048]{1,0:T(8,128)S(1)}, f32[64,2048]{1,0:T(8,128)S(1)}, u32[]{:S(2)}, u32[]{:S(2)}) %collective-permute-start.9) | collective-permute-done | bytes 524320 | tf_op jit(solution)/shard_map/ppermute | solution.py:376
  81.4 1.8 shard_map.55
  83.2 8.2 %collective-permute-done.13.refs_2_ = f32[64,2048]{1,0:T(8,128)S(1)} collective-permute-done((f32[64,2048]{1,0:T(8,128)S(1)}, f32[64,2048]{1,0:T(8,128)S(1)}, u32[]{:S(2)}, u32[]{:S(2)}) %collective-permute-start.13) | collective-permute-done | bytes 524320 | tf_op jit(solution)/shard_map/ppermute | solution.py:376
  91.5 3.4 %shard_map.56 = (f32[64,256]{1,0:T(8,128)S(1)}, f32[4,64,64]{2,1,0:T(8,128)S(1)}) custom-call(bf16[256,16384]{1,0:T(8,128)(2,1)S(1)} %get-tuple-element.41.high, bf16[256,16384]{1,0:T(8,128)(2,1)S(1)} %get-tuple-element.42.low, f32[1,16384]{1,0:T(1,128)S(1)} %get-tuple-element.40.mass, f32[64,2048]{1,0:T(8,128)S(1)} %collective-permute-done.9.refs_0_, ...), custom_call_target="tpu_custom_call" | custom-call | flops 1879048192 | bytes 10485760 | tf_op jit(solution)/shard_map/pallas_call | solution.py:228
  94.9 3.8 %collective-permute-done.10.refs_0_ = f32[64,2048]{1,0:T(8,128)S(1)} collective-permute-done((f32[64,2048]{1,0:T(8,128)S(1)}, f32[64,2048]{1,0:T(8,128)S(1)}, u32[]{:S(2)}, u32[]{:S(2)}) %collective-permute-start.10) | collective-permute-done | bytes 524320 | tf_op jit(solution)/shard_map/ppermute | solution.py:376
  98.6 1.9 shard_map.57
  103.0 3.8 %collective-permute-done.16 = f32[64,384]{1,0:T(8,128)S(1)} collective-permute-done((f32[64,384]{1,0:T(8,128)S(1)}, f32[64,384]{1,0:T(8,128)S(1)}, u32[]{:S(2)}, u32[]{:S(2)}) %collective-permute-start.16) | collective-permute-done | bytes 98336 | tf_op jit(solution)/shard_map/ppermute | solution.py:376
  106.8 2.4 %collective-permute-start.17 = (f32[64,384]{1,0:T(8,128)S(1)}, f32[64,384]{1,0:T(8,128)S(1)}, u32[]{:S(2)}, u32[]{:S(2)}) collective-permute-start(f32[64,384]{1,0:T(8,128)S(1)} %add.57), channel_id=1, source_target_pairs={{0,4},{1,5},{2,6},{3,7},{4,0},{5,1},{6,2},{7,3},{8,12},{9,13},{10,... | collective-permute-start | bytes 294920 | tf_op jit(solution)/shard_map/ppermute | solution.py:376
  109.2 4.7 %collective-permute-done.17 = f32[64,384]{1,0:T(8,128)S(1)} collective-permute-done((f32[64,384]{1,0:T(8,128)S(1)}, f32[64,384]{1,0:T(8,128)S(1)}, u32[]{:S(2)}, u32[]{:S(2)}) %collective-permute-start.17) | collective-permute-done | bytes 98336 | tf_op jit(solution)/shard_map/ppermute | solution.py:376
  120.2 1.8 shard_map.59
  122.0 7.9 %collective-permute-done.22 = f32[64,2048]{1,0:T(8,128)S(1)} collective-permute-done((f32[64,2048]{1,0:T(8,128)S(1)}, f32[64,2048]{1,0:T(8,128)S(1)}, u32[]{:S(2)}, u32[]{:S(2)}) %collective-permute-start.22) | collective-permute-done | bytes 524320 | tf_op jit(solution)/shard_map/ppermute | solution.py:376
  132.9 2.3 %shard_map.58 = (f32[64,64]{1,0:T(8,128)S(1)}, f32[64,64]{1,0:T(8,128)S(1)}) custom-call(f32[64,384]{1,0:T(8,128)S(1)} %add.58.both.coef), custom_call_target="tpu_custom_call" | custom-call | flops 1000000 | bytes 100000 | tf_op jit(solution)/shard_map/pallas_call | solution.py:440
  135.2 7.2 %collective-permute-done.18.refs_2_ = f32[64,2048]{1,0:T(8,128)S(1)} collective-permute-done((f32[64,2048]{1,0:T(8,128)S(1)}, f32[64,2048]{1,0:T(8,128)S(1)}, u32[]{:S(2)}, u32[]{:S(2)}) %collective-permute-start.18) | collective-permute-done | bytes 524320 | tf_op jit(solution)/shard_map/ppermute | solution.py:376
  142.4 8.0 %collective-permute-done.23.refs_5_ = f32[64,2048]{1,0:T(8,128)S(1)} collective-permute-done((f32[64,2048]{1,0:T(8,128)S(1)}, f32[64,2048]{1,0:T(8,128)S(1)}, u32[]{:S(2)}, u32[]{:S(2)}) %collective-permute-start.23) | collective-permute-done | bytes 524320 | tf_op jit(solution)/shard_map/ppermute | solution.py:376
  155.3 2.4 %collective-permute-start.25 = (f32[64,64]{1,0:T(8,128)S(1)}, f32[64,64]{1,0:T(8,128)S(1)}, u32[]{:S(2)}, u32[]{:S(2)}) collective-permute-start(f32[64,64]{1,0:T(8,128)S(1)} %add.61), channel_id=1, source_target_pairs={{0,2},{1,3},{2,0},{3,1},{4,6},{5,7},{6,4},{7,5},{8,10},{9,11},{10,... | collective-permute-start | bytes 49160 | tf_op jit(solution)/shard_map/ppermute | solution.py:376
  157.7 3.4 %collective-permute-start.26 = (f32[64,64]{1,0:T(8,128)S(1)}, f32[64,64]{1,0:T(8,128)S(1)}, u32[]{:S(2)}, u32[]{:S(2)}) collective-permute-start(f32[64,64]{1,0:T(8,128)S(1)} %add.61), channel_id=1, source_target_pairs={{0,4},{1,5},{2,6},{3,7},{4,0},{5,1},{6,2},{7,3},{8,12},{9,13},{10,... | collective-permute-start | bytes 49160 | tf_op jit(solution)/shard_map/ppermute | solution.py:376
  161.1 2.4 %collective-permute-done.26 = f32[64,64]{1,0:T(8,128)S(1)} collective-permute-done((f32[64,64]{1,0:T(8,128)S(1)}, f32[64,64]{1,0:T(8,128)S(1)}, u32[]{:S(2)}, u32[]{:S(2)}) %collective-permute-start.26) | collective-permute-done | bytes 16416 | tf_op jit(solution)/shard_map/ppermute | solution.py:376
  163.5 3.3 %collective-permute-done.27 = f32[64,64]{1,0:T(8,128)S(1)} collective-permute-done((f32[64,64]{1,0:T(8,128)S(1)}, f32[64,64]{1,0:T(8,128)S(1)}, u32[]{:S(2)}, u32[]{:S(2)}) %collective-permute-start.27) | collective-permute-done | bytes 16416 | tf_op jit(solution)/shard_map/ppermute | solution.py:376
  176.3 3.0 %shard_map.63 = (f32[64,64]{1,0:T(8,128)}, f32[64,64]{1,0:T(8,128)S(1)}) custom-call(f32[64,64]{1,0:T(8,128)S(1)} %add_add_fusion.gram, f32[64,64]{1,0:T(8,128)S(1)} %get-tuple-element.73.upper_one), custom_call_target="tpu_custom_call" | custom-call | flops 5000000000 | bytes 100000 | tf_op jit(solution)/shard_map/pallas_call | solution.py:461
  179.3 6.5 %collective-permute-done.35.refs_4_ = f32[64,2048]{1,0:T(8,128)S(1)} collective-permute-done((f32[64,2048]{1,0:T(8,128)S(1)}, f32[64,2048]{1,0:T(8,128)S(1)}, u32[]{:S(2)}, u32[]{:S(2)}) %collective-permute-start.35) | collective-permute-done | bytes 524320 | tf_op jit(solution)/shard_map/ppermute | solution.py:376
  186.6 2.3 %shard_map.64.refs_2_ = f32[64,16384]{1,0:T(8,128)} custom-call(f32[64,64]{1,0:T(8,128)S(1)} %get-tuple-element.74.inverse, f32[64,2048]{1,0:T(8,128)S(1)} %get-tuple-element.70.refs_0_, f32[64,2048]{1,0:T(8,128)S(1)} %get-tuple-element.71.refs_1_, f32[64,2048]{1,0:T(8,128)S(1)} %collective-permute-done.31.refs_2_, ...), custom_call_target="tpu_custom_call" | custom-call | flops 905969664 | bytes 6291456 | tf_op jit(solution)/shard_map/pallas_call | solution.py:362
  188.8 4.8 %collective-permute-done.33.refs_0_ = f32[64,2048]{1,0:T(8,128)S(1)} collective-permute-done((f32[64,2048]{1,0:T(8,128)S(1)}, f32[64,2048]{1,0:T(8,128)S(1)}, u32[]{:S(2)}, u32[]{:S(2)}) %collective-permute-start.33) | collective-permute-done | bytes 524320 | tf_op jit(solution)/shard_map/ppermute | solution.py:376
  (71 shorter events, 44.3 us)
Async XLA Ops:
  16.9 5.4 %collective-permute-start.1 = (f32[64,256]{1,0:T(8,128)S(1)}, f32[64,256]{1,0:T(8,128)S(1)}, u32[]{:S(2)}, u32[]{:S(2)}) collective-permute-start(f32[64,256]{1,0:T(8,128)S(1)} %add.51), channel_id=1, source_target_pairs={{0,2},{1,3},{2,0},{3,1},{4,6},{5,7},{6,4},{7,5},{8,10},{9,11},{10,... | collective-permute-start | bytes 196616 | tf_op jit(solution)/shard_map/ppermute | solution.py:376
  22.3 5.3 %collective-permute-start.2 = (f32[64,256]{1,0:T(8,128)S(1)}, f32[64,256]{1,0:T(8,128)S(1)}, u32[]{:S(2)}, u32[]{:S(2)}) collective-permute-start(f32[64,256]{1,0:T(8,128)S(1)} %add.52), channel_id=1, source_target_pairs={{0,4},{1,5},{2,6},{3,7},{4,0},{5,1},{6,2},{7,3},{8,12},{9,13},{10,... | collective-permute-start | bytes 196616 | tf_op jit(solution)/shard_map/ppermute | solution.py:376
  28.6 14.9 %collective-permute-start.7 = (f32[64,2048]{1,0:T(8,128)S(1)}, f32[64,2048]{1,0:T(8,128)S(1)}, u32[]{:S(2)}, u32[]{:S(2)}) collective-permute-start(f32[64,2048]{1,0:T(8,128)S(1)} %get-tuple-element.53), channel_id=1, source_target_pairs={{0,16},{8,24},{16,0},{24,8},{1,17},{9,25},{17,1},{25,9},{2,18},{10... | collective-permute-start | bytes 1572872 | tf_op jit(solution)/shard_map/ppermute | solution.py:376
  30.4 15.0 %collective-permute-start.5 = (f32[64,2048]{1,0:T(8,128)S(1)}, f32[64,2048]{1,0:T(8,128)S(1)}, u32[]{:S(2)}, u32[]{:S(2)}) collective-permute-start(f32[64,2048]{1,0:T(8,128)S(1)} %get-tuple-element.51), channel_id=1, source_target_pairs={{0,8},{8,0},{16,24},{24,16},{1,9},{9,1},{17,25},{25,17},{2,10},{10... | collective-permute-start | bytes 1572872 | tf_op jit(solution)/shard_map/ppermute | solution.py:376
  32.9 23.6 %collective-permute-start.3 = (f32[64,2048]{1,0:T(8,128)S(1)}, f32[64,2048]{1,0:T(8,128)S(1)}, u32[]{:S(2)}, u32[]{:S(2)}) collective-permute-start(f32[64,2048]{1,0:T(8,128)S(1)} %get-tuple-element.48), channel_id=1, source_target_pairs={{0,8},{8,0},{16,24},{24,16},{1,9},{9,1},{17,25},{25,17},{2,10},{10... | collective-permute-start | bytes 1572872 | tf_op jit(solution)/shard_map/ppermute | solution.py:376
  33.5 23.0 %collective-permute-start.4 = (f32[64,2048]{1,0:T(8,128)S(1)}, f32[64,2048]{1,0:T(8,128)S(1)}, u32[]{:S(2)}, u32[]{:S(2)}) collective-permute-start(f32[64,2048]{1,0:T(8,128)S(1)} %get-tuple-element.49), channel_id=1, source_target_pairs={{0,16},{8,24},{16,0},{24,8},{1,17},{9,25},{17,1},{25,9},{2,18},{10... | collective-permute-start | bytes 1572872 | tf_op jit(solution)/shard_map/ppermute | solution.py:376
  43.6 20.7 %collective-permute-start.8 = (f32[64,2048]{1,0:T(8,128)S(1)}, f32[64,2048]{1,0:T(8,128)S(1)}, u32[]{:S(2)}, u32[]{:S(2)}) collective-permute-start(f32[64,2048]{1,0:T(8,128)S(1)} %add.55), channel_id=1, source_target_pairs={{0,8},{8,0},{16,24},{24,16},{1,9},{9,1},{17,25},{25,17},{2,10},{10... | collective-permute-start | bytes 1572872 | tf_op jit(solution)/shard_map/ppermute | solution.py:376
  45.4 18.9 %collective-permute-start.6 = (f32[64,2048]{1,0:T(8,128)S(1)}, f32[64,2048]{1,0:T(8,128)S(1)}, u32[]{:S(2)}, u32[]{:S(2)}) collective-permute-start(f32[64,2048]{1,0:T(8,128)S(1)} %add.54), channel_id=1, source_target_pairs={{0,16},{8,24},{16,0},{24,8},{1,17},{9,25},{17,1},{25,9},{2,18},{10... | collective-permute-start | bytes 1572872 | tf_op jit(solution)/shard_map/ppermute | solution.py:376
  64.4 14.9 %collective-permute-start.9 = (f32[64,2048]{1,0:T(8,128)S(1)}, f32[64,2048]{1,0:T(8,128)S(1)}, u32[]{:S(2)}, u32[]{:S(2)}) collective-permute-start(f32[64,2048]{1,0:T(8,128)S(1)} %get-tuple-element.54.refs_0_), channel_id=1, source_target_pairs={{0,16},{8,24},{16,0},{24,8},{1,17},{9,25},{17,1},{25,9},{2,18},{10... | collective-permute-start | bytes 1572872 | tf_op jit(solution)/shard_map/ppermute | solution.py:376
  65.4 15.7 %collective-permute-start.11 = (f32[64,2048]{1,0:T(8,128)S(1)}, f32[64,2048]{1,0:T(8,128)S(1)}, u32[]{:S(2)}, u32[]{:S(2)}) collective-permute-start(f32[64,2048]{1,0:T(8,128)S(1)} %get-tuple-element.55.refs_1_), channel_id=1, source_target_pairs={{0,8},{8,0},{16,24},{24,16},{1,9},{9,1},{17,25},{25,17},{2,10},{10... | collective-permute-start | bytes 1572872 | tf_op jit(solution)/shard_map/ppermute | solution.py:376
  66.5 25.0 %collective-permute-start.13 = (f32[64,2048]{1,0:T(8,128)S(1)}, f32[64,2048]{1,0:T(8,128)S(1)}, u32[]{:S(2)}, u32[]{:S(2)}) collective-permute-start(f32[64,2048]{1,0:T(8,128)S(1)} %get-tuple-element.54.refs_0_), channel_id=1, source_target_pairs={{0,8},{8,0},{16,24},{24,16},{1,9},{9,1},{17,25},{25,17},{2,10},{10... | collective-permute-start | bytes 1572872 | tf_op jit(solution)/shard_map/ppermute | solution.py:376
  67.4 24.1 %collective-permute-start.14 = (f32[64,2048]{1,0:T(8,128)S(1)}, f32[64,2048]{1,0:T(8,128)S(1)}, u32[]{:S(2)}, u32[]{:S(2)}) collective-permute-start(f32[64,2048]{1,0:T(8,128)S(1)} %get-tuple-element.55.refs_1_), channel_id=1, source_target_pairs={{0,16},{8,24},{16,0},{24,8},{1,17},{9,25},{17,1},{25,9},{2,18},{10... | collective-permute-start | bytes 1572872 | tf_op jit(solution)/shard_map/ppermute | solution.py:376
  79.4 19.3 %collective-permute-start.10 = (f32[64,2048]{1,0:T(8,128)S(1)}, f32[64,2048]{1,0:T(8,128)S(1)}, u32[]{:S(2)}, u32[]{:S(2)}) collective-permute-start(f32[64,2048]{1,0:T(8,128)S(1)} %collective-permute-done.9.refs_0_), channel_id=1, source_target_pairs={{0,8},{8,0},{16,24},{24,16},{1,9},{9,1},{17,25},{25,17},{2,10},{10... | collective-permute-start | bytes 1572872 | tf_op jit(solution)/shard_map/ppermute | solution.py:376
  81.0 17.6 %collective-permute-start.12 = (f32[64,2048]{1,0:T(8,128)S(1)}, f32[64,2048]{1,0:T(8,128)S(1)}, u32[]{:S(2)}, u32[]{:S(2)}) collective-permute-start(f32[64,2048]{1,0:T(8,128)S(1)} %collective-permute-done.11.refs_1_), channel_id=1, source_target_pairs={{0,16},{8,24},{16,0},{24,8},{1,17},{9,25},{17,1},{25,9},{2,18},{10... | collective-permute-start | bytes 1572872 | tf_op jit(solution)/shard_map/ppermute | solution.py:376
  101.9 4.9 %collective-permute-start.16 = (f32[64,384]{1,0:T(8,128)S(1)}, f32[64,384]{1,0:T(8,128)S(1)}, u32[]{:S(2)}, u32[]{:S(2)}) collective-permute-start(f32[64,384]{1,0:T(8,128)S(1)} %add.56), channel_id=1, source_target_pairs={{0,2},{1,3},{2,0},{3,1},{4,6},{5,7},{6,4},{7,5},{8,10},{9,11},{10,... | collective-permute-start | bytes 294920 | tf_op jit(solution)/shard_map/ppermute | solution.py:376
  106.8 7.2 %collective-permute-start.17 = (f32[64,384]{1,0:T(8,128)S(1)}, f32[64,384]{1,0:T(8,128)S(1)}, u32[]{:S(2)}, u32[]{:S(2)}) collective-permute-start(f32[64,384]{1,0:T(8,128)S(1)} %add.57), channel_id=1, source_target_pairs={{0,4},{1,5},{2,6},{3,7},{4,0},{5,1},{6,2},{7,3},{8,12},{9,13},{10,... | collective-permute-start | bytes 294920 | tf_op jit(solution)/shard_map/ppermute | solution.py:376
  115.0 14.9 %collective-permute-start.22 = (f32[64,2048]{1,0:T(8,128)S(1)}, f32[64,2048]{1,0:T(8,128)S(1)}, u32[]{:S(2)}, u32[]{:S(2)}) collective-permute-start(f32[64,2048]{1,0:T(8,128)S(1)} %get-tuple-element.68), channel_id=1, source_target_pairs={{0,16},{8,24},{16,0},{24,8},{1,17},{9,25},{17,1},{25,9},{2,18},{10... | collective-permute-start | bytes 1572872 | tf_op jit(solution)/shard_map/ppermute | solution.py:376
  116.3 15.3 %collective-permute-start.20 = (f32[64,2048]{1,0:T(8,128)S(1)}, f32[64,2048]{1,0:T(8,128)S(1)}, u32[]{:S(2)}, u32[]{:S(2)}) collective-permute-start(f32[64,2048]{1,0:T(8,128)S(1)} %get-tuple-element.66), channel_id=1, source_target_pairs={{0,8},{8,0},{16,24},{24,16},{1,9},{9,1},{17,25},{25,17},{2,10},{10... | collective-permute-start | bytes 1572872 | tf_op jit(solution)/shard_map/ppermute | solution.py:376
  118.8 23.6 %collective-permute-start.18 = (f32[64,2048]{1,0:T(8,128)S(1)}, f32[64,2048]{1,0:T(8,128)S(1)}, u32[]{:S(2)}, u32[]{:S(2)}) collective-permute-start(f32[64,2048]{1,0:T(8,128)S(1)} %get-tuple-element.63), channel_id=1, source_target_pairs={{0,8},{8,0},{16,24},{24,16},{1,9},{9,1},{17,25},{25,17},{2,10},{10... | collective-permute-start | bytes 1572872 | tf_op jit(solution)/shard_map/ppermute | solution.py:376
  119.4 23.0 %collective-permute-start.19 = (f32[64,2048]{1,0:T(8,128)S(1)}, f32[64,2048]{1,0:T(8,128)S(1)}, u32[]{:S(2)}, u32[]{:S(2)}) collective-permute-start(f32[64,2048]{1,0:T(8,128)S(1)} %get-tuple-element.64), channel_id=1, source_target_pairs={{0,16},{8,24},{16,0},{24,8},{1,17},{9,25},{17,1},{25,9},{2,18},{10... | collective-permute-start | bytes 1572872 | tf_op jit(solution)/shard_map/ppermute | solution.py:376
  130.0 20.4 %collective-permute-start.23 = (f32[64,2048]{1,0:T(8,128)S(1)}, f32[64,2048]{1,0:T(8,128)S(1)}, u32[]{:S(2)}, u32[]{:S(2)}) collective-permute-start(f32[64,2048]{1,0:T(8,128)S(1)} %add.60), channel_id=1, source_target_pairs={{0,8},{8,0},{16,24},{24,16},{1,9},{9,1},{17,25},{25,17},{2,10},{10... | collective-permute-start | bytes 1572872 | tf_op jit(solution)/shard_map/ppermute | solution.py:376
  131.6 18.8 %collective-permute-start.21 = (f32[64,2048]{1,0:T(8,128)S(1)}, f32[64,2048]{1,0:T(8,128)S(1)}, u32[]{:S(2)}, u32[]{:S(2)}) collective-permute-start(f32[64,2048]{1,0:T(8,128)S(1)} %add.59), channel_id=1, source_target_pairs={{0,16},{8,24},{16,0},{24,8},{1,17},{9,25},{17,1},{25,9},{2,18},{10... | collective-permute-start | bytes 1572872 | tf_op jit(solution)/shard_map/ppermute | solution.py:376
  151.8 22.1 %collective-permute-start.31 = (f32[64,2048]{1,0:T(8,128)S(1)}, f32[64,2048]{1,0:T(8,128)S(1)}, u32[]{:S(2)}, u32[]{:S(2)}) collective-permute-start(f32[64,2048]{1,0:T(8,128)S(1)} %get-tuple-element.70.refs_0_), channel_id=1, source_target_pairs={{0,16},{8,24},{16,0},{24,8},{1,17},{9,25},{17,1},{25,9},{2,18},{10... | collective-permute-start | bytes 1572872 | tf_op jit(solution)/shard_map/ppermute | solution.py:376
  152.6 21.3 %collective-permute-start.32 = (f32[64,2048]{1,0:T(8,128)S(1)}, f32[64,2048]{1,0:T(8,128)S(1)}, u32[]{:S(2)}, u32[]{:S(2)}) collective-permute-start(f32[64,2048]{1,0:T(8,128)S(1)} %get-tuple-element.71.refs_1_), channel_id=1, source_target_pairs={{0,8},{8,0},{16,24},{24,16},{1,9},{9,1},{17,25},{25,17},{2,10},{10... | collective-permute-start | bytes 1572872 | tf_op jit(solution)/shard_map/ppermute | solution.py:376
  155.3 5.8 %collective-permute-start.25 = (f32[64,64]{1,0:T(8,128)S(1)}, f32[64,64]{1,0:T(8,128)S(1)}, u32[]{:S(2)}, u32[]{:S(2)}) collective-permute-start(f32[64,64]{1,0:T(8,128)S(1)} %add.61), channel_id=1, source_target_pairs={{0,2},{1,3},{2,0},{3,1},{4,6},{5,7},{6,4},{7,5},{8,10},{9,11},{10,... | collective-permute-start | bytes 49160 | tf_op jit(solution)/shard_map/ppermute | solution.py:376
  157.7 5.8 %collective-permute-start.26 = (f32[64,64]{1,0:T(8,128)S(1)}, f32[64,64]{1,0:T(8,128)S(1)}, u32[]{:S(2)}, u32[]{:S(2)}) collective-permute-start(f32[64,64]{1,0:T(8,128)S(1)} %add.61), channel_id=1, source_target_pairs={{0,4},{1,5},{2,6},{3,7},{4,0},{5,1},{6,2},{7,3},{8,12},{9,13},{10,... | collective-permute-start | bytes 49160 | tf_op jit(solution)/shard_map/ppermute | solution.py:376
  161.1 5.7 %collective-permute-start.27 = (f32[64,64]{1,0:T(8,128)S(1)}, f32[64,64]{1,0:T(8,128)S(1)}, u32[]{:S(2)}, u32[]{:S(2)}) collective-permute-start(f32[64,64]{1,0:T(8,128)S(1)} %add.61), channel_id=1, source_target_pairs={{0,6},{1,7},{2,4},{3,5},{4,2},{5,3},{6,0},{7,1},{8,14},{9,15},{10,... | collective-permute-start | bytes 49160 | tf_op jit(solution)/shard_map/ppermute | solution.py:376
  168.6 5.2 %collective-permute-start.30 = (f32[64,64]{1,0:T(8,128)S(1)}, f32[64,64]{1,0:T(8,128)S(1)}, u32[]{:S(2)}, u32[]{:S(2)}) collective-permute-start(f32[64,64]{1,0:T(8,128)S(1)} %add_add_fusion.1), channel_id=1, source_target_pairs={{0,24},{8,16},{16,8},{24,0},{1,25},{9,17},{17,9},{25,1},{2,26},{10... | collective-permute-start | bytes 49160 | tf_op jit(solution)/shard_map/ppermute | solution.py:376
  170.9 14.9 %collective-permute-start.35 = (f32[64,2048]{1,0:T(8,128)S(1)}, f32[64,2048]{1,0:T(8,128)S(1)}, u32[]{:S(2)}, u32[]{:S(2)}) collective-permute-start(f32[64,2048]{1,0:T(8,128)S(1)} %get-tuple-element.70.refs_0_), channel_id=1, source_target_pairs={{0,8},{8,0},{16,24},{24,16},{1,9},{9,1},{17,25},{25,17},{2,10},{10... | collective-permute-start | bytes 1572872 | tf_op jit(solution)/shard_map/ppermute | solution.py:376
  171.7 14.9 %collective-permute-start.36 = (f32[64,2048]{1,0:T(8,128)S(1)}, f32[64,2048]{1,0:T(8,128)S(1)}, u32[]{:S(2)}, u32[]{:S(2)}) collective-permute-start(f32[64,2048]{1,0:T(8,128)S(1)} %get-tuple-element.71.refs_1_), channel_id=1, source_target_pairs={{0,16},{8,24},{16,0},{24,8},{1,17},{9,25},{17,1},{25,9},{2,18},{10... | collective-permute-start | bytes 1572872 | tf_op jit(solution)/shard_map/ppermute | solution.py:376
  173.9 19.7 %collective-permute-start.33 = (f32[64,2048]{1,0:T(8,128)S(1)}, f32[64,2048]{1,0:T(8,128)S(1)}, u32[]{:S(2)}, u32[]{:S(2)}) collective-permute-start(f32[64,2048]{1,0:T(8,128)S(1)} %collective-permute-done.31.refs_2_), channel_id=1, source_target_pairs={{0,8},{8,0},{16,24},{24,16},{1,9},{9,1},{17,25},{25,17},{2,10},{10... | collective-permute-start | bytes 1572872 | tf_op jit(solution)/shard_map/ppermute | solution.py:376
  175.5 18.7 %collective-permute-start.34 = (f32[64,2048]{1,0:T(8,128)S(1)}, f32[64,2048]{1,0:T(8,128)S(1)}, u32[]{:S(2)}, u32[]{:S(2)}) collective-permute-start(f32[64,2048]{1,0:T(8,128)S(1)} %collective-permute-done.32.refs_3_), channel_id=1, source_target_pairs={{0,16},{8,24},{16,0},{24,8},{1,17},{9,25},{17,1},{25,9},{2,18},{10... | collective-permute-start | bytes 1572872 | tf_op jit(solution)/shard_map/ppermute | solution.py:376
  (5 other events, 12.3 us)

commit v4 on v3

--- a/solution.py
+++ b/solution.py
@@ -10,7 +10,7 @@
 F32 = jnp.float32
 BF16 = jnp.bfloat16
 STEP = 1024
-CHUNK = 1024
+CHUNK = 2048
 SLOTS = 4
 ROWS = 16
 GROUP = 4
@@ -385,24 +385,6 @@
     return x
 
 
-def sum_of_four(x, axis, bit=1):
-    one, two, three = (flip(x, axis, n * bit) for n in (1, 2, 3))
-    return (x + one) + (two + three)
-
-
-def sum_by_fours(x, axis):
-    size = lax.axis_size(axis)
-    x = x + flip(x, axis, 1)
-    bit = 2
-    while bit < size:
-        if 2 * bit < size:
-            x = sum_of_four(x, axis, bit)
-        else:
-            x = x + flip(x, axis, bit)
-        bit *= 4
-    return x
-
-
 def local(locked, vectors, mass):
     new, rows = vectors.shape
     total = rows * lax.axis_size("row")
@@ -453,10 +435,11 @@
         compiler_params=PARAMS,
         cost_estimate=cost(36 * new * new * 2 * unit, 24 * new * unit),
     )(mass, inverse, *parts)
+    one, two, three = (flip(gram, "col", n) for n in (1, 2, 3))
+    one, two, three, a, b = lax.optimization_barrier((one, two, three, a, b))
+    gram = sum_over((gram + one) + (two + three), "row")
     ay, bx = flip(a, "col", 2), flip(b, "col", 1)
     ax, by = flip(a, "col", 1), flip(b, "col", 2)
-    gram = sum_of_four(sum_by_fours(gram, "row"), "col")
-    gram, ay, bx = lax.optimization_barrier((gram, ay, bx))
     far = flip(ay, "col", 1), flip(bx, "col", 2)
     factor, inverse = pl.pallas_call(
         last_kernel,

time: 196 us -> 195 us (level)
  waiting for transfers between devices: 108 us -> 106 us
    ppermute x37 -> x36, waiting for transfers between devices: 108 us -> 106 us  [flip(): return lax.ppermute(x, axis, [(i, i ^ bit) for i in range(size)])]
    ppermute x37 -> x36, starting transfers between devices: 46.8 us -> 45.8 us  [flip(): return lax.ppermute(x, axis, [(i, i ^ bit) for i in range(size)])]
  transfers between devices with their start and end apart: 37 -> 36, of which waited for: 24 -> 23; matrix products, arithmetic and copies ran while one was open for 0% -> 0% of each run, Pallas kernels for 9% -> 10%
where the time goes in v4:
time: 195 us; the launch traced here: 193 us
  waiting for transfers between devices  106 us (54%)
  starting transfers between devices  45.8 us (23%)
  Pallas kernels  39.9 us (20%)
    ppermute x36, waiting for transfers between devices, flip(): return lax.ppermute(x, axis, [(i, i ^ bit) for i in range(size)])  106 us
    ppermute x36, starting transfers between devices, flip(): return lax.ppermute(x, axis, [(i, i ^ bit) for i in range(size)])  45.8 us
    pallas_call x1, Pallas kernels, first_coefficients(): pl.pallas_call(functools.partial(first_kernel, total), out_shape=[array(n...  14.4 us
    pallas_call x6, Pallas kernels, corrections(): pl.pallas_call(functools.partial(corrections_kernel, names, len(base)), o...  7.64 us
    pallas_call x3, Pallas kernels, second_coefficients(): pl.pallas_call(functools.partial(second_kernel, count, total, mode), out_...  7.26 us
  transfers between devices with their start and end apart: 36, of which 23 were waited for; matrix products, arithmetic and copies ran while one was open for 0% of the time, Pallas kernels for 10%

profile of v4, /device:TPU:0, one launch (start us, length us, event | category | flops | bytes accessed | tf_op | source)
XLA Modules:
  0.0 192.9 jit_solution(12753123474222332988)
XLA Ops:
  0.6 14.4 %shard_map.50 = (f32[64,256]{1,0:T(8,128)S(1)}, bf16[256,16384]{1,0:T(8,128)(2,1)S(1)}, bf16[256,16384]{1,0:T(8,128)(2,1)S(1)}, f32[1,16384]{1,0:T(1,128)S(1)}, ...) custom-call(f32[256,16384]{1,0:T(8,128)} %locked.1, f32[64,16384]{1,0:T(8,128)} %vectors.1, f32[1,16384]{1,0:T(1,128)} %bitcast.1), custom_call_target="tpu_custom_call" | custom-call | flops 3221225472 | bytes 33554432 | tf_op jit(solution)/shard_map/pallas_call | solution.py:148
  16.5 3.0 %collective-permute-start.1 = (f32[64,256]{1,0:T(8,128)S(1)}, f32[64,256]{1,0:T(8,128)S(1)}, u32[]{:S(2)}, u32[]{:S(2)}) collective-permute-start(f32[64,256]{1,0:T(8,128)S(1)} %add.48), channel_id=1, source_target_pairs={{0,2},{1,3},{2,0},{3,1},{4,6},{5,7},{6,4},{7,5},{8,10},{9,11},{10,... | collective-permute-start | bytes 196616 | tf_op jit(solution)/shard_map/ppermute | solution.py:376
  19.5 2.4 %collective-permute-done.1 = f32[64,256]{1,0:T(8,128)S(1)} collective-permute-done((f32[64,256]{1,0:T(8,128)S(1)}, f32[64,256]{1,0:T(8,128)S(1)}, u32[]{:S(2)}, u32[]{:S(2)}) %collective-permute-start.1) | collective-permute-done | bytes 65568 | tf_op jit(solution)/shard_map/ppermute | solution.py:376
  21.9 2.9 %collective-permute-start.2 = (f32[64,256]{1,0:T(8,128)S(1)}, f32[64,256]{1,0:T(8,128)S(1)}, u32[]{:S(2)}, u32[]{:S(2)}) collective-permute-start(f32[64,256]{1,0:T(8,128)S(1)} %add.49), channel_id=1, source_target_pairs={{0,4},{1,5},{2,6},{3,7},{4,0},{5,1},{6,2},{7,3},{8,12},{9,13},{10,... | collective-permute-start | bytes 196616 | tf_op jit(solution)/shard_map/ppermute | solution.py:376
  24.8 2.4 %collective-permute-done.2 = f32[64,256]{1,0:T(8,128)S(1)} collective-permute-done((f32[64,256]{1,0:T(8,128)S(1)}, f32[64,256]{1,0:T(8,128)S(1)}, u32[]{:S(2)}, u32[]{:S(2)}) %collective-permute-start.2) | collective-permute-done | bytes 65568 | tf_op jit(solution)/shard_map/ppermute | solution.py:376
  33.4 1.8 shard_map.51
  35.3 7.9 %collective-permute-done.7 = f32[64,2048]{1,0:T(8,128)S(1)} collective-permute-done((f32[64,2048]{1,0:T(8,128)S(1)}, f32[64,2048]{1,0:T(8,128)S(1)}, u32[]{:S(2)}, u32[]{:S(2)}) %collective-permute-start.7) | collective-permute-done | bytes 524320 | tf_op jit(solution)/shard_map/ppermute | solution.py:376
  46.6 9.5 %collective-permute-done.3.refs_2_ = f32[64,2048]{1,0:T(8,128)S(1)} collective-permute-done((f32[64,2048]{1,0:T(8,128)S(1)}, f32[64,2048]{1,0:T(8,128)S(1)}, u32[]{:S(2)}, u32[]{:S(2)}) %collective-permute-start.3) | collective-permute-done | bytes 524320 | tf_op jit(solution)/shard_map/ppermute | solution.py:376
  56.1 7.8 %collective-permute-done.8.refs_5_ = f32[64,2048]{1,0:T(8,128)S(1)} collective-permute-done((f32[64,2048]{1,0:T(8,128)S(1)}, f32[64,2048]{1,0:T(8,128)S(1)}, u32[]{:S(2)}, u32[]{:S(2)}) %collective-permute-start.8) | collective-permute-done | bytes 524320 | tf_op jit(solution)/shard_map/ppermute | solution.py:376
  68.2 10.8 %collective-permute-done.9.refs_0_ = f32[64,2048]{1,0:T(8,128)S(1)} collective-permute-done((f32[64,2048]{1,0:T(8,128)S(1)}, f32[64,2048]{1,0:T(8,128)S(1)}, u32[]{:S(2)}, u32[]{:S(2)}) %collective-permute-start.9) | collective-permute-done | bytes 524320 | tf_op jit(solution)/shard_map/ppermute | solution.py:376
  81.0 2.0 %shard_map.55 = (f32[64,256]{1,0:T(8,128)S(1)}, f32[2,64,64]{2,1,0:T(8,128)S(1)}) custom-call(bf16[256,16384]{1,0:T(8,128)(2,1)S(1)} %get-tuple-element.43.high, bf16[256,16384]{1,0:T(8,128)(2,1)S(1)} %get-tuple-element.44.low, f32[1,16384]{1,0:T(1,128)S(1)} %get-tuple-element.42.mass, f32[64,2048]{1,0:T(8,128)S(1)} %get-tuple-element.56.refs_0_, ...), custom_call_target="tpu_custom_call" | custom-call | flops 939524096 | bytes 5242880 | tf_op jit(solution)/shard_map/pallas_call | solution.py:228
  83.1 8.1 %collective-permute-done.13.refs_2_ = f32[64,2048]{1,0:T(8,128)S(1)} collective-permute-done((f32[64,2048]{1,0:T(8,128)S(1)}, f32[64,2048]{1,0:T(8,128)S(1)}, u32[]{:S(2)}, u32[]{:S(2)}) %collective-permute-start.13) | collective-permute-done | bytes 524320 | tf_op jit(solution)/shard_map/ppermute | solution.py:376
  91.1 3.4 %shard_map.56 = (f32[64,256]{1,0:T(8,128)S(1)}, f32[4,64,64]{2,1,0:T(8,128)S(1)}) custom-call(bf16[256,16384]{1,0:T(8,128)(2,1)S(1)} %get-tuple-element.43.high, bf16[256,16384]{1,0:T(8,128)(2,1)S(1)} %get-tuple-element.44.low, f32[1,16384]{1,0:T(1,128)S(1)} %get-tuple-element.42.mass, f32[64,2048]{1,0:T(8,128)S(1)} %collective-permute-done.9.refs_0_, ...), custom_call_target="tpu_custom_call" | custom-call | flops 1879048192 | bytes 10485760 | tf_op jit(solution)/shard_map/pallas_call | solution.py:228
  94.5 3.8 %collective-permute-done.10.refs_0_ = f32[64,2048]{1,0:T(8,128)S(1)} collective-permute-done((f32[64,2048]{1,0:T(8,128)S(1)}, f32[64,2048]{1,0:T(8,128)S(1)}, u32[]{:S(2)}, u32[]{:S(2)}) %collective-permute-start.10) | collective-permute-done | bytes 524320 | tf_op jit(solution)/shard_map/ppermute | solution.py:376
  98.3 1.9 shard_map.57
  102.6 3.8 %collective-permute-done.16 = f32[64,384]{1,0:T(8,128)S(1)} collective-permute-done((f32[64,384]{1,0:T(8,128)S(1)}, f32[64,384]{1,0:T(8,128)S(1)}, u32[]{:S(2)}, u32[]{:S(2)}) %collective-permute-start.16) | collective-permute-done | bytes 98336 | tf_op jit(solution)/shard_map/ppermute | solution.py:376
  106.4 2.4 %collective-permute-start.17 = (f32[64,384]{1,0:T(8,128)S(1)}, f32[64,384]{1,0:T(8,128)S(1)}, u32[]{:S(2)}, u32[]{:S(2)}) collective-permute-start(f32[64,384]{1,0:T(8,128)S(1)} %add.54), channel_id=1, source_target_pairs={{0,4},{1,5},{2,6},{3,7},{4,0},{5,1},{6,2},{7,3},{8,12},{9,13},{10,... | collective-permute-start | bytes 294920 | tf_op jit(solution)/shard_map/ppermute | solution.py:376
  108.9 4.7 %collective-permute-done.17 = f32[64,384]{1,0:T(8,128)S(1)} collective-permute-done((f32[64,384]{1,0:T(8,128)S(1)}, f32[64,384]{1,0:T(8,128)S(1)}, u32[]{:S(2)}, u32[]{:S(2)}) %collective-permute-start.17) | collective-permute-done | bytes 98336 | tf_op jit(solution)/shard_map/ppermute | solution.py:376
  119.8 1.8 shard_map.59
  121.6 7.9 %collective-permute-done.22 = f32[64,2048]{1,0:T(8,128)S(1)} collective-permute-done((f32[64,2048]{1,0:T(8,128)S(1)}, f32[64,2048]{1,0:T(8,128)S(1)}, u32[]{:S(2)}, u32[]{:S(2)}) %collective-permute-start.22) | collective-permute-done | bytes 524320 | tf_op jit(solution)/shard_map/ppermute | solution.py:376
  132.5 2.3 %shard_map.58 = (f32[64,64]{1,0:T(8,128)S(1)}, f32[64,64]{1,0:T(8,128)S(1)}) custom-call(f32[64,384]{1,0:T(8,128)S(1)} %add.55.both.coef), custom_call_target="tpu_custom_call" | custom-call | flops 1000000 | bytes 100000 | tf_op jit(solution)/shard_map/pallas_call | solution.py:422
  134.8 7.2 %collective-permute-done.18.refs_2_ = f32[64,2048]{1,0:T(8,128)S(1)} collective-permute-done((f32[64,2048]{1,0:T(8,128)S(1)}, f32[64,2048]{1,0:T(8,128)S(1)}, u32[]{:S(2)}, u32[]{:S(2)}) %collective-permute-start.18) | collective-permute-done | bytes 524320 | tf_op jit(solution)/shard_map/ppermute | solution.py:376
  142.0 8.0 %collective-permute-done.23.refs_5_ = f32[64,2048]{1,0:T(8,128)S(1)} collective-permute-done((f32[64,2048]{1,0:T(8,128)S(1)}, f32[64,2048]{1,0:T(8,128)S(1)}, u32[]{:S(2)}, u32[]{:S(2)}) %collective-permute-start.23) | collective-permute-done | bytes 524320 | tf_op jit(solution)/shard_map/ppermute | solution.py:376
  155.4 1.8 collective-permute-done.25
  164.2 2.1 %collective-permute-start.28 = (f32[64,64]{1,0:T(8,128)S(1)}, f32[64,64]{1,0:T(8,128)S(1)}, u32[]{:S(2)}, u32[]{:S(2)}) collective-permute-start(f32[64,64]{1,0:T(8,128)S(1)} %add.61), channel_id=1, source_target_pairs={{0,2},{1,3},{2,0},{3,1},{4,6},{5,7},{6,4},{7,5},{8,10},{9,11},{10,... | collective-permute-start | bytes 49160 | tf_op jit(solution)/shard_map/ppermute | solution.py:376
  166.3 1.9 collective-permute-done.28
  168.2 3.4 %collective-permute-start.29 = (f32[64,64]{1,0:T(8,128)S(1)}, f32[64,64]{1,0:T(8,128)S(1)}, u32[]{:S(2)}, u32[]{:S(2)}) collective-permute-start(f32[64,64]{1,0:T(8,128)S(1)} %add.62), channel_id=1, source_target_pairs={{0,4},{1,5},{2,6},{3,7},{4,0},{5,1},{6,2},{7,3},{8,12},{9,13},{10,... | collective-permute-start | bytes 49160 | tf_op jit(solution)/shard_map/ppermute | solution.py:376
  171.6 2.2 %collective-permute-done.29 = f32[64,64]{1,0:T(8,128)S(1)} collective-permute-done((f32[64,64]{1,0:T(8,128)S(1)}, f32[64,64]{1,0:T(8,128)S(1)}, u32[]{:S(2)}, u32[]{:S(2)}) %collective-permute-start.29) | collective-permute-done | bytes 16416 | tf_op jit(solution)/shard_map/ppermute | solution.py:376
  175.7 3.0 %shard_map.63 = (f32[64,64]{1,0:T(8,128)}, f32[64,64]{1,0:T(8,128)S(1)}) custom-call(f32[64,64]{1,0:T(8,128)S(1)} %add.63.gram, f32[64,64]{1,0:T(8,128)S(1)} %get-tuple-element.77.upper_one), custom_call_target="tpu_custom_call" | custom-call | flops 5000000000 | bytes 100000 | tf_op jit(solution)/shard_map/pallas_call | solution.py:444
  178.8 6.5 %collective-permute-done.34.refs_4_ = f32[64,2048]{1,0:T(8,128)S(1)} collective-permute-done((f32[64,2048]{1,0:T(8,128)S(1)}, f32[64,2048]{1,0:T(8,128)S(1)}, u32[]{:S(2)}, u32[]{:S(2)}) %collective-permute-start.34) | collective-permute-done | bytes 524320 | tf_op jit(solution)/shard_map/ppermute | solution.py:376
  185.2 2.3 %shard_map.64.refs_2_ = f32[64,16384]{1,0:T(8,128)} custom-call(f32[64,64]{1,0:T(8,128)S(1)} %get-tuple-element.78.inverse, f32[64,2048]{1,0:T(8,128)S(1)} %get-tuple-element.79.refs_0_, f32[64,2048]{1,0:T(8,128)S(1)} %get-tuple-element.80.refs_1_, f32[64,2048]{1,0:T(8,128)S(1)} %collective-permute-done.30.refs_2_, ...), custom_call_target="tpu_custom_call" | custom-call | flops 905969664 | bytes 6291456 | tf_op jit(solution)/shard_map/pallas_call | solution.py:362
  187.5 3.8 %collective-permute-done.31.refs_0_ = f32[64,2048]{1,0:T(8,128)S(1)} collective-permute-done((f32[64,2048]{1,0:T(8,128)S(1)}, f32[64,2048]{1,0:T(8,128)S(1)}, u32[]{:S(2)}, u32[]{:S(2)}) %collective-permute-start.31) | collective-permute-done | bytes 524320 | tf_op jit(solution)/shard_map/ppermute | solution.py:376
  (70 shorter events, 44.7 us)
Async XLA Ops:
  16.5 5.4 %collective-permute-start.1 = (f32[64,256]{1,0:T(8,128)S(1)}, f32[64,256]{1,0:T(8,128)S(1)}, u32[]{:S(2)}, u32[]{:S(2)}) collective-permute-start(f32[64,256]{1,0:T(8,128)S(1)} %add.48), channel_id=1, source_target_pairs={{0,2},{1,3},{2,0},{3,1},{4,6},{5,7},{6,4},{7,5},{8,10},{9,11},{10,... | collective-permute-start | bytes 196616 | tf_op jit(solution)/shard_map/ppermute | solution.py:376
  21.9 5.3 %collective-permute-start.2 = (f32[64,256]{1,0:T(8,128)S(1)}, f32[64,256]{1,0:T(8,128)S(1)}, u32[]{:S(2)}, u32[]{:S(2)}) collective-permute-start(f32[64,256]{1,0:T(8,128)S(1)} %add.49), channel_id=1, source_target_pairs={{0,4},{1,5},{2,6},{3,7},{4,0},{5,1},{6,2},{7,3},{8,12},{9,13},{10,... | collective-permute-start | bytes 196616 | tf_op jit(solution)/shard_map/ppermute | solution.py:376
  28.2 14.9 %collective-permute-start.7 = (f32[64,2048]{1,0:T(8,128)S(1)}, f32[64,2048]{1,0:T(8,128)S(1)}, u32[]{:S(2)}, u32[]{:S(2)}) collective-permute-start(f32[64,2048]{1,0:T(8,128)S(1)} %get-tuple-element.55), channel_id=1, source_target_pairs={{0,16},{8,24},{16,0},{24,8},{1,17},{9,25},{17,1},{25,9},{2,18},{10... | collective-permute-start | bytes 1572872 | tf_op jit(solution)/shard_map/ppermute | solution.py:376
  30.0 15.0 %collective-permute-start.5 = (f32[64,2048]{1,0:T(8,128)S(1)}, f32[64,2048]{1,0:T(8,128)S(1)}, u32[]{:S(2)}, u32[]{:S(2)}) collective-permute-start(f32[64,2048]{1,0:T(8,128)S(1)} %get-tuple-element.53), channel_id=1, source_target_pairs={{0,8},{8,0},{16,24},{24,16},{1,9},{9,1},{17,25},{25,17},{2,10},{10... | collective-permute-start | bytes 1572872 | tf_op jit(solution)/shard_map/ppermute | solution.py:376
  32.5 23.6 %collective-permute-start.3 = (f32[64,2048]{1,0:T(8,128)S(1)}, f32[64,2048]{1,0:T(8,128)S(1)}, u32[]{:S(2)}, u32[]{:S(2)}) collective-permute-start(f32[64,2048]{1,0:T(8,128)S(1)} %get-tuple-element.50), channel_id=1, source_target_pairs={{0,8},{8,0},{16,24},{24,16},{1,9},{9,1},{17,25},{25,17},{2,10},{10... | collective-permute-start | bytes 1572872 | tf_op jit(solution)/shard_map/ppermute | solution.py:376
  33.1 23.0 %collective-permute-start.4 = (f32[64,2048]{1,0:T(8,128)S(1)}, f32[64,2048]{1,0:T(8,128)S(1)}, u32[]{:S(2)}, u32[]{:S(2)}) collective-permute-start(f32[64,2048]{1,0:T(8,128)S(1)} %get-tuple-element.51), channel_id=1, source_target_pairs={{0,16},{8,24},{16,0},{24,8},{1,17},{9,25},{17,1},{25,9},{2,18},{10... | collective-permute-start | bytes 1572872 | tf_op jit(solution)/shard_map/ppermute | solution.py:376
  43.2 20.7 %collective-permute-start.8 = (f32[64,2048]{1,0:T(8,128)S(1)}, f32[64,2048]{1,0:T(8,128)S(1)}, u32[]{:S(2)}, u32[]{:S(2)}) collective-permute-start(f32[64,2048]{1,0:T(8,128)S(1)} %add.52), channel_id=1, source_target_pairs={{0,8},{8,0},{16,24},{24,16},{1,9},{9,1},{17,25},{25,17},{2,10},{10... | collective-permute-start | bytes 1572872 | tf_op jit(solution)/shard_map/ppermute | solution.py:376
  45.0 18.9 %collective-permute-start.6 = (f32[64,2048]{1,0:T(8,128)S(1)}, f32[64,2048]{1,0:T(8,128)S(1)}, u32[]{:S(2)}, u32[]{:S(2)}) collective-permute-start(f32[64,2048]{1,0:T(8,128)S(1)} %add.51), channel_id=1, source_target_pairs={{0,16},{8,24},{16,0},{24,8},{1,17},{9,25},{17,1},{25,9},{2,18},{10... | collective-permute-start | bytes 1572872 | tf_op jit(solution)/shard_map/ppermute | solution.py:376
  64.1 14.9 %collective-permute-start.9 = (f32[64,2048]{1,0:T(8,128)S(1)}, f32[64,2048]{1,0:T(8,128)S(1)}, u32[]{:S(2)}, u32[]{:S(2)}) collective-permute-start(f32[64,2048]{1,0:T(8,128)S(1)} %get-tuple-element.56.refs_0_), channel_id=1, source_target_pairs={{0,16},{8,24},{16,0},{24,8},{1,17},{9,25},{17,1},{25,9},{2,18},{10... | collective-permute-start | bytes 1572872 | tf_op jit(solution)/shard_map/ppermute | solution.py:376
  65.0 15.7 %collective-permute-start.11 = (f32[64,2048]{1,0:T(8,128)S(1)}, f32[64,2048]{1,0:T(8,128)S(1)}, u32[]{:S(2)}, u32[]{:S(2)}) collective-permute-start(f32[64,2048]{1,0:T(8,128)S(1)} %get-tuple-element.57.refs_1_), channel_id=1, source_target_pairs={{0,8},{8,0},{16,24},{24,16},{1,9},{9,1},{17,25},{25,17},{2,10},{10... | collective-permute-start | bytes 1572872 | tf_op jit(solution)/shard_map/ppermute | solution.py:376
  66.1 25.0 %collective-permute-start.13 = (f32[64,2048]{1,0:T(8,128)S(1)}, f32[64,2048]{1,0:T(8,128)S(1)}, u32[]{:S(2)}, u32[]{:S(2)}) collective-permute-start(f32[64,2048]{1,0:T(8,128)S(1)} %get-tuple-element.56.refs_0_), channel_id=1, source_target_pairs={{0,8},{8,0},{16,24},{24,16},{1,9},{9,1},{17,25},{25,17},{2,10},{10... | collective-permute-start | bytes 1572872 | tf_op jit(solution)/shard_map/ppermute | solution.py:376
  67.0 24.1 %collective-permute-start.14 = (f32[64,2048]{1,0:T(8,128)S(1)}, f32[64,2048]{1,0:T(8,128)S(1)}, u32[]{:S(2)}, u32[]{:S(2)}) collective-permute-start(f32[64,2048]{1,0:T(8,128)S(1)} %get-tuple-element.57.refs_1_), channel_id=1, source_target_pairs={{0,16},{8,24},{16,0},{24,8},{1,17},{9,25},{17,1},{25,9},{2,18},{10... | collective-permute-start | bytes 1572872 | tf_op jit(solution)/shard_map/ppermute | solution.py:376
  79.0 19.3 %collective-permute-start.10 = (f32[64,2048]{1,0:T(8,128)S(1)}, f32[64,2048]{1,0:T(8,128)S(1)}, u32[]{:S(2)}, u32[]{:S(2)}) collective-permute-start(f32[64,2048]{1,0:T(8,128)S(1)} %collective-permute-done.9.refs_0_), channel_id=1, source_target_pairs={{0,8},{8,0},{16,24},{24,16},{1,9},{9,1},{17,25},{25,17},{2,10},{10... | collective-permute-start | bytes 1572872 | tf_op jit(solution)/shard_map/ppermute | solution.py:376
  80.7 17.6 %collective-permute-start.12 = (f32[64,2048]{1,0:T(8,128)S(1)}, f32[64,2048]{1,0:T(8,128)S(1)}, u32[]{:S(2)}, u32[]{:S(2)}) collective-permute-start(f32[64,2048]{1,0:T(8,128)S(1)} %collective-permute-done.11.refs_1_), channel_id=1, source_target_pairs={{0,16},{8,24},{16,0},{24,8},{1,17},{9,25},{17,1},{25,9},{2,18},{10... | collective-permute-start | bytes 1572872 | tf_op jit(solution)/shard_map/ppermute | solution.py:376
  101.5 4.9 %collective-permute-start.16 = (f32[64,384]{1,0:T(8,128)S(1)}, f32[64,384]{1,0:T(8,128)S(1)}, u32[]{:S(2)}, u32[]{:S(2)}) collective-permute-start(f32[64,384]{1,0:T(8,128)S(1)} %add.53), channel_id=1, source_target_pairs={{0,2},{1,3},{2,0},{3,1},{4,6},{5,7},{6,4},{7,5},{8,10},{9,11},{10,... | collective-permute-start | bytes 294920 | tf_op jit(solution)/shard_map/ppermute | solution.py:376
  106.4 7.1 %collective-permute-start.17 = (f32[64,384]{1,0:T(8,128)S(1)}, f32[64,384]{1,0:T(8,128)S(1)}, u32[]{:S(2)}, u32[]{:S(2)}) collective-permute-start(f32[64,384]{1,0:T(8,128)S(1)} %add.54), channel_id=1, source_target_pairs={{0,4},{1,5},{2,6},{3,7},{4,0},{5,1},{6,2},{7,3},{8,12},{9,13},{10,... | collective-permute-start | bytes 294920 | tf_op jit(solution)/shard_map/ppermute | solution.py:376
  114.6 14.9 %collective-permute-start.22 = (f32[64,2048]{1,0:T(8,128)S(1)}, f32[64,2048]{1,0:T(8,128)S(1)}, u32[]{:S(2)}, u32[]{:S(2)}) collective-permute-start(f32[64,2048]{1,0:T(8,128)S(1)} %get-tuple-element.70), channel_id=1, source_target_pairs={{0,16},{8,24},{16,0},{24,8},{1,17},{9,25},{17,1},{25,9},{2,18},{10... | collective-permute-start | bytes 1572872 | tf_op jit(solution)/shard_map/ppermute | solution.py:376
  115.9 15.3 %collective-permute-start.20 = (f32[64,2048]{1,0:T(8,128)S(1)}, f32[64,2048]{1,0:T(8,128)S(1)}, u32[]{:S(2)}, u32[]{:S(2)}) collective-permute-start(f32[64,2048]{1,0:T(8,128)S(1)} %get-tuple-element.68), channel_id=1, source_target_pairs={{0,8},{8,0},{16,24},{24,16},{1,9},{9,1},{17,25},{25,17},{2,10},{10... | collective-permute-start | bytes 1572872 | tf_op jit(solution)/shard_map/ppermute | solution.py:376
  118.4 23.6 %collective-permute-start.18 = (f32[64,2048]{1,0:T(8,128)S(1)}, f32[64,2048]{1,0:T(8,128)S(1)}, u32[]{:S(2)}, u32[]{:S(2)}) collective-permute-start(f32[64,2048]{1,0:T(8,128)S(1)} %get-tuple-element.65), channel_id=1, source_target_pairs={{0,8},{8,0},{16,24},{24,16},{1,9},{9,1},{17,25},{25,17},{2,10},{10... | collective-permute-start | bytes 1572872 | tf_op jit(solution)/shard_map/ppermute | solution.py:376
  119.0 23.0 %collective-permute-start.19 = (f32[64,2048]{1,0:T(8,128)S(1)}, f32[64,2048]{1,0:T(8,128)S(1)}, u32[]{:S(2)}, u32[]{:S(2)}) collective-permute-start(f32[64,2048]{1,0:T(8,128)S(1)} %get-tuple-element.66), channel_id=1, source_target_pairs={{0,16},{8,24},{16,0},{24,8},{1,17},{9,25},{17,1},{25,9},{2,18},{10... | collective-permute-start | bytes 1572872 | tf_op jit(solution)/shard_map/ppermute | solution.py:376
  129.6 20.4 %collective-permute-start.23 = (f32[64,2048]{1,0:T(8,128)S(1)}, f32[64,2048]{1,0:T(8,128)S(1)}, u32[]{:S(2)}, u32[]{:S(2)}) collective-permute-start(f32[64,2048]{1,0:T(8,128)S(1)} %add.57), channel_id=1, source_target_pairs={{0,8},{8,0},{16,24},{24,16},{1,9},{9,1},{17,25},{25,17},{2,10},{10... | collective-permute-start | bytes 1572872 | tf_op jit(solution)/shard_map/ppermute | solution.py:376
  131.2 18.8 %collective-permute-start.21 = (f32[64,2048]{1,0:T(8,128)S(1)}, f32[64,2048]{1,0:T(8,128)S(1)}, u32[]{:S(2)}, u32[]{:S(2)}) collective-permute-start(f32[64,2048]{1,0:T(8,128)S(1)} %add.56), channel_id=1, source_target_pairs={{0,16},{8,24},{16,0},{24,8},{1,17},{9,25},{17,1},{25,9},{2,18},{10... | collective-permute-start | bytes 1572872 | tf_op jit(solution)/shard_map/ppermute | solution.py:376
  152.9 4.3 %collective-permute-start.25 = (f32[64,64]{1,0:T(8,128)S(1)}, f32[64,64]{1,0:T(8,128)S(1)}, u32[]{:S(2)}, u32[]{:S(2)}) collective-permute-start(f32[64,64]{1,0:T(8,128)S(1)} %get-tuple-element.71), channel_id=1, source_target_pairs={{0,16},{8,24},{16,0},{24,8},{1,17},{9,25},{17,1},{25,9},{2,18},{10... | collective-permute-start | bytes 49160 | tf_op jit(solution)/shard_map/ppermute | solution.py:376
  153.7 5.1 %collective-permute-start.26 = (f32[64,64]{1,0:T(8,128)S(1)}, f32[64,64]{1,0:T(8,128)S(1)}, u32[]{:S(2)}, u32[]{:S(2)}) collective-permute-start(f32[64,64]{1,0:T(8,128)S(1)} %get-tuple-element.71), channel_id=1, source_target_pairs={{0,24},{8,16},{16,8},{24,0},{1,25},{9,17},{17,9},{25,1},{2,26},{10... | collective-permute-start | bytes 49160 | tf_op jit(solution)/shard_map/ppermute | solution.py:376
  158.9 15.0 %collective-permute-start.30 = (f32[64,2048]{1,0:T(8,128)S(1)}, f32[64,2048]{1,0:T(8,128)S(1)}, u32[]{:S(2)}, u32[]{:S(2)}) collective-permute-start(f32[64,2048]{1,0:T(8,128)S(1)} %get-tuple-element.79.refs_0_), channel_id=1, source_target_pairs={{0,16},{8,24},{16,0},{24,8},{1,17},{9,25},{17,1},{25,9},{2,18},{10... | collective-permute-start | bytes 1572872 | tf_op jit(solution)/shard_map/ppermute | solution.py:376
  160.1 14.5 %collective-permute-start.32 = (f32[64,2048]{1,0:T(8,128)S(1)}, f32[64,2048]{1,0:T(8,128)S(1)}, u32[]{:S(2)}, u32[]{:S(2)}) collective-permute-start(f32[64,2048]{1,0:T(8,128)S(1)} %get-tuple-element.80.refs_1_), channel_id=1, source_target_pairs={{0,8},{8,0},{16,24},{24,16},{1,9},{9,1},{17,25},{25,17},{2,10},{10... | collective-permute-start | bytes 1572872 | tf_op jit(solution)/shard_map/ppermute | solution.py:376
  160.6 24.6 %collective-permute-start.34 = (f32[64,2048]{1,0:T(8,128)S(1)}, f32[64,2048]{1,0:T(8,128)S(1)}, u32[]{:S(2)}, u32[]{:S(2)}) collective-permute-start(f32[64,2048]{1,0:T(8,128)S(1)} %get-tuple-element.79.refs_0_), channel_id=1, source_target_pairs={{0,8},{8,0},{16,24},{24,16},{1,9},{9,1},{17,25},{25,17},{2,10},{10... | collective-permute-start | bytes 1572872 | tf_op jit(solution)/shard_map/ppermute | solution.py:376
  162.1 23.1 %collective-permute-start.35 = (f32[64,2048]{1,0:T(8,128)S(1)}, f32[64,2048]{1,0:T(8,128)S(1)}, u32[]{:S(2)}, u32[]{:S(2)}) collective-permute-start(f32[64,2048]{1,0:T(8,128)S(1)} %get-tuple-element.80.refs_1_), channel_id=1, source_target_pairs={{0,16},{8,24},{16,0},{24,8},{1,17},{9,25},{17,1},{25,9},{2,18},{10... | collective-permute-start | bytes 1572872 | tf_op jit(solution)/shard_map/ppermute | solution.py:376
  164.2 4.0 %collective-permute-start.28 = (f32[64,64]{1,0:T(8,128)S(1)}, f32[64,64]{1,0:T(8,128)S(1)}, u32[]{:S(2)}, u32[]{:S(2)}) collective-permute-start(f32[64,64]{1,0:T(8,128)S(1)} %add.61), channel_id=1, source_target_pairs={{0,2},{1,3},{2,0},{3,1},{4,6},{5,7},{6,4},{7,5},{8,10},{9,11},{10,... | collective-permute-start | bytes 49160 | tf_op jit(solution)/shard_map/ppermute | solution.py:376
  168.2 5.6 %collective-permute-start.29 = (f32[64,64]{1,0:T(8,128)S(1)}, f32[64,64]{1,0:T(8,128)S(1)}, u32[]{:S(2)}, u32[]{:S(2)}) collective-permute-start(f32[64,64]{1,0:T(8,128)S(1)} %add.62), channel_id=1, source_target_pairs={{0,4},{1,5},{2,6},{3,7},{4,0},{5,1},{6,2},{7,3},{8,12},{9,13},{10,... | collective-permute-start | bytes 49160 | tf_op jit(solution)/shard_map/ppermute | solution.py:376
  173.8 17.5 %collective-permute-start.31 = (f32[64,2048]{1,0:T(8,128)S(1)}, f32[64,2048]{1,0:T(8,128)S(1)}, u32[]{:S(2)}, u32[]{:S(2)}) collective-permute-start(f32[64,2048]{1,0:T(8,128)S(1)} %collective-permute-done.30.refs_2_), channel_id=1, source_target_pairs={{0,8},{8,0},{16,24},{24,16},{1,9},{9,1},{17,25},{25,17},{2,10},{10... | collective-permute-start | bytes 1572872 | tf_op jit(solution)/shard_map/ppermute | solution.py:376
  174.5 16.8 %collective-permute-start.33 = (f32[64,2048]{1,0:T(8,128)S(1)}, f32[64,2048]{1,0:T(8,128)S(1)}, u32[]{:S(2)}, u32[]{:S(2)}) collective-permute-start(f32[64,2048]{1,0:T(8,128)S(1)} %collective-permute-done.32.refs_3_), channel_id=1, source_target_pairs={{0,16},{8,24},{16,0},{24,8},{1,17},{9,25},{17,1},{25,9},{2,18},{10... | collective-permute-start | bytes 1572872 | tf_op jit(solution)/shard_map/ppermute | solution.py:376
  (4 other events, 8.0 us)

commit v5 on v4

--- a/solution.py
+++ b/solution.py
@@ -11,7 +11,7 @@
 BF16 = jnp.bfloat16
 STEP = 1024
 CHUNK = 2048
-SLOTS = 4
+SLOTS = 7
 ROWS = 16
 GROUP = 4
 VMEM_LIMIT = 24 * 1024 * 1024
@@ -82,6 +82,8 @@
         "pass_on": (2 * i + m, 4 + 2 * j + k),
         "away_first": (2 * k + m, 4 + 2 * m + k),
         "away_second": (2 * k + j, 4 + 2 * m + i),
+        "over_x": (2 * k + j, 4 + 2 * j + k),
+        "over_y": (2 * i + m, 4 + 2 * m + i),
     }
 
 
@@ -106,7 +108,7 @@
 
     mass_copy = pltpu.make_async_copy(mass, mass_out, more_sems.at[0])
     mass_copy.start()
-    for index in range(SLOTS - 1):
+    for index in range(min(SLOTS - 1, count)):
         for copy in copies(index):
             copy.start()
     places = places_of("own")
@@ -144,6 +146,7 @@
 
 def first_coefficients(locked, vectors, mass, unit, total):
     (held, rows), new = locked.shape, vectors.shape[0]
+    slots = min(SLOTS, rows // CHUNK)
     in_hbm = [pltpu.with_memory_space_constraint(x, pltpu.HBM) for x in (locked, vectors, mass)]
     return pl.pallas_call(
         functools.partial(first_kernel, total),
@@ -158,11 +161,11 @@
         in_specs=[HBM] * 3,
         out_specs=[VMEM] * 6,
         scratch_shapes=[
-            pltpu.VMEM((SLOTS, held, CHUNK), F32),
-            pltpu.VMEM((SLOTS, new, CHUNK), F32),
+            pltpu.VMEM((slots, held, CHUNK), F32),
+            pltpu.VMEM((slots, new, CHUNK), F32),
             pltpu.VMEM((2, 3 * new, CHUNK), BF16),
             pltpu.VMEM((2 * held, 3 * new), F32),
-            pltpu.SemaphoreType.DMA((2, SLOTS)),
+            pltpu.SemaphoreType.DMA((2, slots)),
             pltpu.SemaphoreType.DMA((3,)),
         ],
         compiler_params=PARAMS,
@@ -212,7 +215,9 @@
     gram = grams[0]
     for place in range(1, 8):
         gram = gram + grams[place]
-    out[...] = jnp.concatenate([second, gram, jnp.zeros_like(gram)], axis=1) * (1.0 / total)
+    flat = new * new // held
+    gram = jnp.concatenate([gram[row : row + flat] for row in range(0, new, flat)], axis=1)
+    out[...] = jnp.concatenate([second, gram], axis=0) * (1.0 / total)
 
 
 def second_coefficients(mode, high, low, mass, blocks, total, *others):
@@ -221,7 +226,7 @@
     pieces = pltpu.VMEM((count, 3 * new, unit), BF16)
     scratch = [pltpu.VMEM((2 * held, 3 * new), F32), pieces, pieces]
     if mode == "far":
-        shapes = [array(new, held + 2 * new)]
+        shapes = [array(new + new * new // held, held)]
         scratch.insert(0, pltpu.VMEM((8, new, new), F32))
     else:
         shapes = [array(new, held), array(count, new, new)]
@@ -240,7 +245,7 @@
     base, outs = refs[:bases], refs[bases:]
     new, unit = outs[0].shape
     held = high.shape[0]
-    pieces = thirds(coef[:, :held])
+    pieces = thirds(coef[:new, :])
     pieces = jnp.concatenate([pieces, pieces], axis=1)
     places = places_of(*names)
     for which, place in enumerate(places):
@@ -252,8 +257,8 @@
             outs[which][:, here] = base[taken_off][:, here] - term if taken_off >= 0 else term
 
 
-def corrections(names, coef, high, low, unit, base=()):
-    new, held, count = coef.shape[0], high.shape[0], 2 * len(names)
+def corrections(names, coef, high, low, new, unit, base=()):
+    held, count = high.shape[0], 2 * len(names)
     return pl.pallas_call(
         functools.partial(corrections_kernel, names, len(base)),
         out_shape=[array(new, unit)] * count,
@@ -310,13 +315,14 @@
 
 def factor_kernel(both, upper_out, inverse_out):
     size = upper_out.shape[0]
-    held = both.shape[1] - 2 * size
-    upper_out[...], inverse_out[...] = eliminate(both[:, held : held + size])
+    packed = both[size:, :]
+    gram = jnp.concatenate([packed[:, lane : lane + size] for lane in range(0, packed.shape[1], size)], axis=0)
+    upper_out[...], inverse_out[...] = eliminate(gram)
 
 
 def middle_kernel(total, mass, inverse, *refs):
     ins, outs = refs[:6], refs[6:]
-    new, unit = outs[0].shape
+    new, unit = ins[0].shape
     left = spread(inverse[...])
     places = places_of("own")
     acc = jnp.zeros((new, new), F32)
@@ -325,9 +331,9 @@
             span = pl.ds(start, STEP)
             projected = ins[which][:, span] - ins[2 + which][:, span] - ins[4 + which][:, span]
             middle = apply_left(left, projected)
-            outs[which][:, span] = middle
+            outs[0][pl.ds(which * new, new), span] = middle
             acc = acc + gram_of(middle, mass[:, columns(place, unit, start, STEP)])
-    outs[2][...] = acc * (1.0 / total)
+    outs[1][...] = acc * (1.0 / total)
 
 
 def last_kernel(gram, upper_one, factor_out, inverse_out):
@@ -338,16 +344,17 @@
     inverse_out[...] = inverse
 
 
-def finish_kernel(names, inverse, *refs):
-    count = 2 * len(names)
-    blocks, (out, buf, sems) = refs[:count], refs[-3:]
-    unit = blocks[0].shape[1]
+def finish_kernel(order, given, inverse, *refs):
+    blocks, (out, buf, sems) = refs[:given], refs[-3:]
+    new, unit = buf.shape[1:]
     left = spread(inverse[...])
+    stack = blocks[0].shape[0] // new
     copies = []
-    for which, place in enumerate(places_of(*names)):
+    for which, place in enumerate(places_of(*order)):
+        rows = pl.ds(which % stack * new, new)
         for start in range(0, unit, STEP):
             span = pl.ds(start, STEP)
-            buf[which, :, span] = apply_left(left, blocks[which][:, span])
+            buf[which, :, span] = apply_left(left, blocks[which // stack][rows, span])
         copy = pltpu.make_async_copy(buf.at[which], out.at[:, columns(place, unit)], sems.at[which])
         copy.start()
         copies.append(copy)
@@ -355,17 +362,17 @@
         copy.wait()
 
 
-def finish(names, inverse, blocks, rows, target=None):
-    new, unit = blocks[0].shape
-    count = len(blocks)
+def finish(order, inverse, blocks, new, rows, target=None):
+    unit = blocks[0].shape[1]
+    given, count = len(blocks), len(blocks) * blocks[0].shape[0] // new
     extra = [] if target is None else [target]
     return pl.pallas_call(
-        functools.partial(finish_kernel, names),
+        functools.partial(finish_kernel, order, given),
         out_shape=array(new, rows),
-        in_specs=[VMEM] * (1 + count) + [HBM] * len(extra),
+        in_specs=[VMEM] * (1 + given) + [HBM] * len(extra),
         out_specs=HBM,
         scratch_shapes=[pltpu.VMEM((count, new, unit), F32), pltpu.SemaphoreType.DMA((count,))],
-        input_output_aliases={} if target is None else {1 + count: 0},
+        input_output_aliases={} if target is None else {1 + given: 0},
         compiler_params=PARAMS,
         cost_estimate=cost(18 * new * new * count * unit, 8 * new * count * unit),
     )(inverse, *blocks, *extra)
@@ -392,11 +399,11 @@
     first, high, low, mass, *here = first_coefficients(locked, vectors, mass.reshape(1, rows), unit, total)
 
     def scatter_sum(coef, base):
-        a1, b1 = corrections(("away_first",), coef, high, low, unit)
+        a1, b1 = corrections(("away_first",), coef, high, low, new, unit)
         ra1, rb1 = flip(a1, "col", 1), flip(b1, "col", 2)
-        a2, b2 = corrections(("away_second",), coef, high, low, unit)
+        a2, b2 = corrections(("away_second",), coef, high, low, new, unit)
         ra2, rb2 = flip(a2, "col", 1), flip(b2, "col", 2)
-        a3, b3, a4, b4 = corrections(("pass_on", "own"), coef, high, low, unit, base)
+        a3, b3, a4, b4 = corrections(("pass_on", "own"), coef, high, low, new, unit, base)
         ra3, rb3 = flip(a3 + ra1, "col", 2), flip(b3 + rb1, "col", 1)
         return a4, b4, ra2, rb2, ra3, rb3
 
@@ -427,19 +434,19 @@
         compiler_params=PARAMS,
         cost_estimate=cost(1e6, 1e5),
     )(second)
-    a, b, gram = pl.pallas_call(
+    pair, gram = pl.pallas_call(
         functools.partial(middle_kernel, total),
-        out_shape=[array(new, unit)] * 2 + [array(new, new)],
+        out_shape=[array(2 * new, unit), array(new, new)],
         in_specs=[VMEM] * 8,
-        out_specs=[VMEM] * 3,
+        out_specs=[VMEM] * 2,
         compiler_params=PARAMS,
         cost_estimate=cost(36 * new * new * 2 * unit, 24 * new * unit),
     )(mass, inverse, *parts)
+    over_x, over_y = flip(pair, "col", 1), flip(pair, "col", 2)
+    gram = sum_over(gram, "row")
     one, two, three = (flip(gram, "col", n) for n in (1, 2, 3))
-    one, two, three, a, b = lax.optimization_barrier((one, two, three, a, b))
-    gram = sum_over((gram + one) + (two + three), "row")
-    ay, bx = flip(a, "col", 2), flip(b, "col", 1)
-    ax, by = flip(a, "col", 1), flip(b, "col", 2)
+    one, two, three, ay, bx = lax.optimization_barrier((one, two, three, over_y[:new], over_x[new:]))
+    gram = (gram + one) + (two + three)
     far = flip(ay, "col", 1), flip(bx, "col", 2)
     factor, inverse = pl.pallas_call(
         last_kernel,
@@ -449,8 +456,8 @@
         compiler_params=PARAMS,
         cost_estimate=cost(5e9, 1e5),
     )(gram, upper)
-    appended = finish(("own",) + NEAR, inverse, (a, b, ay, bx, ax, by), rows)
-    appended = finish(FAR, inverse, far, rows, appended)
+    appended = finish(("own", "over_x", "over_y"), inverse, (pair, over_x, over_y), new, rows)
+    appended = finish(FAR, inverse, far, new, rows, appended)
     return (appended, factor)
 
 

time: 195 us -> 192 us (0.985)
  waiting for transfers between devices: 106 us -> 102 us
  Pallas kernels: 39.9 us -> 42.1 us
    ppermute x36 -> x34, waiting for transfers between devices: 106 us -> 102 us  [flip(): return lax.ppermute(x, axis, [(i, i ^ bit) for i in range(size)])]
    pallas_call x1, Pallas kernels: 14.4 us -> 16.6 us  [first_coefficients(): pl.pallas_call(functools.partial(first_kernel, total), out_shape=[array(n...]
    ppermute x36 -> x34, starting transfers between devices: 45.8 us -> 44.9 us  [flip(): return lax.ppermute(x, axis, [(i, i ^ bit) for i in range(size)])]
  transfers between devices with their start and end apart: 36 -> 34, of which waited for: 23 -> 24; matrix products, arithmetic and copies ran while one was open for 0% -> 0% of each run, Pallas kernels for 10% -> 10%
where the time goes in v5:
time: 192 us; the launch traced here: 190 us
  waiting for transfers between devices  102 us (53%)
  starting transfers between devices  44.9 us (23%)
  Pallas kernels  42.1 us (22%)
    ppermute x34, waiting for transfers between devices, flip(): return lax.ppermute(x, axis, [(i, i ^ bit) for i in range(size)])  102 us
    ppermute x34, starting transfers between devices, flip(): return lax.ppermute(x, axis, [(i, i ^ bit) for i in range(size)])  44.9 us
    pallas_call x1, Pallas kernels, first_coefficients(): pl.pallas_call(functools.partial(first_kernel, total), out_shape=[array(n...  16.6 us
    pallas_call x6, Pallas kernels, corrections(): pl.pallas_call(functools.partial(corrections_kernel, names, len(base)), o...  7.65 us
    pallas_call x3, Pallas kernels, second_coefficients(): pl.pallas_call(functools.partial(second_kernel, count, total, mode), out_...  7.33 us
  transfers between devices with their start and end apart: 34, of which 24 were waited for; matrix products, arithmetic and copies ran while one was open for 0% of the time, Pallas kernels for 10%

profile of v5, /device:TPU:0, one launch (start us, length us, event | category | flops | bytes accessed | tf_op | source)
XLA Modules:
  0.0 190.2 jit_solution(14986039508106455896)
XLA Ops:
  0.6 16.6 %shard_map.50 = (f32[64,256]{1,0:T(8,128)S(1)}, bf16[256,16384]{1,0:T(8,128)(2,1)S(1)}, bf16[256,16384]{1,0:T(8,128)(2,1)S(1)}, f32[1,16384]{1,0:T(1,128)S(1)}, ...) custom-call(f32[256,16384]{1,0:T(8,128)} %locked.1, f32[64,16384]{1,0:T(8,128)} %vectors.1, f32[1,16384]{1,0:T(1,128)} %bitcast.1), custom_call_target="tpu_custom_call" | custom-call | flops 3221225472 | bytes 33554432 | tf_op jit(solution)/shard_map/pallas_call | solution.py:151
  18.7 3.0 %collective-permute-start.1 = (f32[64,256]{1,0:T(8,128)S(1)}, f32[64,256]{1,0:T(8,128)S(1)}, u32[]{:S(2)}, u32[]{:S(2)}) collective-permute-start(f32[64,256]{1,0:T(8,128)S(1)} %add.48), channel_id=1, source_target_pairs={{0,2},{1,3},{2,0},{3,1},{4,6},{5,7},{6,4},{7,5},{8,10},{9,11},{10,... | collective-permute-start | bytes 196616 | tf_op jit(solution)/shard_map/ppermute | solution.py:383
  21.7 2.4 %collective-permute-done.1 = f32[64,256]{1,0:T(8,128)S(1)} collective-permute-done((f32[64,256]{1,0:T(8,128)S(1)}, f32[64,256]{1,0:T(8,128)S(1)}, u32[]{:S(2)}, u32[]{:S(2)}) %collective-permute-start.1) | collective-permute-done | bytes 65568 | tf_op jit(solution)/shard_map/ppermute | solution.py:383
  24.1 2.9 %collective-permute-start.2 = (f32[64,256]{1,0:T(8,128)S(1)}, f32[64,256]{1,0:T(8,128)S(1)}, u32[]{:S(2)}, u32[]{:S(2)}) collective-permute-start(f32[64,256]{1,0:T(8,128)S(1)} %add.49), channel_id=1, source_target_pairs={{0,4},{1,5},{2,6},{3,7},{4,0},{5,1},{6,2},{7,3},{8,12},{9,13},{10,... | collective-permute-start | bytes 196616 | tf_op jit(solution)/shard_map/ppermute | solution.py:383
  27.0 2.4 %collective-permute-done.2 = f32[64,256]{1,0:T(8,128)S(1)} collective-permute-done((f32[64,256]{1,0:T(8,128)S(1)}, f32[64,256]{1,0:T(8,128)S(1)}, u32[]{:S(2)}, u32[]{:S(2)}) %collective-permute-start.2) | collective-permute-done | bytes 65568 | tf_op jit(solution)/shard_map/ppermute | solution.py:383
  35.6 1.8 shard_map.51
  37.4 7.9 %collective-permute-done.7 = f32[64,2048]{1,0:T(8,128)S(1)} collective-permute-done((f32[64,2048]{1,0:T(8,128)S(1)}, f32[64,2048]{1,0:T(8,128)S(1)}, u32[]{:S(2)}, u32[]{:S(2)}) %collective-permute-start.7) | collective-permute-done | bytes 524320 | tf_op jit(solution)/shard_map/ppermute | solution.py:383
  48.8 9.5 %collective-permute-done.3.refs_2_ = f32[64,2048]{1,0:T(8,128)S(1)} collective-permute-done((f32[64,2048]{1,0:T(8,128)S(1)}, f32[64,2048]{1,0:T(8,128)S(1)}, u32[]{:S(2)}, u32[]{:S(2)}) %collective-permute-start.3) | collective-permute-done | bytes 524320 | tf_op jit(solution)/shard_map/ppermute | solution.py:383
  58.3 7.8 %collective-permute-done.8.refs_5_ = f32[64,2048]{1,0:T(8,128)S(1)} collective-permute-done((f32[64,2048]{1,0:T(8,128)S(1)}, f32[64,2048]{1,0:T(8,128)S(1)}, u32[]{:S(2)}, u32[]{:S(2)}) %collective-permute-start.8) | collective-permute-done | bytes 524320 | tf_op jit(solution)/shard_map/ppermute | solution.py:383
  70.4 10.8 %collective-permute-done.9.refs_0_ = f32[64,2048]{1,0:T(8,128)S(1)} collective-permute-done((f32[64,2048]{1,0:T(8,128)S(1)}, f32[64,2048]{1,0:T(8,128)S(1)}, u32[]{:S(2)}, u32[]{:S(2)}) %collective-permute-start.9) | collective-permute-done | bytes 524320 | tf_op jit(solution)/shard_map/ppermute | solution.py:383
  83.2 2.0 %shard_map.55 = (f32[64,256]{1,0:T(8,128)S(1)}, f32[2,64,64]{2,1,0:T(8,128)S(1)}) custom-call(bf16[256,16384]{1,0:T(8,128)(2,1)S(1)} %get-tuple-element.42.high, bf16[256,16384]{1,0:T(8,128)(2,1)S(1)} %get-tuple-element.43.low, f32[1,16384]{1,0:T(1,128)S(1)} %get-tuple-element.41.mass, f32[64,2048]{1,0:T(8,128)S(1)} %get-tuple-element.55.refs_0_, ...), custom_call_target="tpu_custom_call" | custom-call | flops 939524096 | bytes 5242880 | tf_op jit(solution)/shard_map/pallas_call | solution.py:233
  85.2 8.0 %collective-permute-done.13.refs_2_ = f32[64,2048]{1,0:T(8,128)S(1)} collective-permute-done((f32[64,2048]{1,0:T(8,128)S(1)}, f32[64,2048]{1,0:T(8,128)S(1)}, u32[]{:S(2)}, u32[]{:S(2)}) %collective-permute-start.13) | collective-permute-done | bytes 524320 | tf_op jit(solution)/shard_map/ppermute | solution.py:383
  93.3 3.4 %shard_map.56 = (f32[64,256]{1,0:T(8,128)S(1)}, f32[4,64,64]{2,1,0:T(8,128)S(1)}) custom-call(bf16[256,16384]{1,0:T(8,128)(2,1)S(1)} %get-tuple-element.42.high, bf16[256,16384]{1,0:T(8,128)(2,1)S(1)} %get-tuple-element.43.low, f32[1,16384]{1,0:T(1,128)S(1)} %get-tuple-element.41.mass, f32[64,2048]{1,0:T(8,128)S(1)} %collective-permute-done.9.refs_0_, ...), custom_call_target="tpu_custom_call" | custom-call | flops 1879048192 | bytes 10485760 | tf_op jit(solution)/shard_map/pallas_call | solution.py:233
  96.7 3.8 %collective-permute-done.10.refs_0_ = f32[64,2048]{1,0:T(8,128)S(1)} collective-permute-done((f32[64,2048]{1,0:T(8,128)S(1)}, f32[64,2048]{1,0:T(8,128)S(1)}, u32[]{:S(2)}, u32[]{:S(2)}) %collective-permute-start.10) | collective-permute-done | bytes 524320 | tf_op jit(solution)/shard_map/ppermute | solution.py:383
  100.4 1.9 %shard_map.57 = f32[80,256]{1,0:T(8,128)S(1)} custom-call(bf16[256,16384]{1,0:T(8,128)(2,1)S(1)} %get-tuple-element.42.high, bf16[256,16384]{1,0:T(8,128)(2,1)S(1)} %get-tuple-element.43.low, f32[1,16384]{1,0:T(1,128)S(1)} %get-tuple-element.41.mass, f32[64,2048]{1,0:T(8,128)S(1)} %collective-permute-done.10.refs_0_, ...), custom_call_target="tpu_custom_call" | custom-call | flops 939524096 | bytes 5242880 | tf_op jit(solution)/shard_map/pallas_call | solution.py:233
  104.8 3.5 %collective-permute-done.16 = f32[80,256]{1,0:T(8,128)S(1)} collective-permute-done((f32[80,256]{1,0:T(8,128)S(1)}, f32[80,256]{1,0:T(8,128)S(1)}, u32[]{:S(2)}, u32[]{:S(2)}) %collective-permute-start.16) | collective-permute-done | bytes 81952 | tf_op jit(solution)/shard_map/ppermute | solution.py:383
  108.3 2.4 %collective-permute-start.17 = (f32[80,256]{1,0:T(8,128)S(1)}, f32[80,256]{1,0:T(8,128)S(1)}, u32[]{:S(2)}, u32[]{:S(2)}) collective-permute-start(f32[80,256]{1,0:T(8,128)S(1)} %add.54), channel_id=1, source_target_pairs={{0,4},{1,5},{2,6},{3,7},{4,0},{5,1},{6,2},{7,3},{8,12},{9,13},{10,... | collective-permute-start | bytes 245768 | tf_op jit(solution)/shard_map/ppermute | solution.py:383
  110.7 4.0 %collective-permute-done.17 = f32[80,256]{1,0:T(8,128)S(1)} collective-permute-done((f32[80,256]{1,0:T(8,128)S(1)}, f32[80,256]{1,0:T(8,128)S(1)}, u32[]{:S(2)}, u32[]{:S(2)}) %collective-permute-start.17) | collective-permute-done | bytes 81952 | tf_op jit(solution)/shard_map/ppermute | solution.py:383
  121.0 1.8 shard_map.59
  122.8 7.9 %collective-permute-done.22 = f32[64,2048]{1,0:T(8,128)S(1)} collective-permute-done((f32[64,2048]{1,0:T(8,128)S(1)}, f32[64,2048]{1,0:T(8,128)S(1)}, u32[]{:S(2)}, u32[]{:S(2)}) %collective-permute-start.22) | collective-permute-done | bytes 524320 | tf_op jit(solution)/shard_map/ppermute | solution.py:383
  133.7 2.3 %shard_map.58 = (f32[64,64]{1,0:T(8,128)S(1)}, f32[64,64]{1,0:T(8,128)S(1)}) custom-call(f32[80,256]{1,0:T(8,128)S(1)} %add.55.both.coef), custom_call_target="tpu_custom_call" | custom-call | flops 1000000 | bytes 100000 | tf_op jit(solution)/shard_map/pallas_call | solution.py:429
  136.0 7.2 %collective-permute-done.18.refs_2_ = f32[64,2048]{1,0:T(8,128)S(1)} collective-permute-done((f32[64,2048]{1,0:T(8,128)S(1)}, f32[64,2048]{1,0:T(8,128)S(1)}, u32[]{:S(2)}, u32[]{:S(2)}) %collective-permute-start.18) | collective-permute-done | bytes 524320 | tf_op jit(solution)/shard_map/ppermute | solution.py:383
  143.2 7.1 %collective-permute-done.23.refs_5_ = f32[64,2048]{1,0:T(8,128)S(1)} collective-permute-done((f32[64,2048]{1,0:T(8,128)S(1)}, f32[64,2048]{1,0:T(8,128)S(1)}, u32[]{:S(2)}, u32[]{:S(2)}) %collective-permute-start.23) | collective-permute-done | bytes 524320 | tf_op jit(solution)/shard_map/ppermute | solution.py:383
  155.2 2.9 %collective-permute-start.25 = (f32[64,64]{1,0:T(8,128)S(1)}, f32[64,64]{1,0:T(8,128)S(1)}, u32[]{:S(2)}, u32[]{:S(2)}) collective-permute-start(f32[64,64]{1,0:T(8,128)S(1)} %add.58), channel_id=1, source_target_pairs={{0,2},{1,3},{2,0},{3,1},{4,6},{5,7},{6,4},{7,5},{8,10},{9,11},{10,... | collective-permute-start | bytes 49160 | tf_op jit(solution)/shard_map/ppermute | solution.py:383
  158.1 1.9 collective-permute-done.25
  160.0 3.5 %collective-permute-start.26 = (f32[64,64]{1,0:T(8,128)S(1)}, f32[64,64]{1,0:T(8,128)S(1)}, u32[]{:S(2)}, u32[]{:S(2)}) collective-permute-start(f32[64,64]{1,0:T(8,128)S(1)} %add.59), channel_id=1, source_target_pairs={{0,4},{1,5},{2,6},{3,7},{4,0},{5,1},{6,2},{7,3},{8,12},{9,13},{10,... | collective-permute-start | bytes 49160 | tf_op jit(solution)/shard_map/ppermute | solution.py:383
  163.5 2.2 %collective-permute-done.26 = f32[64,64]{1,0:T(8,128)S(1)} collective-permute-done((f32[64,64]{1,0:T(8,128)S(1)}, f32[64,64]{1,0:T(8,128)S(1)}, u32[]{:S(2)}, u32[]{:S(2)}) %collective-permute-start.26) | collective-permute-done | bytes 16416 | tf_op jit(solution)/shard_map/ppermute | solution.py:383
  169.3 4.2 %collective-permute-done.30.refs_2_ = f32[128,2048]{1,0:T(8,128)S(1)} collective-permute-done((f32[128,2048]{1,0:T(8,128)S(1)}, f32[128,2048]{1,0:T(8,128)S(1)}, u32[]{:S(2)}, u32[]{:S(2)}) %collective-permute-start.30) | collective-permute-done | bytes 1048608 | tf_op jit(solution)/shard_map/ppermute | solution.py:383
  173.5 2.0 %collective-permute-done.31.refs_1_ = f32[128,2048]{1,0:T(8,128)S(1)} collective-permute-done((f32[128,2048]{1,0:T(8,128)S(1)}, f32[128,2048]{1,0:T(8,128)S(1)}, u32[]{:S(2)}, u32[]{:S(2)}) %collective-permute-start.31) | collective-permute-done | bytes 1048608 | tf_op jit(solution)/shard_map/ppermute | solution.py:383
  179.9 3.0 %shard_map.63 = (f32[64,64]{1,0:T(8,128)}, f32[64,64]{1,0:T(8,128)S(1)}) custom-call(f32[64,64]{1,0:T(8,128)S(1)} %add_add_fusion.gram, f32[64,64]{1,0:T(8,128)S(1)} %get-tuple-element.75.upper_one), custom_call_target="tpu_custom_call" | custom-call | flops 5000000000 | bytes 100000 | tf_op jit(solution)/shard_map/pallas_call | solution.py:451
  182.9 2.3 %shard_map.64.refs_2_ = f32[64,16384]{1,0:T(8,128)} custom-call(f32[64,64]{1,0:T(8,128)S(1)} %get-tuple-element.76.inverse, f32[128,2048]{1,0:T(8,128)S(1)} %get-tuple-element.71.refs_0_, f32[128,2048]{1,0:T(8,128)S(1)} %collective-permute-done.31.refs_1_, f32[128,2048]{1,0:T(8,128)S(1)} %collective-permute-done.30.refs_2_), custom_call_target="tpu_custom_call" | custom-call | flops 905969664 | bytes 6291456 | tf_op jit(solution)/shard_map/pallas_call | solution.py:369
  185.2 2.0 %collective-permute-done.32.refs_0_ = f32[64,2048]{1,0:T(8,128)S(1)} collective-permute-done((f32[64,2048]{1,0:T(8,128)S(1)}, f32[64,2048]{1,0:T(8,128)S(1)}, u32[]{:S(2)}, u32[]{:S(2)}) %collective-permute-start.32) | collective-permute-done | bytes 524320 | tf_op jit(solution)/shard_map/ppermute | solution.py:383
  (68 shorter events, 44.8 us)
Async XLA Ops:
  17.2 1.4 collective-permute-start
  18.7 5.4 %collective-permute-start.1 = (f32[64,256]{1,0:T(8,128)S(1)}, f32[64,256]{1,0:T(8,128)S(1)}, u32[]{:S(2)}, u32[]{:S(2)}) collective-permute-start(f32[64,256]{1,0:T(8,128)S(1)} %add.48), channel_id=1, source_target_pairs={{0,2},{1,3},{2,0},{3,1},{4,6},{5,7},{6,4},{7,5},{8,10},{9,11},{10,... | collective-permute-start | bytes 196616 | tf_op jit(solution)/shard_map/ppermute | solution.py:383
  24.1 5.3 %collective-permute-start.2 = (f32[64,256]{1,0:T(8,128)S(1)}, f32[64,256]{1,0:T(8,128)S(1)}, u32[]{:S(2)}, u32[]{:S(2)}) collective-permute-start(f32[64,256]{1,0:T(8,128)S(1)} %add.49), channel_id=1, source_target_pairs={{0,4},{1,5},{2,6},{3,7},{4,0},{5,1},{6,2},{7,3},{8,12},{9,13},{10,... | collective-permute-start | bytes 196616 | tf_op jit(solution)/shard_map/ppermute | solution.py:383
  30.4 14.9 %collective-permute-start.7 = (f32[64,2048]{1,0:T(8,128)S(1)}, f32[64,2048]{1,0:T(8,128)S(1)}, u32[]{:S(2)}, u32[]{:S(2)}) collective-permute-start(f32[64,2048]{1,0:T(8,128)S(1)} %get-tuple-element.54), channel_id=1, source_target_pairs={{0,16},{8,24},{16,0},{24,8},{1,17},{9,25},{17,1},{25,9},{2,18},{10... | collective-permute-start | bytes 1572872 | tf_op jit(solution)/shard_map/ppermute | solution.py:383
  32.2 15.0 %collective-permute-start.5 = (f32[64,2048]{1,0:T(8,128)S(1)}, f32[64,2048]{1,0:T(8,128)S(1)}, u32[]{:S(2)}, u32[]{:S(2)}) collective-permute-start(f32[64,2048]{1,0:T(8,128)S(1)} %get-tuple-element.52), channel_id=1, source_target_pairs={{0,8},{8,0},{16,24},{24,16},{1,9},{9,1},{17,25},{25,17},{2,10},{10... | collective-permute-start | bytes 1572872 | tf_op jit(solution)/shard_map/ppermute | solution.py:383
  34.7 23.6 %collective-permute-start.3 = (f32[64,2048]{1,0:T(8,128)S(1)}, f32[64,2048]{1,0:T(8,128)S(1)}, u32[]{:S(2)}, u32[]{:S(2)}) collective-permute-start(f32[64,2048]{1,0:T(8,128)S(1)} %get-tuple-element.49), channel_id=1, source_target_pairs={{0,8},{8,0},{16,24},{24,16},{1,9},{9,1},{17,25},{25,17},{2,10},{10... | collective-permute-start | bytes 1572872 | tf_op jit(solution)/shard_map/ppermute | solution.py:383
  35.3 23.0 %collective-permute-start.4 = (f32[64,2048]{1,0:T(8,128)S(1)}, f32[64,2048]{1,0:T(8,128)S(1)}, u32[]{:S(2)}, u32[]{:S(2)}) collective-permute-start(f32[64,2048]{1,0:T(8,128)S(1)} %get-tuple-element.50), channel_id=1, source_target_pairs={{0,16},{8,24},{16,0},{24,8},{1,17},{9,25},{17,1},{25,9},{2,18},{10... | collective-permute-start | bytes 1572872 | tf_op jit(solution)/shard_map/ppermute | solution.py:383
  45.4 20.7 %collective-permute-start.8 = (f32[64,2048]{1,0:T(8,128)S(1)}, f32[64,2048]{1,0:T(8,128)S(1)}, u32[]{:S(2)}, u32[]{:S(2)}) collective-permute-start(f32[64,2048]{1,0:T(8,128)S(1)} %add.52), channel_id=1, source_target_pairs={{0,8},{8,0},{16,24},{24,16},{1,9},{9,1},{17,25},{25,17},{2,10},{10... | collective-permute-start | bytes 1572872 | tf_op jit(solution)/shard_map/ppermute | solution.py:383
  47.2 18.9 %collective-permute-start.6 = (f32[64,2048]{1,0:T(8,128)S(1)}, f32[64,2048]{1,0:T(8,128)S(1)}, u32[]{:S(2)}, u32[]{:S(2)}) collective-permute-start(f32[64,2048]{1,0:T(8,128)S(1)} %add.51), channel_id=1, source_target_pairs={{0,16},{8,24},{16,0},{24,8},{1,17},{9,25},{17,1},{25,9},{2,18},{10... | collective-permute-start | bytes 1572872 | tf_op jit(solution)/shard_map/ppermute | solution.py:383
  66.2 14.9 %collective-permute-start.9 = (f32[64,2048]{1,0:T(8,128)S(1)}, f32[64,2048]{1,0:T(8,128)S(1)}, u32[]{:S(2)}, u32[]{:S(2)}) collective-permute-start(f32[64,2048]{1,0:T(8,128)S(1)} %get-tuple-element.55.refs_0_), channel_id=1, source_target_pairs={{0,16},{8,24},{16,0},{24,8},{1,17},{9,25},{17,1},{25,9},{2,18},{10... | collective-permute-start | bytes 1572872 | tf_op jit(solution)/shard_map/ppermute | solution.py:383
  67.2 15.7 %collective-permute-start.11 = (f32[64,2048]{1,0:T(8,128)S(1)}, f32[64,2048]{1,0:T(8,128)S(1)}, u32[]{:S(2)}, u32[]{:S(2)}) collective-permute-start(f32[64,2048]{1,0:T(8,128)S(1)} %get-tuple-element.56.refs_1_), channel_id=1, source_target_pairs={{0,8},{8,0},{16,24},{24,16},{1,9},{9,1},{17,25},{25,17},{2,10},{10... | collective-permute-start | bytes 1572872 | tf_op jit(solution)/shard_map/ppermute | solution.py:383
  68.3 25.0 %collective-permute-start.13 = (f32[64,2048]{1,0:T(8,128)S(1)}, f32[64,2048]{1,0:T(8,128)S(1)}, u32[]{:S(2)}, u32[]{:S(2)}) collective-permute-start(f32[64,2048]{1,0:T(8,128)S(1)} %get-tuple-element.55.refs_0_), channel_id=1, source_target_pairs={{0,8},{8,0},{16,24},{24,16},{1,9},{9,1},{17,25},{25,17},{2,10},{10... | collective-permute-start | bytes 1572872 | tf_op jit(solution)/shard_map/ppermute | solution.py:383
  69.2 24.1 %collective-permute-start.14 = (f32[64,2048]{1,0:T(8,128)S(1)}, f32[64,2048]{1,0:T(8,128)S(1)}, u32[]{:S(2)}, u32[]{:S(2)}) collective-permute-start(f32[64,2048]{1,0:T(8,128)S(1)} %get-tuple-element.56.refs_1_), channel_id=1, source_target_pairs={{0,16},{8,24},{16,0},{24,8},{1,17},{9,25},{17,1},{25,9},{2,18},{10... | collective-permute-start | bytes 1572872 | tf_op jit(solution)/shard_map/ppermute | solution.py:383
  81.2 19.3 %collective-permute-start.10 = (f32[64,2048]{1,0:T(8,128)S(1)}, f32[64,2048]{1,0:T(8,128)S(1)}, u32[]{:S(2)}, u32[]{:S(2)}) collective-permute-start(f32[64,2048]{1,0:T(8,128)S(1)} %collective-permute-done.9.refs_0_), channel_id=1, source_target_pairs={{0,8},{8,0},{16,24},{24,16},{1,9},{9,1},{17,25},{25,17},{2,10},{10... | collective-permute-start | bytes 1572872 | tf_op jit(solution)/shard_map/ppermute | solution.py:383
  82.8 17.6 %collective-permute-start.12 = (f32[64,2048]{1,0:T(8,128)S(1)}, f32[64,2048]{1,0:T(8,128)S(1)}, u32[]{:S(2)}, u32[]{:S(2)}) collective-permute-start(f32[64,2048]{1,0:T(8,128)S(1)} %collective-permute-done.11.refs_1_), channel_id=1, source_target_pairs={{0,16},{8,24},{16,0},{24,8},{1,17},{9,25},{17,1},{25,9},{2,18},{10... | collective-permute-start | bytes 1572872 | tf_op jit(solution)/shard_map/ppermute | solution.py:383
  103.7 4.6 %collective-permute-start.16 = (f32[80,256]{1,0:T(8,128)S(1)}, f32[80,256]{1,0:T(8,128)S(1)}, u32[]{:S(2)}, u32[]{:S(2)}) collective-permute-start(f32[80,256]{1,0:T(8,128)S(1)} %add.53), channel_id=1, source_target_pairs={{0,2},{1,3},{2,0},{3,1},{4,6},{5,7},{6,4},{7,5},{8,10},{9,11},{10,... | collective-permute-start | bytes 245768 | tf_op jit(solution)/shard_map/ppermute | solution.py:383
  108.3 6.4 %collective-permute-start.17 = (f32[80,256]{1,0:T(8,128)S(1)}, f32[80,256]{1,0:T(8,128)S(1)}, u32[]{:S(2)}, u32[]{:S(2)}) collective-permute-start(f32[80,256]{1,0:T(8,128)S(1)} %add.54), channel_id=1, source_target_pairs={{0,4},{1,5},{2,6},{3,7},{4,0},{5,1},{6,2},{7,3},{8,12},{9,13},{10,... | collective-permute-start | bytes 245768 | tf_op jit(solution)/shard_map/ppermute | solution.py:383
  115.8 14.9 %collective-permute-start.22 = (f32[64,2048]{1,0:T(8,128)S(1)}, f32[64,2048]{1,0:T(8,128)S(1)}, u32[]{:S(2)}, u32[]{:S(2)}) collective-permute-start(f32[64,2048]{1,0:T(8,128)S(1)} %get-tuple-element.69), channel_id=1, source_target_pairs={{0,16},{8,24},{16,0},{24,8},{1,17},{9,25},{17,1},{25,9},{2,18},{10... | collective-permute-start | bytes 1572872 | tf_op jit(solution)/shard_map/ppermute | solution.py:383
  117.1 15.3 %collective-permute-start.20 = (f32[64,2048]{1,0:T(8,128)S(1)}, f32[64,2048]{1,0:T(8,128)S(1)}, u32[]{:S(2)}, u32[]{:S(2)}) collective-permute-start(f32[64,2048]{1,0:T(8,128)S(1)} %get-tuple-element.67), channel_id=1, source_target_pairs={{0,8},{8,0},{16,24},{24,16},{1,9},{9,1},{17,25},{25,17},{2,10},{10... | collective-permute-start | bytes 1572872 | tf_op jit(solution)/shard_map/ppermute | solution.py:383
  119.6 23.6 %collective-permute-start.18 = (f32[64,2048]{1,0:T(8,128)S(1)}, f32[64,2048]{1,0:T(8,128)S(1)}, u32[]{:S(2)}, u32[]{:S(2)}) collective-permute-start(f32[64,2048]{1,0:T(8,128)S(1)} %get-tuple-element.64), channel_id=1, source_target_pairs={{0,8},{8,0},{16,24},{24,16},{1,9},{9,1},{17,25},{25,17},{2,10},{10... | collective-permute-start | bytes 1572872 | tf_op jit(solution)/shard_map/ppermute | solution.py:383
  120.1 23.0 %collective-permute-start.19 = (f32[64,2048]{1,0:T(8,128)S(1)}, f32[64,2048]{1,0:T(8,128)S(1)}, u32[]{:S(2)}, u32[]{:S(2)}) collective-permute-start(f32[64,2048]{1,0:T(8,128)S(1)} %get-tuple-element.65), channel_id=1, source_target_pairs={{0,16},{8,24},{16,0},{24,8},{1,17},{9,25},{17,1},{25,9},{2,18},{10... | collective-permute-start | bytes 1572872 | tf_op jit(solution)/shard_map/ppermute | solution.py:383
  130.8 19.5 %collective-permute-start.23 = (f32[64,2048]{1,0:T(8,128)S(1)}, f32[64,2048]{1,0:T(8,128)S(1)}, u32[]{:S(2)}, u32[]{:S(2)}) collective-permute-start(f32[64,2048]{1,0:T(8,128)S(1)} %add.57), channel_id=1, source_target_pairs={{0,8},{8,0},{16,24},{24,16},{1,9},{9,1},{17,25},{25,17},{2,10},{10... | collective-permute-start | bytes 1572872 | tf_op jit(solution)/shard_map/ppermute | solution.py:383
  132.4 17.9 %collective-permute-start.21 = (f32[64,2048]{1,0:T(8,128)S(1)}, f32[64,2048]{1,0:T(8,128)S(1)}, u32[]{:S(2)}, u32[]{:S(2)}) collective-permute-start(f32[64,2048]{1,0:T(8,128)S(1)} %add.56), channel_id=1, source_target_pairs={{0,16},{8,24},{16,0},{24,8},{1,17},{9,25},{17,1},{25,9},{2,18},{10... | collective-permute-start | bytes 1572872 | tf_op jit(solution)/shard_map/ppermute | solution.py:383
  151.6 21.8 %collective-permute-start.30 = (f32[128,2048]{1,0:T(8,128)S(1)}, f32[128,2048]{1,0:T(8,128)S(1)}, u32[]{:S(2)}, u32[]{:S(2)}) collective-permute-start(f32[128,2048]{1,0:T(8,128)S(1)} %get-tuple-element.71.refs_0_), channel_id=1, source_target_pairs={{0,16},{8,24},{16,0},{24,8},{1,17},{9,25},{17,1},{25,9},{2,18},{10... | collective-permute-start | bytes 3145736 | tf_op jit(solution)/shard_map/ppermute | solution.py:383
  152.5 23.0 %collective-permute-start.31 = (f32[128,2048]{1,0:T(8,128)S(1)}, f32[128,2048]{1,0:T(8,128)S(1)}, u32[]{:S(2)}, u32[]{:S(2)}) collective-permute-start(f32[128,2048]{1,0:T(8,128)S(1)} %get-tuple-element.71.refs_0_), channel_id=1, source_target_pairs={{0,8},{8,0},{16,24},{24,16},{1,9},{9,1},{17,25},{25,17},{2,10},{10... | collective-permute-start | bytes 3145736 | tf_op jit(solution)/shard_map/ppermute | solution.py:383
  155.2 4.8 %collective-permute-start.25 = (f32[64,64]{1,0:T(8,128)S(1)}, f32[64,64]{1,0:T(8,128)S(1)}, u32[]{:S(2)}, u32[]{:S(2)}) collective-permute-start(f32[64,64]{1,0:T(8,128)S(1)} %add.58), channel_id=1, source_target_pairs={{0,2},{1,3},{2,0},{3,1},{4,6},{5,7},{6,4},{7,5},{8,10},{9,11},{10,... | collective-permute-start | bytes 49160 | tf_op jit(solution)/shard_map/ppermute | solution.py:383
  160.0 5.8 %collective-permute-start.26 = (f32[64,64]{1,0:T(8,128)S(1)}, f32[64,64]{1,0:T(8,128)S(1)}, u32[]{:S(2)}, u32[]{:S(2)}) collective-permute-start(f32[64,64]{1,0:T(8,128)S(1)} %add.59), channel_id=1, source_target_pairs={{0,4},{1,5},{2,6},{3,7},{4,0},{5,1},{6,2},{7,3},{8,12},{9,13},{10,... | collective-permute-start | bytes 49160 | tf_op jit(solution)/shard_map/ppermute | solution.py:383
  165.8 10.4 %collective-permute-start.27 = (f32[64,64]{1,0:T(8,128)S(1)}, f32[64,64]{1,0:T(8,128)S(1)}, u32[]{:S(2)}, u32[]{:S(2)}) collective-permute-start(f32[64,64]{1,0:T(8,128)S(1)} %add.60), channel_id=1, source_target_pairs={{0,8},{8,0},{16,24},{24,16},{1,9},{9,1},{17,25},{25,17},{2,10},{10... | collective-permute-start | bytes 49160 | tf_op jit(solution)/shard_map/ppermute | solution.py:383
  166.3 9.9 %collective-permute-start.28 = (f32[64,64]{1,0:T(8,128)S(1)}, f32[64,64]{1,0:T(8,128)S(1)}, u32[]{:S(2)}, u32[]{:S(2)}) collective-permute-start(f32[64,64]{1,0:T(8,128)S(1)} %add.60), channel_id=1, source_target_pairs={{0,16},{8,24},{16,0},{24,8},{1,17},{9,25},{17,1},{25,9},{2,18},{10... | collective-permute-start | bytes 49160 | tf_op jit(solution)/shard_map/ppermute | solution.py:383
  167.5 10.4 %collective-permute-start.29 = (f32[64,64]{1,0:T(8,128)S(1)}, f32[64,64]{1,0:T(8,128)S(1)}, u32[]{:S(2)}, u32[]{:S(2)}) collective-permute-start(f32[64,64]{1,0:T(8,128)S(1)} %add.60), channel_id=1, source_target_pairs={{0,24},{8,16},{16,8},{24,0},{1,25},{9,17},{17,9},{25,1},{2,26},{10... | collective-permute-start | bytes 49160 | tf_op jit(solution)/shard_map/ppermute | solution.py:383
  177.9 9.2 %collective-permute-start.32 = (f32[64,2048]{1,0:T(8,128)S(1)}, f32[64,2048]{1,0:T(8,128)S(1)}, u32[]{:S(2)}, u32[]{:S(2)}) collective-permute-start(f32[64,2048]{1,0:T(8,128)S(1)} %slice.8), channel_id=1, source_target_pairs={{0,8},{8,0},{16,24},{24,16},{1,9},{9,1},{17,25},{25,17},{2,10},{10... | collective-permute-start | bytes 1572872 | tf_op jit(solution)/shard_map/ppermute | solution.py:383
  179.5 9.2 %collective-permute-start.33 = (f32[64,2048]{1,0:T(8,128)S(1)}, f32[64,2048]{1,0:T(8,128)S(1)}, u32[]{:S(2)}, u32[]{:S(2)}) collective-permute-start(f32[64,2048]{1,0:T(8,128)S(1)} %slice.9), channel_id=1, source_target_pairs={{0,16},{8,24},{16,0},{24,8},{1,17},{9,25},{17,1},{25,9},{2,18},{10... | collective-permute-start | bytes 1572872 | tf_op jit(solution)/shard_map/ppermute | solution.py:383
  (2 other events, 2.6 us)

commit v6 on v5

--- a/solution.py
+++ b/solution.py
@@ -10,8 +10,7 @@
 F32 = jnp.float32
 BF16 = jnp.bfloat16
 STEP = 1024
-CHUNK = 2048
-SLOTS = 7
+SLOTS = 4
 ROWS = 16
 GROUP = 4
 VMEM_LIMIT = 24 * 1024 * 1024
@@ -40,13 +39,17 @@
         high[here, span], low[here, span] = halves(source[here, :])
 
 
-def put_thirds(target, source, weights=None):
+def put_pieces(target, source, weights=None):
     size = source.shape[0]
+    count = target.shape[0] // size
     for row in range(0, size, ROWS):
-        part = source[pl.ds(row, ROWS), :]
-        part = thirds(part if weights is None else part * weights)
-        for third in range(3):
-            target[pl.ds(third * size + row, ROWS), :] = part[third * ROWS : (third + 1) * ROWS]
+        rest = source[pl.ds(row, ROWS), :]
+        rest = rest if weights is None else rest * weights
+        for piece in range(count):
+            part = rest.astype(BF16)
+            target[pl.ds(piece * size + row, ROWS), :] = part
+            if piece + 1 < count:
+                rest = rest - part.astype(F32)
 
 
 def dot_nt(a, b):
@@ -93,14 +96,16 @@
 
 
 def first_kernel(
-    total, locked, vectors, mass, out, high, low, mass_out, here_a, here_b, held_buf, new_buf, pieces, acc, sems, more_sems
+    total, locked, vectors, mass, out, he, ho, le, lo, mass_out, here_a, here_b, held_buf, new_buf, pe, po, acc, sems, more_sems
 ):
     held, rows = locked.shape
     unit = here_a.shape[1]
-    count = rows // CHUNK
+    chunk = unit // 2
+    count = rows // chunk
+    high, low, pieces = (he, ho), (le, lo), (pe, po)
 
     def copies(index):
-        span, slot = pl.ds(index * CHUNK, CHUNK), index % SLOTS
+        span, slot = pl.ds(index * chunk, chunk), index % SLOTS
         return (
             pltpu.make_async_copy(vectors.at[:, span], new_buf.at[slot], sems.at[0, slot]),
             pltpu.make_async_copy(locked.at[:, span], held_buf.at[slot], sems.at[1, slot]),
@@ -128,43 +133,46 @@
             for copy in copies(index):
                 copy.wait()
         if index > 0:
-            span = pl.ds((index - 1) * CHUNK, CHUNK)
-            left = jnp.concatenate([high[:, span], low[:, span]], axis=0)
-            term = dot_nt(left, pieces[(index - 1) % 2])
+            half, span = (index - 1) % 2, pl.ds((index - 1) // 2 * chunk, chunk)
+            left = jnp.concatenate([high[half][:, span], low[half][:, span]], axis=0)
+            term = dot_nt(left, pieces[half][...])
             if index == 1:
                 acc[...] = term
             else:
                 acc[...] += term
         if index < count:
-            span, slot = pl.ds(index * CHUNK, CHUNK), index % SLOTS
-            put_thirds(pieces.at[index % 2], new_buf.at[slot], mass_out[:, span])
-            put_halves(high, low, span, held_buf.at[slot])
+            half, slot = index % 2, index % SLOTS
+            put_pieces(pieces[half], new_buf.at[slot], mass_out[:, pl.ds(index * chunk, chunk)])
+            put_halves(high[half], low[half], pl.ds(index // 2 * chunk, chunk), held_buf.at[slot])
     for copy in own_copies:
         copy.wait()
-    out[...] = fold_rows((acc[:held] + acc[held:]).T, out.shape[0]) * (1.0 / total)
+    both = (acc[held:] + acc[:held]).T
+    new = out.shape[0]
+    out[...] = (both[new:] + both[:new]) * (1.0 / total)
 
 
 def first_coefficients(locked, vectors, mass, unit, total):
     (held, rows), new = locked.shape, vectors.shape[0]
-    slots = min(SLOTS, rows // CHUNK)
+    chunk = unit // 2
+    slots = min(SLOTS, rows // chunk)
     in_hbm = [pltpu.with_memory_space_constraint(x, pltpu.HBM) for x in (locked, vectors, mass)]
     return pl.pallas_call(
         functools.partial(first_kernel, total),
         out_shape=[
             array(new, held),
-            array(held, rows, dtype=BF16),
-            array(held, rows, dtype=BF16),
+            *[array(held, rows // 2, dtype=BF16)] * 4,
             array(1, rows),
             array(new, unit),
             array(new, unit),
         ],
         in_specs=[HBM] * 3,
-        out_specs=[VMEM] * 6,
+        out_specs=[VMEM] * 8,
         scratch_shapes=[
-            pltpu.VMEM((slots, held, CHUNK), F32),
-            pltpu.VMEM((slots, new, CHUNK), F32),
-            pltpu.VMEM((2, 3 * new, CHUNK), BF16),
-            pltpu.VMEM((2 * held, 3 * new), F32),
+            pltpu.VMEM((slots, held, chunk), F32),
+            pltpu.VMEM((slots, new, chunk), F32),
+            pltpu.VMEM((2 * new, chunk), BF16),
+            pltpu.VMEM((2 * new, chunk), BF16),
+            pltpu.VMEM((2 * held, 2 * new), F32),
             pltpu.SemaphoreType.DMA((2, slots)),
             pltpu.SemaphoreType.DMA((3,)),
         ],
@@ -178,10 +186,10 @@
     return (part[:, 2 * size :] + part[:, size : 2 * size]) + part[:, :size]
 
 
-def second_kernel(count, total, mode, high, low, mass, *refs):
+def second_kernel(count, total, mode, he, ho, le, lo, mass, *refs):
     blocks, rest = refs[:count], refs[count:]
     new, unit = blocks[0].shape
-    held = high.shape[0]
+    held = he.shape[0]
     rest, (acc, plain, weighted) = rest[:-3], rest[-3:]
     if mode == "own":
         out, grams = rest
@@ -192,10 +200,12 @@
     parts = {"own": ("own",), "near": NEAR, "far": FAR + ("own",) + NEAR}[mode]
     ids = places_of(*parts)
     for place in range(count):
-        span = columns(ids[place], unit)
-        put_thirds(weighted.at[place], blocks[place], mass[:, span])
-        put_thirds(plain.at[place], blocks[place])
-        left = jnp.concatenate([high[:, span], low[:, span], plain[place]], axis=0)
+        put_pieces(weighted.at[place], blocks[place], mass[:, columns(ids[place], unit)])
+        put_pieces(plain.at[place], blocks[place])
+        span = columns(ids[place], unit // 2)
+        high = jnp.concatenate([he[:, span], ho[:, span]], axis=1)
+        low = jnp.concatenate([le[:, span], lo[:, span]], axis=1)
+        left = jnp.concatenate([high, low, plain[place]], axis=0)
         term = dot_nt(left, weighted[place])
         grams[ids[place] if mode == "far" else place] = fold_gram(term[2 * held :], new)
         if place == 0:
@@ -220,9 +230,9 @@
     out[...] = jnp.concatenate([second, gram], axis=0) * (1.0 / total)
 
 
-def second_coefficients(mode, high, low, mass, blocks, total, *others):
+def second_coefficients(mode, split, mass, blocks, total, *others):
     new, unit = blocks[0].shape
-    held, count = high.shape[0], len(blocks)
+    held, count = split[0].shape[0], len(blocks)
     pieces = pltpu.VMEM((count, 3 * new, unit), BF16)
     scratch = [pltpu.VMEM((2 * held, 3 * new), F32), pieces, pieces]
     if mode == "far":
@@ -233,40 +243,41 @@
     return pl.pallas_call(
         functools.partial(second_kernel, count, total, mode),
         out_shape=shapes,
-        in_specs=[VMEM] * (3 + count + len(others)),
+        in_specs=[VMEM] * (5 + count + len(others)),
         out_specs=[VMEM] * len(shapes),
         scratch_shapes=scratch,
         compiler_params=PARAMS,
         cost_estimate=cost(14 * held * new * count * unit, 4 * (held + new) * count * unit),
-    )(high, low, mass, *blocks, *others)
-
-
-def corrections_kernel(names, bases, coef, high, low, *refs):
+    )(*split, mass, *blocks, *others)
+
+
+def corrections_kernel(names, bases, coef, he, ho, le, lo, *refs):
     base, outs = refs[:bases], refs[bases:]
     new, unit = outs[0].shape
-    held = high.shape[0]
+    half = unit // 2
     pieces = thirds(coef[:new, :])
     pieces = jnp.concatenate([pieces, pieces], axis=1)
     places = places_of(*names)
     for which, place in enumerate(places):
         taken_off = which - (len(places) - bases)
         for start in range(0, unit, STEP):
-            span, here = columns(place, unit, start, STEP), pl.ds(start, STEP)
+            span, here = columns(place, half, start % half, STEP), pl.ds(start, STEP)
+            high, low = (he, le) if start < half else (ho, lo)
             term = dot_nn(pieces, jnp.concatenate([high[:, span], low[:, span]], axis=0))
             term = fold_rows(term, new)
             outs[which][:, here] = base[taken_off][:, here] - term if taken_off >= 0 else term
 
 
-def corrections(names, coef, high, low, new, unit, base=()):
-    held, count = high.shape[0], 2 * len(names)
+def corrections(names, coef, split, new, unit, base=()):
+    held, count = split[0].shape[0], 2 * len(names)
     return pl.pallas_call(
         functools.partial(corrections_kernel, names, len(base)),
         out_shape=[array(new, unit)] * count,
-        in_specs=[VMEM] * (3 + len(base)),
+        in_specs=[VMEM] * (5 + len(base)),
         out_specs=[VMEM] * count,
         compiler_params=PARAMS,
         cost_estimate=cost(12 * held * new * count * unit, 4 * (held + new) * count * unit),
-    )(coef, high, low, *base)
+    )(coef, *split, *base)
 
 
 def take_off_kernel(*refs):
@@ -396,14 +407,14 @@
     new, rows = vectors.shape
     total = rows * lax.axis_size("row")
     unit = rows // 8
-    first, high, low, mass, *here = first_coefficients(locked, vectors, mass.reshape(1, rows), unit, total)
+    first, *split, mass, here_a, here_b = first_coefficients(locked, vectors, mass.reshape(1, rows), unit, total)
 
     def scatter_sum(coef, base):
-        a1, b1 = corrections(("away_first",), coef, high, low, new, unit)
+        a1, b1 = corrections(("away_first",), coef, split, new, unit)
         ra1, rb1 = flip(a1, "col", 1), flip(b1, "col", 2)
-        a2, b2 = corrections(("away_second",), coef, high, low, new, unit)
+        a2, b2 = corrections(("away_second",), coef, split, new, unit)
         ra2, rb2 = flip(a2, "col", 1), flip(b2, "col", 2)
-        a3, b3, a4, b4 = corrections(("pass_on", "own"), coef, high, low, new, unit, base)
+        a3, b3, a4, b4 = corrections(("pass_on", "own"), coef, split, new, unit, base)
         ra3, rb3 = flip(a3 + ra1, "col", 2), flip(b3 + rb1, "col", 1)
         return a4, b4, ra2, rb2, ra3, rb3
 
@@ -415,14 +426,14 @@
         out_specs=[VMEM] * 2,
         compiler_params=PARAMS,
         cost_estimate=cost(6 * new * unit, 32 * new * unit),
-    )(*scatter_sum(first, here))
+    )(*scatter_sum(first, (here_a, here_b)))
     a, b = once
     ay, bx = flip(a, "col", 2), flip(b, "col", 1)
     ax, by = flip(a, "col", 1), flip(b, "col", 2)
     far = flip(ay, "col", 1), flip(bx, "col", 2)
-    second, grams = second_coefficients("own", high, low, mass, once, total)
-    second, more = second_coefficients("near", high, low, mass, (ay, bx, ax, by), total, second)
-    (second,) = second_coefficients("far", high, low, mass, far, total, second, grams, more)
+    second, grams = second_coefficients("own", split, mass, once, total)
+    second, more = second_coefficients("near", split, mass, (ay, bx, ax, by), total, second)
+    (second,) = second_coefficients("far", split, mass, far, total, second, grams, more)
     second = sum_over(second, "row")
     parts = scatter_sum(second, once)
 
@@ -445,9 +456,8 @@
     over_x, over_y = flip(pair, "col", 1), flip(pair, "col", 2)
     gram = sum_over(gram, "row")
     one, two, three = (flip(gram, "col", n) for n in (1, 2, 3))
-    one, two, three, ay, bx = lax.optimization_barrier((one, two, three, over_y[:new], over_x[new:]))
     gram = (gram + one) + (two + three)
-    far = flip(ay, "col", 1), flip(bx, "col", 2)
+    far = flip(over_y[:new], "col", 1), flip(over_x[new:], "col", 2)
     factor, inverse = pl.pallas_call(
         last_kernel,
         out_shape=[array(new, new)] * 2,

time: 192 us -> 189 us (0.984)
  Pallas kernels: 42.1 us -> 38.6 us
    pallas_call x1, Pallas kernels: 16.6 us -> 13.1 us  [first_coefficients(): pl.pallas_call(functools.partial(first_kernel, total), out_shape=[array(n...]
  transfers between devices with their start and end apart: 34 -> 34, of which waited for: 24 -> 22; matrix products, arithmetic and copies ran while one was open for 0% -> 0% of each run, Pallas kernels for 10% -> 10%
where the time goes in v6:
time: 189 us; the launch traced here: 187 us
  waiting for transfers between devices  102 us (54%)
  starting transfers between devices  45 us (24%)
  Pallas kernels  38.6 us (20%)
    ppermute x34, waiting for transfers between devices, flip(): return lax.ppermute(x, axis, [(i, i ^ bit) for i in range(size)])  102 us
    ppermute x34, starting transfers between devices, flip(): return lax.ppermute(x, axis, [(i, i ^ bit) for i in range(size)])  45 us
    pallas_call x1, Pallas kernels, first_coefficients(): pl.pallas_call(functools.partial(first_kernel, total), out_shape=[array(n...  13.1 us
    pallas_call x6, Pallas kernels, corrections(): pl.pallas_call(functools.partial(corrections_kernel, names, len(base)), o...  7.65 us
    pallas_call x3, Pallas kernels, second_coefficients(): pl.pallas_call(functools.partial(second_kernel, count, total, mode), out_...  7.3 us
  transfers between devices with their start and end apart: 34, of which 22 were waited for; matrix products, arithmetic and copies ran while one was open for 0% of the time, Pallas kernels for 10%

profile of v6, /device:TPU:0, one launch (start us, length us, event | category | flops | bytes accessed | tf_op | source)
XLA Modules:
  0.0 186.8 jit_solution(16208062063133219532)
XLA Ops:
  0.6 13.1 %shard_map.50 = (f32[64,256]{1,0:T(8,128)S(1)}, bf16[256,8192]{1,0:T(8,128)(2,1)S(1)}, bf16[256,8192]{1,0:T(8,128)(2,1)S(1)}, bf16[256,8192]{1,0:T(8,128)(2,1)S(...) custom-call(f32[256,16384]{1,0:T(8,128)} %locked.1, ...), custom_call_target="tpu_custom_call" | custom-call | flops 3221225472 | bytes 33554432 | tf_op jit(solution)/shard_map/pallas_call | solution.py:159
  15.1 3.0 %collective-permute-start.1 = (f32[64,256]{1,0:T(8,128)S(1)}, f32[64,256]{1,0:T(8,128)S(1)}, u32[]{:S(2)}, u32[]{:S(2)}) collective-permute-start(f32[64,256]{1,0:T(8,128)S(1)} %add.48), channel_id=1, source_target_pairs={{0,2},{1,3},{2,0},{3,1},{4,6},{5,7},{6,4},{7,5},{8,10},{9,11},{10,... | collective-permute-start | bytes 196616 | tf_op jit(solution)/shard_map/ppermute | solution.py:394
  18.1 2.4 %collective-permute-done.1 = f32[64,256]{1,0:T(8,128)S(1)} collective-permute-done((f32[64,256]{1,0:T(8,128)S(1)}, f32[64,256]{1,0:T(8,128)S(1)}, u32[]{:S(2)}, u32[]{:S(2)}) %collective-permute-start.1) | collective-permute-done | bytes 65568 | tf_op jit(solution)/shard_map/ppermute | solution.py:394
  20.6 2.9 %collective-permute-start.2 = (f32[64,256]{1,0:T(8,128)S(1)}, f32[64,256]{1,0:T(8,128)S(1)}, u32[]{:S(2)}, u32[]{:S(2)}) collective-permute-start(f32[64,256]{1,0:T(8,128)S(1)} %add.49), channel_id=1, source_target_pairs={{0,4},{1,5},{2,6},{3,7},{4,0},{5,1},{6,2},{7,3},{8,12},{9,13},{10,... | collective-permute-start | bytes 196616 | tf_op jit(solution)/shard_map/ppermute | solution.py:394
  23.5 2.4 %collective-permute-done.2 = f32[64,256]{1,0:T(8,128)S(1)} collective-permute-done((f32[64,256]{1,0:T(8,128)S(1)}, f32[64,256]{1,0:T(8,128)S(1)}, u32[]{:S(2)}, u32[]{:S(2)}) %collective-permute-start.2) | collective-permute-done | bytes 65568 | tf_op jit(solution)/shard_map/ppermute | solution.py:394
  26.9 1.8 collective-permute-start.7
  32.1 1.8 shard_map.51
  33.9 7.9 %collective-permute-done.7 = f32[64,2048]{1,0:T(8,128)S(1)} collective-permute-done((f32[64,2048]{1,0:T(8,128)S(1)}, f32[64,2048]{1,0:T(8,128)S(1)}, u32[]{:S(2)}, u32[]{:S(2)}) %collective-permute-start.7) | collective-permute-done | bytes 524320 | tf_op jit(solution)/shard_map/ppermute | solution.py:394
  45.3 9.5 %collective-permute-done.3.refs_2_ = f32[64,2048]{1,0:T(8,128)S(1)} collective-permute-done((f32[64,2048]{1,0:T(8,128)S(1)}, f32[64,2048]{1,0:T(8,128)S(1)}, u32[]{:S(2)}, u32[]{:S(2)}) %collective-permute-start.3) | collective-permute-done | bytes 524320 | tf_op jit(solution)/shard_map/ppermute | solution.py:394
  54.8 7.8 %collective-permute-done.8.refs_5_ = f32[64,2048]{1,0:T(8,128)S(1)} collective-permute-done((f32[64,2048]{1,0:T(8,128)S(1)}, f32[64,2048]{1,0:T(8,128)S(1)}, u32[]{:S(2)}, u32[]{:S(2)}) %collective-permute-start.8) | collective-permute-done | bytes 524320 | tf_op jit(solution)/shard_map/ppermute | solution.py:394
  66.8 10.8 %collective-permute-done.9.refs_0_ = f32[64,2048]{1,0:T(8,128)S(1)} collective-permute-done((f32[64,2048]{1,0:T(8,128)S(1)}, f32[64,2048]{1,0:T(8,128)S(1)}, u32[]{:S(2)}, u32[]{:S(2)}) %collective-permute-start.9) | collective-permute-done | bytes 524320 | tf_op jit(solution)/shard_map/ppermute | solution.py:394
  79.7 2.0 %shard_map.55 = (f32[64,256]{1,0:T(8,128)S(1)}, f32[2,64,64]{2,1,0:T(8,128)S(1)}) custom-call(bf16[256,8192]{1,0:T(8,128)(2,1)S(1)} %get-tuple-element.39.he, bf16[256,8192]{1,0:T(8,128)(2,1)S(1)} %get-tuple-element.40.ho, bf16[256,8192]{1,0:T(8,128)(2,1)S(1)} %get-tuple-element.41.le, bf16[256,8192]{1,0:T(8,128)(2,1)S(1)} %get-tuple-element.42.lo, ...), custom_call_target="tpu_custom_call" | custom-call | flops 939524096 | bytes 5242880 | tf_op jit(solution)/shard_map/pallas_call | solution.py:243
  81.7 8.1 %collective-permute-done.13.refs_2_ = f32[64,2048]{1,0:T(8,128)S(1)} collective-permute-done((f32[64,2048]{1,0:T(8,128)S(1)}, f32[64,2048]{1,0:T(8,128)S(1)}, u32[]{:S(2)}, u32[]{:S(2)}) %collective-permute-start.13) | collective-permute-done | bytes 524320 | tf_op jit(solution)/shard_map/ppermute | solution.py:394
  89.8 3.4 %shard_map.56 = (f32[64,256]{1,0:T(8,128)S(1)}, f32[4,64,64]{2,1,0:T(8,128)S(1)}) custom-call(bf16[256,8192]{1,0:T(8,128)(2,1)S(1)} %get-tuple-element.39.he, bf16[256,8192]{1,0:T(8,128)(2,1)S(1)} %get-tuple-element.40.ho, bf16[256,8192]{1,0:T(8,128)(2,1)S(1)} %get-tuple-element.41.le, bf16[256,8192]{1,0:T(8,128)(2,1)S(1)} %get-tuple-element.42.lo, ...), custom_call_target="tpu_custom_call" | custom-call | flops 1879048192 | bytes 10485760 | tf_op jit(solution)/shard_map/pallas_call | solution.py:243
  93.1 3.8 %collective-permute-done.10.refs_0_ = f32[64,2048]{1,0:T(8,128)S(1)} collective-permute-done((f32[64,2048]{1,0:T(8,128)S(1)}, f32[64,2048]{1,0:T(8,128)S(1)}, u32[]{:S(2)}, u32[]{:S(2)}) %collective-permute-start.10) | collective-permute-done | bytes 524320 | tf_op jit(solution)/shard_map/ppermute | solution.py:394
  96.9 1.9 %shard_map.57 = f32[80,256]{1,0:T(8,128)S(1)} custom-call(bf16[256,8192]{1,0:T(8,128)(2,1)S(1)} %get-tuple-element.39.he, bf16[256,8192]{1,0:T(8,128)(2,1)S(1)} %get-tuple-element.40.ho, bf16[256,8192]{1,0:T(8,128)(2,1)S(1)} %get-tuple-element.41.le, bf16[256,8192]{1,0:T(8,128)(2,1)S(1)} %get-tuple-element.42.lo, f32[1,16384]{1,0:T(1,128)S(1)} %get-tuple-element.38.mass, ...), custom_call_target="tpu_custom_call" | custom-call | flops 939524096 | bytes 5242880 | tf_op jit(solution)/shard_map/pallas_call | solution.py:243
  101.3 3.5 %collective-permute-done.16 = f32[80,256]{1,0:T(8,128)S(1)} collective-permute-done((f32[80,256]{1,0:T(8,128)S(1)}, f32[80,256]{1,0:T(8,128)S(1)}, u32[]{:S(2)}, u32[]{:S(2)}) %collective-permute-start.16) | collective-permute-done | bytes 81952 | tf_op jit(solution)/shard_map/ppermute | solution.py:394
  104.8 2.4 %collective-permute-start.17 = (f32[80,256]{1,0:T(8,128)S(1)}, f32[80,256]{1,0:T(8,128)S(1)}, u32[]{:S(2)}, u32[]{:S(2)}) collective-permute-start(f32[80,256]{1,0:T(8,128)S(1)} %add.54), channel_id=1, source_target_pairs={{0,4},{1,5},{2,6},{3,7},{4,0},{5,1},{6,2},{7,3},{8,12},{9,13},{10,... | collective-permute-start | bytes 245768 | tf_op jit(solution)/shard_map/ppermute | solution.py:394
  107.2 4.0 %collective-permute-done.17 = f32[80,256]{1,0:T(8,128)S(1)} collective-permute-done((f32[80,256]{1,0:T(8,128)S(1)}, f32[80,256]{1,0:T(8,128)S(1)}, u32[]{:S(2)}, u32[]{:S(2)}) %collective-permute-start.17) | collective-permute-done | bytes 81952 | tf_op jit(solution)/shard_map/ppermute | solution.py:394
  117.4 1.8 shard_map.59
  119.3 7.9 %collective-permute-done.22 = f32[64,2048]{1,0:T(8,128)S(1)} collective-permute-done((f32[64,2048]{1,0:T(8,128)S(1)}, f32[64,2048]{1,0:T(8,128)S(1)}, u32[]{:S(2)}, u32[]{:S(2)}) %collective-permute-start.22) | collective-permute-done | bytes 524320 | tf_op jit(solution)/shard_map/ppermute | solution.py:394
  130.1 2.3 %shard_map.58 = (f32[64,64]{1,0:T(8,128)S(1)}, f32[64,64]{1,0:T(8,128)S(1)}) custom-call(f32[80,256]{1,0:T(8,128)S(1)} %add.55.both.coef), custom_call_target="tpu_custom_call" | custom-call | flops 1000000 | bytes 100000 | tf_op jit(solution)/shard_map/pallas_call | solution.py:440
  132.5 7.2 %collective-permute-done.18.refs_2_ = f32[64,2048]{1,0:T(8,128)S(1)} collective-permute-done((f32[64,2048]{1,0:T(8,128)S(1)}, f32[64,2048]{1,0:T(8,128)S(1)}, u32[]{:S(2)}, u32[]{:S(2)}) %collective-permute-start.18) | collective-permute-done | bytes 524320 | tf_op jit(solution)/shard_map/ppermute | solution.py:394
  139.6 7.1 %collective-permute-done.23.refs_5_ = f32[64,2048]{1,0:T(8,128)S(1)} collective-permute-done((f32[64,2048]{1,0:T(8,128)S(1)}, f32[64,2048]{1,0:T(8,128)S(1)}, u32[]{:S(2)}, u32[]{:S(2)}) %collective-permute-start.23) | collective-permute-done | bytes 524320 | tf_op jit(solution)/shard_map/ppermute | solution.py:394
  151.7 2.9 %collective-permute-start.25 = (f32[64,64]{1,0:T(8,128)S(1)}, f32[64,64]{1,0:T(8,128)S(1)}, u32[]{:S(2)}, u32[]{:S(2)}) collective-permute-start(f32[64,64]{1,0:T(8,128)S(1)} %add.58), channel_id=1, source_target_pairs={{0,2},{1,3},{2,0},{3,1},{4,6},{5,7},{6,4},{7,5},{8,10},{9,11},{10,... | collective-permute-start | bytes 49160 | tf_op jit(solution)/shard_map/ppermute | solution.py:394
  154.6 1.9 %collective-permute-done.25 = f32[64,64]{1,0:T(8,128)S(1)} collective-permute-done((f32[64,64]{1,0:T(8,128)S(1)}, f32[64,64]{1,0:T(8,128)S(1)}, u32[]{:S(2)}, u32[]{:S(2)}) %collective-permute-start.25) | collective-permute-done | bytes 16416 | tf_op jit(solution)/shard_map/ppermute | solution.py:394
  156.5 3.5 %collective-permute-start.26 = (f32[64,64]{1,0:T(8,128)S(1)}, f32[64,64]{1,0:T(8,128)S(1)}, u32[]{:S(2)}, u32[]{:S(2)}) collective-permute-start(f32[64,64]{1,0:T(8,128)S(1)} %add.59), channel_id=1, source_target_pairs={{0,4},{1,5},{2,6},{3,7},{4,0},{5,1},{6,2},{7,3},{8,12},{9,13},{10,... | collective-permute-start | bytes 49160 | tf_op jit(solution)/shard_map/ppermute | solution.py:394
  160.0 2.2 %collective-permute-done.26 = f32[64,64]{1,0:T(8,128)S(1)} collective-permute-done((f32[64,64]{1,0:T(8,128)S(1)}, f32[64,64]{1,0:T(8,128)S(1)}, u32[]{:S(2)}, u32[]{:S(2)}) %collective-permute-start.26) | collective-permute-done | bytes 16416 | tf_op jit(solution)/shard_map/ppermute | solution.py:394
  165.8 6.8 %collective-permute-done.27 = f32[64,64]{1,0:T(8,128)S(1)} collective-permute-done((f32[64,64]{1,0:T(8,128)S(1)}, f32[64,64]{1,0:T(8,128)S(1)}, u32[]{:S(2)}, u32[]{:S(2)}) %collective-permute-start.27) | collective-permute-done | bytes 16416 | tf_op jit(solution)/shard_map/ppermute | solution.py:394
  176.4 3.0 %shard_map.63 = (f32[64,64]{1,0:T(8,128)}, f32[64,64]{1,0:T(8,128)S(1)}) custom-call(f32[64,64]{1,0:T(8,128)S(1)} %add_add_fusion.gram, f32[64,64]{1,0:T(8,128)S(1)} %get-tuple-element.70.upper_one), custom_call_target="tpu_custom_call" | custom-call | flops 5000000000 | bytes 100000 | tf_op jit(solution)/shard_map/pallas_call | solution.py:461
  179.4 2.3 %shard_map.64.refs_2_ = f32[64,16384]{1,0:T(8,128)} custom-call(f32[64,64]{1,0:T(8,128)S(1)} %get-tuple-element.71.inverse, f32[128,2048]{1,0:T(8,128)S(1)} %get-tuple-element.72.refs_0_, f32[128,2048]{1,0:T(8,128)S(1)} %collective-permute-done.32.refs_1_, f32[128,2048]{1,0:T(8,128)S(1)} %collective-permute-done.30.refs_2_), custom_call_target="tpu_custom_call" | custom-call | flops 905969664 | bytes 6291456 | tf_op jit(solution)/shard_map/pallas_call | solution.py:380
  181.7 1.8 collective-permute-done.31.refs_0_
  (68 shorter events, 42.6 us)
Async XLA Ops:
  13.7 1.4 collective-permute-start
  15.1 5.4 %collective-permute-start.1 = (f32[64,256]{1,0:T(8,128)S(1)}, f32[64,256]{1,0:T(8,128)S(1)}, u32[]{:S(2)}, u32[]{:S(2)}) collective-permute-start(f32[64,256]{1,0:T(8,128)S(1)} %add.48), channel_id=1, source_target_pairs={{0,2},{1,3},{2,0},{3,1},{4,6},{5,7},{6,4},{7,5},{8,10},{9,11},{10,... | collective-permute-start | bytes 196616 | tf_op jit(solution)/shard_map/ppermute | solution.py:394
  20.6 5.3 %collective-permute-start.2 = (f32[64,256]{1,0:T(8,128)S(1)}, f32[64,256]{1,0:T(8,128)S(1)}, u32[]{:S(2)}, u32[]{:S(2)}) collective-permute-start(f32[64,256]{1,0:T(8,128)S(1)} %add.49), channel_id=1, source_target_pairs={{0,4},{1,5},{2,6},{3,7},{4,0},{5,1},{6,2},{7,3},{8,12},{9,13},{10,... | collective-permute-start | bytes 196616 | tf_op jit(solution)/shard_map/ppermute | solution.py:394
  26.9 14.9 %collective-permute-start.7 = (f32[64,2048]{1,0:T(8,128)S(1)}, f32[64,2048]{1,0:T(8,128)S(1)}, u32[]{:S(2)}, u32[]{:S(2)}) collective-permute-start(f32[64,2048]{1,0:T(8,128)S(1)} %get-tuple-element.53), channel_id=1, source_target_pairs={{0,16},{8,24},{16,0},{24,8},{1,17},{9,25},{17,1},{25,9},{2,18},{10... | collective-permute-start | bytes 1572872 | tf_op jit(solution)/shard_map/ppermute | solution.py:394
  28.7 15.0 %collective-permute-start.5 = (f32[64,2048]{1,0:T(8,128)S(1)}, f32[64,2048]{1,0:T(8,128)S(1)}, u32[]{:S(2)}, u32[]{:S(2)}) collective-permute-start(f32[64,2048]{1,0:T(8,128)S(1)} %get-tuple-element.51), channel_id=1, source_target_pairs={{0,8},{8,0},{16,24},{24,16},{1,9},{9,1},{17,25},{25,17},{2,10},{10... | collective-permute-start | bytes 1572872 | tf_op jit(solution)/shard_map/ppermute | solution.py:394
  31.2 23.6 %collective-permute-start.3 = (f32[64,2048]{1,0:T(8,128)S(1)}, f32[64,2048]{1,0:T(8,128)S(1)}, u32[]{:S(2)}, u32[]{:S(2)}) collective-permute-start(f32[64,2048]{1,0:T(8,128)S(1)} %get-tuple-element.48), channel_id=1, source_target_pairs={{0,8},{8,0},{16,24},{24,16},{1,9},{9,1},{17,25},{25,17},{2,10},{10... | collective-permute-start | bytes 1572872 | tf_op jit(solution)/shard_map/ppermute | solution.py:394
  31.8 23.0 %collective-permute-start.4 = (f32[64,2048]{1,0:T(8,128)S(1)}, f32[64,2048]{1,0:T(8,128)S(1)}, u32[]{:S(2)}, u32[]{:S(2)}) collective-permute-start(f32[64,2048]{1,0:T(8,128)S(1)} %get-tuple-element.49), channel_id=1, source_target_pairs={{0,16},{8,24},{16,0},{24,8},{1,17},{9,25},{17,1},{25,9},{2,18},{10... | collective-permute-start | bytes 1572872 | tf_op jit(solution)/shard_map/ppermute | solution.py:394
  41.9 20.7 %collective-permute-start.8 = (f32[64,2048]{1,0:T(8,128)S(1)}, f32[64,2048]{1,0:T(8,128)S(1)}, u32[]{:S(2)}, u32[]{:S(2)}) collective-permute-start(f32[64,2048]{1,0:T(8,128)S(1)} %add.52), channel_id=1, source_target_pairs={{0,8},{8,0},{16,24},{24,16},{1,9},{9,1},{17,25},{25,17},{2,10},{10... | collective-permute-start | bytes 1572872 | tf_op jit(solution)/shard_map/ppermute | solution.py:394
  43.7 18.8 %collective-permute-start.6 = (f32[64,2048]{1,0:T(8,128)S(1)}, f32[64,2048]{1,0:T(8,128)S(1)}, u32[]{:S(2)}, u32[]{:S(2)}) collective-permute-start(f32[64,2048]{1,0:T(8,128)S(1)} %add.51), channel_id=1, source_target_pairs={{0,16},{8,24},{16,0},{24,8},{1,17},{9,25},{17,1},{25,9},{2,18},{10... | collective-permute-start | bytes 1572872 | tf_op jit(solution)/shard_map/ppermute | solution.py:394
  62.7 14.9 %collective-permute-start.9 = (f32[64,2048]{1,0:T(8,128)S(1)}, f32[64,2048]{1,0:T(8,128)S(1)}, u32[]{:S(2)}, u32[]{:S(2)}) collective-permute-start(f32[64,2048]{1,0:T(8,128)S(1)} %get-tuple-element.54.refs_0_), channel_id=1, source_target_pairs={{0,16},{8,24},{16,0},{24,8},{1,17},{9,25},{17,1},{25,9},{2,18},{10... | collective-permute-start | bytes 1572872 | tf_op jit(solution)/shard_map/ppermute | solution.py:394
  63.7 15.7 %collective-permute-start.11 = (f32[64,2048]{1,0:T(8,128)S(1)}, f32[64,2048]{1,0:T(8,128)S(1)}, u32[]{:S(2)}, u32[]{:S(2)}) collective-permute-start(f32[64,2048]{1,0:T(8,128)S(1)} %get-tuple-element.55.refs_1_), channel_id=1, source_target_pairs={{0,8},{8,0},{16,24},{24,16},{1,9},{9,1},{17,25},{25,17},{2,10},{10... | collective-permute-start | bytes 1572872 | tf_op jit(solution)/shard_map/ppermute | solution.py:394
  64.8 25.0 %collective-permute-start.13 = (f32[64,2048]{1,0:T(8,128)S(1)}, f32[64,2048]{1,0:T(8,128)S(1)}, u32[]{:S(2)}, u32[]{:S(2)}) collective-permute-start(f32[64,2048]{1,0:T(8,128)S(1)} %get-tuple-element.54.refs_0_), channel_id=1, source_target_pairs={{0,8},{8,0},{16,24},{24,16},{1,9},{9,1},{17,25},{25,17},{2,10},{10... | collective-permute-start | bytes 1572872 | tf_op jit(solution)/shard_map/ppermute | solution.py:394
  65.7 24.1 %collective-permute-start.14 = (f32[64,2048]{1,0:T(8,128)S(1)}, f32[64,2048]{1,0:T(8,128)S(1)}, u32[]{:S(2)}, u32[]{:S(2)}) collective-permute-start(f32[64,2048]{1,0:T(8,128)S(1)} %get-tuple-element.55.refs_1_), channel_id=1, source_target_pairs={{0,16},{8,24},{16,0},{24,8},{1,17},{9,25},{17,1},{25,9},{2,18},{10... | collective-permute-start | bytes 1572872 | tf_op jit(solution)/shard_map/ppermute | solution.py:394
  77.6 19.3 %collective-permute-start.10 = (f32[64,2048]{1,0:T(8,128)S(1)}, f32[64,2048]{1,0:T(8,128)S(1)}, u32[]{:S(2)}, u32[]{:S(2)}) collective-permute-start(f32[64,2048]{1,0:T(8,128)S(1)} %collective-permute-done.9.refs_0_), channel_id=1, source_target_pairs={{0,8},{8,0},{16,24},{24,16},{1,9},{9,1},{17,25},{25,17},{2,10},{10... | collective-permute-start | bytes 1572872 | tf_op jit(solution)/shard_map/ppermute | solution.py:394
  79.3 17.6 %collective-permute-start.12 = (f32[64,2048]{1,0:T(8,128)S(1)}, f32[64,2048]{1,0:T(8,128)S(1)}, u32[]{:S(2)}, u32[]{:S(2)}) collective-permute-start(f32[64,2048]{1,0:T(8,128)S(1)} %collective-permute-done.11.refs_1_), channel_id=1, source_target_pairs={{0,16},{8,24},{16,0},{24,8},{1,17},{9,25},{17,1},{25,9},{2,18},{10... | collective-permute-start | bytes 1572872 | tf_op jit(solution)/shard_map/ppermute | solution.py:394
  100.2 4.6 %collective-permute-start.16 = (f32[80,256]{1,0:T(8,128)S(1)}, f32[80,256]{1,0:T(8,128)S(1)}, u32[]{:S(2)}, u32[]{:S(2)}) collective-permute-start(f32[80,256]{1,0:T(8,128)S(1)} %add.53), channel_id=1, source_target_pairs={{0,2},{1,3},{2,0},{3,1},{4,6},{5,7},{6,4},{7,5},{8,10},{9,11},{10,... | collective-permute-start | bytes 245768 | tf_op jit(solution)/shard_map/ppermute | solution.py:394
  104.8 6.5 %collective-permute-start.17 = (f32[80,256]{1,0:T(8,128)S(1)}, f32[80,256]{1,0:T(8,128)S(1)}, u32[]{:S(2)}, u32[]{:S(2)}) collective-permute-start(f32[80,256]{1,0:T(8,128)S(1)} %add.54), channel_id=1, source_target_pairs={{0,4},{1,5},{2,6},{3,7},{4,0},{5,1},{6,2},{7,3},{8,12},{9,13},{10,... | collective-permute-start | bytes 245768 | tf_op jit(solution)/shard_map/ppermute | solution.py:394
  112.2 14.9 %collective-permute-start.22 = (f32[64,2048]{1,0:T(8,128)S(1)}, f32[64,2048]{1,0:T(8,128)S(1)}, u32[]{:S(2)}, u32[]{:S(2)}) collective-permute-start(f32[64,2048]{1,0:T(8,128)S(1)} %get-tuple-element.68), channel_id=1, source_target_pairs={{0,16},{8,24},{16,0},{24,8},{1,17},{9,25},{17,1},{25,9},{2,18},{10... | collective-permute-start | bytes 1572872 | tf_op jit(solution)/shard_map/ppermute | solution.py:394
  113.5 15.3 %collective-permute-start.20 = (f32[64,2048]{1,0:T(8,128)S(1)}, f32[64,2048]{1,0:T(8,128)S(1)}, u32[]{:S(2)}, u32[]{:S(2)}) collective-permute-start(f32[64,2048]{1,0:T(8,128)S(1)} %get-tuple-element.66), channel_id=1, source_target_pairs={{0,8},{8,0},{16,24},{24,16},{1,9},{9,1},{17,25},{25,17},{2,10},{10... | collective-permute-start | bytes 1572872 | tf_op jit(solution)/shard_map/ppermute | solution.py:394
  116.0 23.6 %collective-permute-start.18 = (f32[64,2048]{1,0:T(8,128)S(1)}, f32[64,2048]{1,0:T(8,128)S(1)}, u32[]{:S(2)}, u32[]{:S(2)}) collective-permute-start(f32[64,2048]{1,0:T(8,128)S(1)} %get-tuple-element.63), channel_id=1, source_target_pairs={{0,8},{8,0},{16,24},{24,16},{1,9},{9,1},{17,25},{25,17},{2,10},{10... | collective-permute-start | bytes 1572872 | tf_op jit(solution)/shard_map/ppermute | solution.py:394
  116.6 23.0 %collective-permute-start.19 = (f32[64,2048]{1,0:T(8,128)S(1)}, f32[64,2048]{1,0:T(8,128)S(1)}, u32[]{:S(2)}, u32[]{:S(2)}) collective-permute-start(f32[64,2048]{1,0:T(8,128)S(1)} %get-tuple-element.64), channel_id=1, source_target_pairs={{0,16},{8,24},{16,0},{24,8},{1,17},{9,25},{17,1},{25,9},{2,18},{10... | collective-permute-start | bytes 1572872 | tf_op jit(solution)/shard_map/ppermute | solution.py:394
  127.2 19.5 %collective-permute-start.23 = (f32[64,2048]{1,0:T(8,128)S(1)}, f32[64,2048]{1,0:T(8,128)S(1)}, u32[]{:S(2)}, u32[]{:S(2)}) collective-permute-start(f32[64,2048]{1,0:T(8,128)S(1)} %add.57), channel_id=1, source_target_pairs={{0,8},{8,0},{16,24},{24,16},{1,9},{9,1},{17,25},{25,17},{2,10},{10... | collective-permute-start | bytes 1572872 | tf_op jit(solution)/shard_map/ppermute | solution.py:394
  128.8 17.9 %collective-permute-start.21 = (f32[64,2048]{1,0:T(8,128)S(1)}, f32[64,2048]{1,0:T(8,128)S(1)}, u32[]{:S(2)}, u32[]{:S(2)}) collective-permute-start(f32[64,2048]{1,0:T(8,128)S(1)} %add.56), channel_id=1, source_target_pairs={{0,16},{8,24},{16,0},{24,8},{1,17},{9,25},{17,1},{25,9},{2,18},{10... | collective-permute-start | bytes 1572872 | tf_op jit(solution)/shard_map/ppermute | solution.py:394
  148.1 26.2 %collective-permute-start.30 = (f32[128,2048]{1,0:T(8,128)S(1)}, f32[128,2048]{1,0:T(8,128)S(1)}, u32[]{:S(2)}, u32[]{:S(2)}) collective-permute-start(f32[128,2048]{1,0:T(8,128)S(1)} %get-tuple-element.72.refs_0_), channel_id=1, source_target_pairs={{0,16},{8,24},{16,0},{24,8},{1,17},{9,25},{17,1},{25,9},{2,18},{10... | collective-permute-start | bytes 3145736 | tf_op jit(solution)/shard_map/ppermute | solution.py:394
  149.0 26.9 %collective-permute-start.32 = (f32[128,2048]{1,0:T(8,128)S(1)}, f32[128,2048]{1,0:T(8,128)S(1)}, u32[]{:S(2)}, u32[]{:S(2)}) collective-permute-start(f32[128,2048]{1,0:T(8,128)S(1)} %get-tuple-element.72.refs_0_), channel_id=1, source_target_pairs={{0,8},{8,0},{16,24},{24,16},{1,9},{9,1},{17,25},{25,17},{2,10},{10... | collective-permute-start | bytes 3145736 | tf_op jit(solution)/shard_map/ppermute | solution.py:394
  151.7 4.8 %collective-permute-start.25 = (f32[64,64]{1,0:T(8,128)S(1)}, f32[64,64]{1,0:T(8,128)S(1)}, u32[]{:S(2)}, u32[]{:S(2)}) collective-permute-start(f32[64,64]{1,0:T(8,128)S(1)} %add.58), channel_id=1, source_target_pairs={{0,2},{1,3},{2,0},{3,1},{4,6},{5,7},{6,4},{7,5},{8,10},{9,11},{10,... | collective-permute-start | bytes 49160 | tf_op jit(solution)/shard_map/ppermute | solution.py:394
  156.5 5.8 %collective-permute-start.26 = (f32[64,64]{1,0:T(8,128)S(1)}, f32[64,64]{1,0:T(8,128)S(1)}, u32[]{:S(2)}, u32[]{:S(2)}) collective-permute-start(f32[64,64]{1,0:T(8,128)S(1)} %add.59), channel_id=1, source_target_pairs={{0,4},{1,5},{2,6},{3,7},{4,0},{5,1},{6,2},{7,3},{8,12},{9,13},{10,... | collective-permute-start | bytes 49160 | tf_op jit(solution)/shard_map/ppermute | solution.py:394
  162.3 10.3 %collective-permute-start.27 = (f32[64,64]{1,0:T(8,128)S(1)}, f32[64,64]{1,0:T(8,128)S(1)}, u32[]{:S(2)}, u32[]{:S(2)}) collective-permute-start(f32[64,64]{1,0:T(8,128)S(1)} %add.60), channel_id=1, source_target_pairs={{0,8},{8,0},{16,24},{24,16},{1,9},{9,1},{17,25},{25,17},{2,10},{10... | collective-permute-start | bytes 49160 | tf_op jit(solution)/shard_map/ppermute | solution.py:394
  162.8 9.8 %collective-permute-start.28 = (f32[64,64]{1,0:T(8,128)S(1)}, f32[64,64]{1,0:T(8,128)S(1)}, u32[]{:S(2)}, u32[]{:S(2)}) collective-permute-start(f32[64,64]{1,0:T(8,128)S(1)} %add.60), channel_id=1, source_target_pairs={{0,16},{8,24},{16,0},{24,8},{1,17},{9,25},{17,1},{25,9},{2,18},{10... | collective-permute-start | bytes 49160 | tf_op jit(solution)/shard_map/ppermute | solution.py:394
  164.0 10.2 %collective-permute-start.29 = (f32[64,64]{1,0:T(8,128)S(1)}, f32[64,64]{1,0:T(8,128)S(1)}, u32[]{:S(2)}, u32[]{:S(2)}) collective-permute-start(f32[64,64]{1,0:T(8,128)S(1)} %add.60), channel_id=1, source_target_pairs={{0,24},{8,16},{16,8},{24,0},{1,25},{9,17},{17,9},{25,1},{2,26},{10... | collective-permute-start | bytes 49160 | tf_op jit(solution)/shard_map/ppermute | solution.py:394
  174.3 9.2 %collective-permute-start.31 = (f32[64,2048]{1,0:T(8,128)S(1)}, f32[64,2048]{1,0:T(8,128)S(1)}, u32[]{:S(2)}, u32[]{:S(2)}) collective-permute-start(f32[64,2048]{1,0:T(8,128)S(1)} %slice.8), channel_id=1, source_target_pairs={{0,8},{8,0},{16,24},{24,16},{1,9},{9,1},{17,25},{25,17},{2,10},{10... | collective-permute-start | bytes 1572872 | tf_op jit(solution)/shard_map/ppermute | solution.py:394
  176.0 9.2 %collective-permute-start.33 = (f32[64,2048]{1,0:T(8,128)S(1)}, f32[64,2048]{1,0:T(8,128)S(1)}, u32[]{:S(2)}, u32[]{:S(2)}) collective-permute-start(f32[64,2048]{1,0:T(8,128)S(1)} %slice.9), channel_id=1, source_target_pairs={{0,16},{8,24},{16,0},{24,8},{1,17},{9,25},{17,1},{25,9},{2,18},{10... | collective-permute-start | bytes 1572872 | tf_op jit(solution)/shard_map/ppermute | solution.py:394
  (2 other events, 2.6 us)

commit v7 on v6

--- a/solution.py
+++ b/solution.py
@@ -132,6 +132,10 @@
                     copy.start()
             for copy in copies(index):
                 copy.wait()
+        if index < count:
+            half, slot = index % 2, index % SLOTS
+            put_pieces(pieces[half], new_buf.at[slot], mass_out[:, pl.ds(index * chunk, chunk)])
+            put_halves(high[half], low[half], pl.ds(index // 2 * chunk, chunk), held_buf.at[slot])
         if index > 0:
             half, span = (index - 1) % 2, pl.ds((index - 1) // 2 * chunk, chunk)
             left = jnp.concatenate([high[half][:, span], low[half][:, span]], axis=0)
@@ -140,10 +144,6 @@
                 acc[...] = term
             else:
                 acc[...] += term
-        if index < count:
-            half, slot = index % 2, index % SLOTS
-            put_pieces(pieces[half], new_buf.at[slot], mass_out[:, pl.ds(index * chunk, chunk)])
-            put_halves(high[half], low[half], pl.ds(index // 2 * chunk, chunk), held_buf.at[slot])
     for copy in own_copies:
         copy.wait()
     both = (acc[held:] + acc[:held]).T
@@ -347,8 +347,8 @@
     outs[1][...] = acc * (1.0 / total)
 
 
-def last_kernel(gram, upper_one, factor_out, inverse_out):
-    upper, inverse = eliminate(gram[...])
+def last_kernel(gram, one, two, three, upper_one, factor_out, inverse_out):
+    upper, inverse = eliminate((gram[...] + one[...]) + (two[...] + three[...]))
     factor_out[...] = jnp.dot(
         upper, upper_one[...], precision=lax.Precision.HIGHEST, preferred_element_type=F32
     )
@@ -456,16 +456,15 @@
     over_x, over_y = flip(pair, "col", 1), flip(pair, "col", 2)
     gram = sum_over(gram, "row")
     one, two, three = (flip(gram, "col", n) for n in (1, 2, 3))
-    gram = (gram + one) + (two + three)
     far = flip(over_y[:new], "col", 1), flip(over_x[new:], "col", 2)
     factor, inverse = pl.pallas_call(
         last_kernel,
         out_shape=[array(new, new)] * 2,
-        in_specs=[VMEM] * 2,
+        in_specs=[VMEM] * 5,
         out_specs=[VMEM] * 2,
         compiler_params=PARAMS,
         cost_estimate=cost(5e9, 1e5),
-    )(gram, upper)
+    )(gram, one, two, three, upper)
     appended = finish(("own", "over_x", "over_y"), inverse, (pair, over_x, over_y), new, rows)
     appended = finish(FAR, inverse, far, new, rows, appended)
     return (appended, factor)

time: 189 us -> 187 us (0.989)
  waiting for transfers between devices: 102 us -> 98 us
  starting transfers between devices: 45 us -> 47 us
    ppermute x34, waiting for transfers between devices: 102 us -> 98 us  [flip(): return lax.ppermute(x, axis, [(i, i ^ bit) for i in range(size)])]
    ppermute x34, starting transfers between devices: 45 us -> 47 us  [flip(): return lax.ppermute(x, axis, [(i, i ^ bit) for i in range(size)])]
where the time goes in v7:
time: 187 us; the launch traced here: 185 us
  waiting for transfers between devices  98 us (52%)
  starting transfers between devices  47 us (25%)
  Pallas kernels  38.6 us (21%)
    ppermute x34, waiting for transfers between devices, flip(): return lax.ppermute(x, axis, [(i, i ^ bit) for i in range(size)])  98 us
    ppermute x34, starting transfers between devices, flip(): return lax.ppermute(x, axis, [(i, i ^ bit) for i in range(size)])  47 us
    pallas_call x1, Pallas kernels, first_coefficients(): pl.pallas_call(functools.partial(first_kernel, total), out_shape=[array(n...  13.1 us
    pallas_call x6, Pallas kernels, corrections(): pl.pallas_call(functools.partial(corrections_kernel, names, len(base)), o...  7.65 us
    pallas_call x3, Pallas kernels, second_coefficients(): pl.pallas_call(functools.partial(second_kernel, count, total, mode), out_...  7.3 us
  transfers between devices with their start and end apart: 34, of which 22 were waited for; matrix products, arithmetic and copies ran while one was open for 0% of the time, Pallas kernels for 10%

profile of v7, /device:TPU:0, one launch (start us, length us, event | category | flops | bytes accessed | tf_op | source)
XLA Modules:
  0.0 184.9 jit_solution(3314526219746065742)
XLA Ops:
  0.6 13.1 %shard_map.50 = (f32[64,256]{1,0:T(8,128)S(1)}, bf16[256,8192]{1,0:T(8,128)(2,1)S(1)}, bf16[256,8192]{1,0:T(8,128)(2,1)S(1)}, bf16[256,8192]{1,0:T(8,128)(2,1)S(...) custom-call(f32[256,16384]{1,0:T(8,128)} %locked.1, ...), custom_call_target="tpu_custom_call" | custom-call | flops 3221225472 | bytes 33554432 | tf_op jit(solution)/shard_map/pallas_call | solution.py:159
  15.1 3.0 %collective-permute-start.1 = (f32[64,256]{1,0:T(8,128)S(1)}, f32[64,256]{1,0:T(8,128)S(1)}, u32[]{:S(2)}, u32[]{:S(2)}) collective-permute-start(f32[64,256]{1,0:T(8,128)S(1)} %add.39), channel_id=1, source_target_pairs={{0,2},{1,3},{2,0},{3,1},{4,6},{5,7},{6,4},{7,5},{8,10},{9,11},{10,... | collective-permute-start | bytes 196616 | tf_op jit(solution)/shard_map/ppermute | solution.py:394
  18.1 2.4 %collective-permute-done.1 = f32[64,256]{1,0:T(8,128)S(1)} collective-permute-done((f32[64,256]{1,0:T(8,128)S(1)}, f32[64,256]{1,0:T(8,128)S(1)}, u32[]{:S(2)}, u32[]{:S(2)}) %collective-permute-start.1) | collective-permute-done | bytes 65568 | tf_op jit(solution)/shard_map/ppermute | solution.py:394
  20.6 2.9 %collective-permute-start.2 = (f32[64,256]{1,0:T(8,128)S(1)}, f32[64,256]{1,0:T(8,128)S(1)}, u32[]{:S(2)}, u32[]{:S(2)}) collective-permute-start(f32[64,256]{1,0:T(8,128)S(1)} %add.40), channel_id=1, source_target_pairs={{0,4},{1,5},{2,6},{3,7},{4,0},{5,1},{6,2},{7,3},{8,12},{9,13},{10,... | collective-permute-start | bytes 196616 | tf_op jit(solution)/shard_map/ppermute | solution.py:394
  23.5 2.4 %collective-permute-done.2 = f32[64,256]{1,0:T(8,128)S(1)} collective-permute-done((f32[64,256]{1,0:T(8,128)S(1)}, f32[64,256]{1,0:T(8,128)S(1)}, u32[]{:S(2)}, u32[]{:S(2)}) %collective-permute-start.2) | collective-permute-done | bytes 65568 | tf_op jit(solution)/shard_map/ppermute | solution.py:394
  26.9 1.8 collective-permute-start.7
  32.1 1.8 shard_map.51
  33.9 7.9 %collective-permute-done.7 = f32[64,2048]{1,0:T(8,128)S(1)} collective-permute-done((f32[64,2048]{1,0:T(8,128)S(1)}, f32[64,2048]{1,0:T(8,128)S(1)}, u32[]{:S(2)}, u32[]{:S(2)}) %collective-permute-start.7) | collective-permute-done | bytes 524320 | tf_op jit(solution)/shard_map/ppermute | solution.py:394
  45.3 9.5 %collective-permute-done.3.refs_2_ = f32[64,2048]{1,0:T(8,128)S(1)} collective-permute-done((f32[64,2048]{1,0:T(8,128)S(1)}, f32[64,2048]{1,0:T(8,128)S(1)}, u32[]{:S(2)}, u32[]{:S(2)}) %collective-permute-start.3) | collective-permute-done | bytes 524320 | tf_op jit(solution)/shard_map/ppermute | solution.py:394
  54.8 7.8 %collective-permute-done.8.refs_5_ = f32[64,2048]{1,0:T(8,128)S(1)} collective-permute-done((f32[64,2048]{1,0:T(8,128)S(1)}, f32[64,2048]{1,0:T(8,128)S(1)}, u32[]{:S(2)}, u32[]{:S(2)}) %collective-permute-start.8) | collective-permute-done | bytes 524320 | tf_op jit(solution)/shard_map/ppermute | solution.py:394
  66.8 10.8 %collective-permute-done.9.refs_0_ = f32[64,2048]{1,0:T(8,128)S(1)} collective-permute-done((f32[64,2048]{1,0:T(8,128)S(1)}, f32[64,2048]{1,0:T(8,128)S(1)}, u32[]{:S(2)}, u32[]{:S(2)}) %collective-permute-start.9) | collective-permute-done | bytes 524320 | tf_op jit(solution)/shard_map/ppermute | solution.py:394
  79.7 2.0 %shard_map.55 = (f32[64,256]{1,0:T(8,128)S(1)}, f32[2,64,64]{2,1,0:T(8,128)S(1)}) custom-call(bf16[256,8192]{1,0:T(8,128)(2,1)S(1)} %get-tuple-element.39.he, bf16[256,8192]{1,0:T(8,128)(2,1)S(1)} %get-tuple-element.40.ho, bf16[256,8192]{1,0:T(8,128)(2,1)S(1)} %get-tuple-element.41.le, bf16[256,8192]{1,0:T(8,128)(2,1)S(1)} %get-tuple-element.42.lo, ...), custom_call_target="tpu_custom_call" | custom-call | flops 939524096 | bytes 5242880 | tf_op jit(solution)/shard_map/pallas_call | solution.py:243
  81.7 8.1 %collective-permute-done.13.refs_2_ = f32[64,2048]{1,0:T(8,128)S(1)} collective-permute-done((f32[64,2048]{1,0:T(8,128)S(1)}, f32[64,2048]{1,0:T(8,128)S(1)}, u32[]{:S(2)}, u32[]{:S(2)}) %collective-permute-start.13) | collective-permute-done | bytes 524320 | tf_op jit(solution)/shard_map/ppermute | solution.py:394
  89.8 3.4 %shard_map.56 = (f32[64,256]{1,0:T(8,128)S(1)}, f32[4,64,64]{2,1,0:T(8,128)S(1)}) custom-call(bf16[256,8192]{1,0:T(8,128)(2,1)S(1)} %get-tuple-element.39.he, bf16[256,8192]{1,0:T(8,128)(2,1)S(1)} %get-tuple-element.40.ho, bf16[256,8192]{1,0:T(8,128)(2,1)S(1)} %get-tuple-element.41.le, bf16[256,8192]{1,0:T(8,128)(2,1)S(1)} %get-tuple-element.42.lo, ...), custom_call_target="tpu_custom_call" | custom-call | flops 1879048192 | bytes 10485760 | tf_op jit(solution)/shard_map/pallas_call | solution.py:243
  93.1 3.8 %collective-permute-done.10.refs_0_ = f32[64,2048]{1,0:T(8,128)S(1)} collective-permute-done((f32[64,2048]{1,0:T(8,128)S(1)}, f32[64,2048]{1,0:T(8,128)S(1)}, u32[]{:S(2)}, u32[]{:S(2)}) %collective-permute-start.10) | collective-permute-done | bytes 524320 | tf_op jit(solution)/shard_map/ppermute | solution.py:394
  96.9 1.9 %shard_map.57 = f32[80,256]{1,0:T(8,128)S(1)} custom-call(bf16[256,8192]{1,0:T(8,128)(2,1)S(1)} %get-tuple-element.39.he, bf16[256,8192]{1,0:T(8,128)(2,1)S(1)} %get-tuple-element.40.ho, bf16[256,8192]{1,0:T(8,128)(2,1)S(1)} %get-tuple-element.41.le, bf16[256,8192]{1,0:T(8,128)(2,1)S(1)} %get-tuple-element.42.lo, f32[1,16384]{1,0:T(1,128)S(1)} %get-tuple-element.38.mass, ...), custom_call_target="tpu_custom_call" | custom-call | flops 939524096 | bytes 5242880 | tf_op jit(solution)/shard_map/pallas_call | solution.py:243
  101.3 3.5 %collective-permute-done.16 = f32[80,256]{1,0:T(8,128)S(1)} collective-permute-done((f32[80,256]{1,0:T(8,128)S(1)}, f32[80,256]{1,0:T(8,128)S(1)}, u32[]{:S(2)}, u32[]{:S(2)}) %collective-permute-start.16) | collective-permute-done | bytes 81952 | tf_op jit(solution)/shard_map/ppermute | solution.py:394
  104.8 2.4 %collective-permute-start.17 = (f32[80,256]{1,0:T(8,128)S(1)}, f32[80,256]{1,0:T(8,128)S(1)}, u32[]{:S(2)}, u32[]{:S(2)}) collective-permute-start(f32[80,256]{1,0:T(8,128)S(1)} %add.45), channel_id=1, source_target_pairs={{0,4},{1,5},{2,6},{3,7},{4,0},{5,1},{6,2},{7,3},{8,12},{9,13},{10,... | collective-permute-start | bytes 245768 | tf_op jit(solution)/shard_map/ppermute | solution.py:394
  107.2 4.0 %collective-permute-done.17 = f32[80,256]{1,0:T(8,128)S(1)} collective-permute-done((f32[80,256]{1,0:T(8,128)S(1)}, f32[80,256]{1,0:T(8,128)S(1)}, u32[]{:S(2)}, u32[]{:S(2)}) %collective-permute-start.17) | collective-permute-done | bytes 81952 | tf_op jit(solution)/shard_map/ppermute | solution.py:394
  117.4 1.8 shard_map.59
  119.3 7.9 %collective-permute-done.22 = f32[64,2048]{1,0:T(8,128)S(1)} collective-permute-done((f32[64,2048]{1,0:T(8,128)S(1)}, f32[64,2048]{1,0:T(8,128)S(1)}, u32[]{:S(2)}, u32[]{:S(2)}) %collective-permute-start.22) | collective-permute-done | bytes 524320 | tf_op jit(solution)/shard_map/ppermute | solution.py:394
  130.1 2.3 %shard_map.58 = (f32[64,64]{1,0:T(8,128)S(1)}, f32[64,64]{1,0:T(8,128)S(1)}) custom-call(f32[80,256]{1,0:T(8,128)S(1)} %add.46.both.coef), custom_call_target="tpu_custom_call" | custom-call | flops 1000000 | bytes 100000 | tf_op jit(solution)/shard_map/pallas_call | solution.py:440
  132.5 7.2 %collective-permute-done.18.refs_2_ = f32[64,2048]{1,0:T(8,128)S(1)} collective-permute-done((f32[64,2048]{1,0:T(8,128)S(1)}, f32[64,2048]{1,0:T(8,128)S(1)}, u32[]{:S(2)}, u32[]{:S(2)}) %collective-permute-start.18) | collective-permute-done | bytes 524320 | tf_op jit(solution)/shard_map/ppermute | solution.py:394
  139.6 7.1 %collective-permute-done.23.refs_5_ = f32[64,2048]{1,0:T(8,128)S(1)} collective-permute-done((f32[64,2048]{1,0:T(8,128)S(1)}, f32[64,2048]{1,0:T(8,128)S(1)}, u32[]{:S(2)}, u32[]{:S(2)}) %collective-permute-start.23) | collective-permute-done | bytes 524320 | tf_op jit(solution)/shard_map/ppermute | solution.py:394
  151.7 2.9 %collective-permute-start.25 = (f32[64,64]{1,0:T(8,128)S(1)}, f32[64,64]{1,0:T(8,128)S(1)}, u32[]{:S(2)}, u32[]{:S(2)}) collective-permute-start(f32[64,64]{1,0:T(8,128)S(1)} %add.49), channel_id=1, source_target_pairs={{0,2},{1,3},{2,0},{3,1},{4,6},{5,7},{6,4},{7,5},{8,10},{9,11},{10,... | collective-permute-start | bytes 49160 | tf_op jit(solution)/shard_map/ppermute | solution.py:394
  154.6 1.9 %collective-permute-done.25 = f32[64,64]{1,0:T(8,128)S(1)} collective-permute-done((f32[64,64]{1,0:T(8,128)S(1)}, f32[64,64]{1,0:T(8,128)S(1)}, u32[]{:S(2)}, u32[]{:S(2)}) %collective-permute-start.25) | collective-permute-done | bytes 16416 | tf_op jit(solution)/shard_map/ppermute | solution.py:394
  156.5 3.5 %collective-permute-start.26 = (f32[64,64]{1,0:T(8,128)S(1)}, f32[64,64]{1,0:T(8,128)S(1)}, u32[]{:S(2)}, u32[]{:S(2)}) collective-permute-start(f32[64,64]{1,0:T(8,128)S(1)} %add.50), channel_id=1, source_target_pairs={{0,4},{1,5},{2,6},{3,7},{4,0},{5,1},{6,2},{7,3},{8,12},{9,13},{10,... | collective-permute-start | bytes 49160 | tf_op jit(solution)/shard_map/ppermute | solution.py:394
  160.0 2.2 %collective-permute-done.26 = f32[64,64]{1,0:T(8,128)S(1)} collective-permute-done((f32[64,64]{1,0:T(8,128)S(1)}, f32[64,64]{1,0:T(8,128)S(1)}, u32[]{:S(2)}, u32[]{:S(2)}) %collective-permute-start.26) | collective-permute-done | bytes 16416 | tf_op jit(solution)/shard_map/ppermute | solution.py:394
  165.8 5.7 %collective-permute-done.30.refs_2_ = f32[128,2048]{1,0:T(8,128)S(1)} collective-permute-done((f32[128,2048]{1,0:T(8,128)S(1)}, f32[128,2048]{1,0:T(8,128)S(1)}, u32[]{:S(2)}, u32[]{:S(2)}) %collective-permute-start.30) | collective-permute-done | bytes 1048608 | tf_op jit(solution)/shard_map/ppermute | solution.py:394
  171.5 2.6 %collective-permute-start.31 = (f32[64,2048]{1,0:T(8,128)S(1)}, f32[64,2048]{1,0:T(8,128)S(1)}, u32[]{:S(2)}, u32[]{:S(2)}) collective-permute-start(f32[64,2048]{1,0:T(8,128)S(1)} %slice.8), channel_id=1, source_target_pairs={{0,8},{8,0},{16,24},{24,16},{1,9},{9,1},{17,25},{25,17},{2,10},{10... | collective-permute-start | bytes 1572872 | tf_op jit(solution)/shard_map/ppermute | solution.py:394
  176.3 3.0 %shard_map.63 = (f32[64,64]{1,0:T(8,128)}, f32[64,64]{1,0:T(8,128)S(1)}) custom-call(f32[64,64]{1,0:T(8,128)S(1)} %add.51.gram, f32[64,64]{1,0:T(8,128)S(1)} %collective-permute-done.27.one, f32[64,64]{1,0:T(8,128)S(1)} %collective-permute-done.28.two, f32[64,64]{1,0:T(8,128)S(1)} %collective-permute-done.29.three, f32[64,64]{1,0:T(8,128)S(1)} %get-tuple-element.70.upper_one), custom_call_target="tpu_custom_call" | custom-call | flops 5000000000 | bytes 100000 | tf_op jit(solution)/shard_map/pallas_call | solution.py:460
  179.3 2.3 %shard_map.64.refs_2_ = f32[64,16384]{1,0:T(8,128)} custom-call(f32[64,64]{1,0:T(8,128)S(1)} %get-tuple-element.71.inverse, f32[128,2048]{1,0:T(8,128)S(1)} %get-tuple-element.72.refs_0_, f32[128,2048]{1,0:T(8,128)S(1)} %collective-permute-done.32.refs_1_, f32[128,2048]{1,0:T(8,128)S(1)} %collective-permute-done.30.refs_2_), custom_call_target="tpu_custom_call" | custom-call | flops 905969664 | bytes 6291456 | tf_op jit(solution)/shard_map/pallas_call | solution.py:380
  (67 shorter events, 41.1 us)
Async XLA Ops:
  13.7 1.4 collective-permute-start
  15.1 5.4 %collective-permute-start.1 = (f32[64,256]{1,0:T(8,128)S(1)}, f32[64,256]{1,0:T(8,128)S(1)}, u32[]{:S(2)}, u32[]{:S(2)}) collective-permute-start(f32[64,256]{1,0:T(8,128)S(1)} %add.39), channel_id=1, source_target_pairs={{0,2},{1,3},{2,0},{3,1},{4,6},{5,7},{6,4},{7,5},{8,10},{9,11},{10,... | collective-permute-start | bytes 196616 | tf_op jit(solution)/shard_map/ppermute | solution.py:394
  20.6 5.3 %collective-permute-start.2 = (f32[64,256]{1,0:T(8,128)S(1)}, f32[64,256]{1,0:T(8,128)S(1)}, u32[]{:S(2)}, u32[]{:S(2)}) collective-permute-start(f32[64,256]{1,0:T(8,128)S(1)} %add.40), channel_id=1, source_target_pairs={{0,4},{1,5},{2,6},{3,7},{4,0},{5,1},{6,2},{7,3},{8,12},{9,13},{10,... | collective-permute-start | bytes 196616 | tf_op jit(solution)/shard_map/ppermute | solution.py:394
  26.9 14.9 %collective-permute-start.7 = (f32[64,2048]{1,0:T(8,128)S(1)}, f32[64,2048]{1,0:T(8,128)S(1)}, u32[]{:S(2)}, u32[]{:S(2)}) collective-permute-start(f32[64,2048]{1,0:T(8,128)S(1)} %get-tuple-element.53), channel_id=1, source_target_pairs={{0,16},{8,24},{16,0},{24,8},{1,17},{9,25},{17,1},{25,9},{2,18},{10... | collective-permute-start | bytes 1572872 | tf_op jit(solution)/shard_map/ppermute | solution.py:394
  28.7 15.0 %collective-permute-start.5 = (f32[64,2048]{1,0:T(8,128)S(1)}, f32[64,2048]{1,0:T(8,128)S(1)}, u32[]{:S(2)}, u32[]{:S(2)}) collective-permute-start(f32[64,2048]{1,0:T(8,128)S(1)} %get-tuple-element.51), channel_id=1, source_target_pairs={{0,8},{8,0},{16,24},{24,16},{1,9},{9,1},{17,25},{25,17},{2,10},{10... | collective-permute-start | bytes 1572872 | tf_op jit(solution)/shard_map/ppermute | solution.py:394
  31.2 23.6 %collective-permute-start.3 = (f32[64,2048]{1,0:T(8,128)S(1)}, f32[64,2048]{1,0:T(8,128)S(1)}, u32[]{:S(2)}, u32[]{:S(2)}) collective-permute-start(f32[64,2048]{1,0:T(8,128)S(1)} %get-tuple-element.48), channel_id=1, source_target_pairs={{0,8},{8,0},{16,24},{24,16},{1,9},{9,1},{17,25},{25,17},{2,10},{10... | collective-permute-start | bytes 1572872 | tf_op jit(solution)/shard_map/ppermute | solution.py:394
  31.8 23.0 %collective-permute-start.4 = (f32[64,2048]{1,0:T(8,128)S(1)}, f32[64,2048]{1,0:T(8,128)S(1)}, u32[]{:S(2)}, u32[]{:S(2)}) collective-permute-start(f32[64,2048]{1,0:T(8,128)S(1)} %get-tuple-element.49), channel_id=1, source_target_pairs={{0,16},{8,24},{16,0},{24,8},{1,17},{9,25},{17,1},{25,9},{2,18},{10... | collective-permute-start | bytes 1572872 | tf_op jit(solution)/shard_map/ppermute | solution.py:394
  41.9 20.7 %collective-permute-start.8 = (f32[64,2048]{1,0:T(8,128)S(1)}, f32[64,2048]{1,0:T(8,128)S(1)}, u32[]{:S(2)}, u32[]{:S(2)}) collective-permute-start(f32[64,2048]{1,0:T(8,128)S(1)} %add.43), channel_id=1, source_target_pairs={{0,8},{8,0},{16,24},{24,16},{1,9},{9,1},{17,25},{25,17},{2,10},{10... | collective-permute-start | bytes 1572872 | tf_op jit(solution)/shard_map/ppermute | solution.py:394
  43.7 18.8 %collective-permute-start.6 = (f32[64,2048]{1,0:T(8,128)S(1)}, f32[64,2048]{1,0:T(8,128)S(1)}, u32[]{:S(2)}, u32[]{:S(2)}) collective-permute-start(f32[64,2048]{1,0:T(8,128)S(1)} %add.42), channel_id=1, source_target_pairs={{0,16},{8,24},{16,0},{24,8},{1,17},{9,25},{17,1},{25,9},{2,18},{10... | collective-permute-start | bytes 1572872 | tf_op jit(solution)/shard_map/ppermute | solution.py:394
  62.7 14.9 %collective-permute-start.9 = (f32[64,2048]{1,0:T(8,128)S(1)}, f32[64,2048]{1,0:T(8,128)S(1)}, u32[]{:S(2)}, u32[]{:S(2)}) collective-permute-start(f32[64,2048]{1,0:T(8,128)S(1)} %get-tuple-element.54.refs_0_), channel_id=1, source_target_pairs={{0,16},{8,24},{16,0},{24,8},{1,17},{9,25},{17,1},{25,9},{2,18},{10... | collective-permute-start | bytes 1572872 | tf_op jit(solution)/shard_map/ppermute | solution.py:394
  63.7 15.7 %collective-permute-start.11 = (f32[64,2048]{1,0:T(8,128)S(1)}, f32[64,2048]{1,0:T(8,128)S(1)}, u32[]{:S(2)}, u32[]{:S(2)}) collective-permute-start(f32[64,2048]{1,0:T(8,128)S(1)} %get-tuple-element.55.refs_1_), channel_id=1, source_target_pairs={{0,8},{8,0},{16,24},{24,16},{1,9},{9,1},{17,25},{25,17},{2,10},{10... | collective-permute-start | bytes 1572872 | tf_op jit(solution)/shard_map/ppermute | solution.py:394
  64.8 25.0 %collective-permute-start.13 = (f32[64,2048]{1,0:T(8,128)S(1)}, f32[64,2048]{1,0:T(8,128)S(1)}, u32[]{:S(2)}, u32[]{:S(2)}) collective-permute-start(f32[64,2048]{1,0:T(8,128)S(1)} %get-tuple-element.54.refs_0_), channel_id=1, source_target_pairs={{0,8},{8,0},{16,24},{24,16},{1,9},{9,1},{17,25},{25,17},{2,10},{10... | collective-permute-start | bytes 1572872 | tf_op jit(solution)/shard_map/ppermute | solution.py:394
  65.7 24.1 %collective-permute-start.14 = (f32[64,2048]{1,0:T(8,128)S(1)}, f32[64,2048]{1,0:T(8,128)S(1)}, u32[]{:S(2)}, u32[]{:S(2)}) collective-permute-start(f32[64,2048]{1,0:T(8,128)S(1)} %get-tuple-element.55.refs_1_), channel_id=1, source_target_pairs={{0,16},{8,24},{16,0},{24,8},{1,17},{9,25},{17,1},{25,9},{2,18},{10... | collective-permute-start | bytes 1572872 | tf_op jit(solution)/shard_map/ppermute | solution.py:394
  77.6 19.3 %collective-permute-start.10 = (f32[64,2048]{1,0:T(8,128)S(1)}, f32[64,2048]{1,0:T(8,128)S(1)}, u32[]{:S(2)}, u32[]{:S(2)}) collective-permute-start(f32[64,2048]{1,0:T(8,128)S(1)} %collective-permute-done.9.refs_0_), channel_id=1, source_target_pairs={{0,8},{8,0},{16,24},{24,16},{1,9},{9,1},{17,25},{25,17},{2,10},{10... | collective-permute-start | bytes 1572872 | tf_op jit(solution)/shard_map/ppermute | solution.py:394
  79.3 17.6 %collective-permute-start.12 = (f32[64,2048]{1,0:T(8,128)S(1)}, f32[64,2048]{1,0:T(8,128)S(1)}, u32[]{:S(2)}, u32[]{:S(2)}) collective-permute-start(f32[64,2048]{1,0:T(8,128)S(1)} %collective-permute-done.11.refs_1_), channel_id=1, source_target_pairs={{0,16},{8,24},{16,0},{24,8},{1,17},{9,25},{17,1},{25,9},{2,18},{10... | collective-permute-start | bytes 1572872 | tf_op jit(solution)/shard_map/ppermute | solution.py:394
  100.2 4.6 %collective-permute-start.16 = (f32[80,256]{1,0:T(8,128)S(1)}, f32[80,256]{1,0:T(8,128)S(1)}, u32[]{:S(2)}, u32[]{:S(2)}) collective-permute-start(f32[80,256]{1,0:T(8,128)S(1)} %add.44), channel_id=1, source_target_pairs={{0,2},{1,3},{2,0},{3,1},{4,6},{5,7},{6,4},{7,5},{8,10},{9,11},{10,... | collective-permute-start | bytes 245768 | tf_op jit(solution)/shard_map/ppermute | solution.py:394
  104.8 6.5 %collective-permute-start.17 = (f32[80,256]{1,0:T(8,128)S(1)}, f32[80,256]{1,0:T(8,128)S(1)}, u32[]{:S(2)}, u32[]{:S(2)}) collective-permute-start(f32[80,256]{1,0:T(8,128)S(1)} %add.45), channel_id=1, source_target_pairs={{0,4},{1,5},{2,6},{3,7},{4,0},{5,1},{6,2},{7,3},{8,12},{9,13},{10,... | collective-permute-start | bytes 245768 | tf_op jit(solution)/shard_map/ppermute | solution.py:394
  112.2 14.9 %collective-permute-start.22 = (f32[64,2048]{1,0:T(8,128)S(1)}, f32[64,2048]{1,0:T(8,128)S(1)}, u32[]{:S(2)}, u32[]{:S(2)}) collective-permute-start(f32[64,2048]{1,0:T(8,128)S(1)} %get-tuple-element.68), channel_id=1, source_target_pairs={{0,16},{8,24},{16,0},{24,8},{1,17},{9,25},{17,1},{25,9},{2,18},{10... | collective-permute-start | bytes 1572872 | tf_op jit(solution)/shard_map/ppermute | solution.py:394
  113.5 15.3 %collective-permute-start.20 = (f32[64,2048]{1,0:T(8,128)S(1)}, f32[64,2048]{1,0:T(8,128)S(1)}, u32[]{:S(2)}, u32[]{:S(2)}) collective-permute-start(f32[64,2048]{1,0:T(8,128)S(1)} %get-tuple-element.66), channel_id=1, source_target_pairs={{0,8},{8,0},{16,24},{24,16},{1,9},{9,1},{17,25},{25,17},{2,10},{10... | collective-permute-start | bytes 1572872 | tf_op jit(solution)/shard_map/ppermute | solution.py:394
  116.0 23.6 %collective-permute-start.18 = (f32[64,2048]{1,0:T(8,128)S(1)}, f32[64,2048]{1,0:T(8,128)S(1)}, u32[]{:S(2)}, u32[]{:S(2)}) collective-permute-start(f32[64,2048]{1,0:T(8,128)S(1)} %get-tuple-element.63), channel_id=1, source_target_pairs={{0,8},{8,0},{16,24},{24,16},{1,9},{9,1},{17,25},{25,17},{2,10},{10... | collective-permute-start | bytes 1572872 | tf_op jit(solution)/shard_map/ppermute | solution.py:394
  116.6 23.0 %collective-permute-start.19 = (f32[64,2048]{1,0:T(8,128)S(1)}, f32[64,2048]{1,0:T(8,128)S(1)}, u32[]{:S(2)}, u32[]{:S(2)}) collective-permute-start(f32[64,2048]{1,0:T(8,128)S(1)} %get-tuple-element.64), channel_id=1, source_target_pairs={{0,16},{8,24},{16,0},{24,8},{1,17},{9,25},{17,1},{25,9},{2,18},{10... | collective-permute-start | bytes 1572872 | tf_op jit(solution)/shard_map/ppermute | solution.py:394
  127.2 19.5 %collective-permute-start.23 = (f32[64,2048]{1,0:T(8,128)S(1)}, f32[64,2048]{1,0:T(8,128)S(1)}, u32[]{:S(2)}, u32[]{:S(2)}) collective-permute-start(f32[64,2048]{1,0:T(8,128)S(1)} %add.48), channel_id=1, source_target_pairs={{0,8},{8,0},{16,24},{24,16},{1,9},{9,1},{17,25},{25,17},{2,10},{10... | collective-permute-start | bytes 1572872 | tf_op jit(solution)/shard_map/ppermute | solution.py:394
  128.8 17.9 %collective-permute-start.21 = (f32[64,2048]{1,0:T(8,128)S(1)}, f32[64,2048]{1,0:T(8,128)S(1)}, u32[]{:S(2)}, u32[]{:S(2)}) collective-permute-start(f32[64,2048]{1,0:T(8,128)S(1)} %add.47), channel_id=1, source_target_pairs={{0,16},{8,24},{16,0},{24,8},{1,17},{9,25},{17,1},{25,9},{2,18},{10... | collective-permute-start | bytes 1572872 | tf_op jit(solution)/shard_map/ppermute | solution.py:394
  148.1 23.3 %collective-permute-start.30 = (f32[128,2048]{1,0:T(8,128)S(1)}, f32[128,2048]{1,0:T(8,128)S(1)}, u32[]{:S(2)}, u32[]{:S(2)}) collective-permute-start(f32[128,2048]{1,0:T(8,128)S(1)} %get-tuple-element.72.refs_0_), channel_id=1, source_target_pairs={{0,16},{8,24},{16,0},{24,8},{1,17},{9,25},{17,1},{25,9},{2,18},{10... | collective-permute-start | bytes 3145736 | tf_op jit(solution)/shard_map/ppermute | solution.py:394
  149.0 25.1 %collective-permute-start.32 = (f32[128,2048]{1,0:T(8,128)S(1)}, f32[128,2048]{1,0:T(8,128)S(1)}, u32[]{:S(2)}, u32[]{:S(2)}) collective-permute-start(f32[128,2048]{1,0:T(8,128)S(1)} %get-tuple-element.72.refs_0_), channel_id=1, source_target_pairs={{0,8},{8,0},{16,24},{24,16},{1,9},{9,1},{17,25},{25,17},{2,10},{10... | collective-permute-start | bytes 3145736 | tf_op jit(solution)/shard_map/ppermute | solution.py:394
  151.7 4.8 %collective-permute-start.25 = (f32[64,64]{1,0:T(8,128)S(1)}, f32[64,64]{1,0:T(8,128)S(1)}, u32[]{:S(2)}, u32[]{:S(2)}) collective-permute-start(f32[64,64]{1,0:T(8,128)S(1)} %add.49), channel_id=1, source_target_pairs={{0,2},{1,3},{2,0},{3,1},{4,6},{5,7},{6,4},{7,5},{8,10},{9,11},{10,... | collective-permute-start | bytes 49160 | tf_op jit(solution)/shard_map/ppermute | solution.py:394
  156.5 5.8 %collective-permute-start.26 = (f32[64,64]{1,0:T(8,128)S(1)}, f32[64,64]{1,0:T(8,128)S(1)}, u32[]{:S(2)}, u32[]{:S(2)}) collective-permute-start(f32[64,64]{1,0:T(8,128)S(1)} %add.50), channel_id=1, source_target_pairs={{0,4},{1,5},{2,6},{3,7},{4,0},{5,1},{6,2},{7,3},{8,12},{9,13},{10,... | collective-permute-start | bytes 49160 | tf_op jit(solution)/shard_map/ppermute | solution.py:394
  162.3 13.3 %collective-permute-start.27 = (f32[64,64]{1,0:T(8,128)S(1)}, f32[64,64]{1,0:T(8,128)S(1)}, u32[]{:S(2)}, u32[]{:S(2)}) collective-permute-start(f32[64,64]{1,0:T(8,128)S(1)} %add.51.gram), channel_id=1, source_target_pairs={{0,8},{8,0},{16,24},{24,16},{1,9},{9,1},{17,25},{25,17},{2,10},{10... | collective-permute-start | bytes 49160 | tf_op jit(solution)/shard_map/ppermute | solution.py:394
  162.8 12.8 %collective-permute-start.28 = (f32[64,64]{1,0:T(8,128)S(1)}, f32[64,64]{1,0:T(8,128)S(1)}, u32[]{:S(2)}, u32[]{:S(2)}) collective-permute-start(f32[64,64]{1,0:T(8,128)S(1)} %add.51.gram), channel_id=1, source_target_pairs={{0,16},{8,24},{16,0},{24,8},{1,17},{9,25},{17,1},{25,9},{2,18},{10... | collective-permute-start | bytes 49160 | tf_op jit(solution)/shard_map/ppermute | solution.py:394
  164.0 12.3 %collective-permute-start.29 = (f32[64,64]{1,0:T(8,128)S(1)}, f32[64,64]{1,0:T(8,128)S(1)}, u32[]{:S(2)}, u32[]{:S(2)}) collective-permute-start(f32[64,64]{1,0:T(8,128)S(1)} %add.51.gram), channel_id=1, source_target_pairs={{0,24},{8,16},{16,8},{24,0},{1,25},{9,17},{17,9},{25,1},{2,26},{10... | collective-permute-start | bytes 49160 | tf_op jit(solution)/shard_map/ppermute | solution.py:394
  171.5 10.9 %collective-permute-start.31 = (f32[64,2048]{1,0:T(8,128)S(1)}, f32[64,2048]{1,0:T(8,128)S(1)}, u32[]{:S(2)}, u32[]{:S(2)}) collective-permute-start(f32[64,2048]{1,0:T(8,128)S(1)} %slice.8), channel_id=1, source_target_pairs={{0,8},{8,0},{16,24},{24,16},{1,9},{9,1},{17,25},{25,17},{2,10},{10... | collective-permute-start | bytes 1572872 | tf_op jit(solution)/shard_map/ppermute | solution.py:394
  174.1 9.2 %collective-permute-start.33 = (f32[64,2048]{1,0:T(8,128)S(1)}, f32[64,2048]{1,0:T(8,128)S(1)}, u32[]{:S(2)}, u32[]{:S(2)}) collective-permute-start(f32[64,2048]{1,0:T(8,128)S(1)} %slice.9), channel_id=1, source_target_pairs={{0,16},{8,24},{16,0},{24,8},{1,17},{9,25},{17,1},{25,9},{2,18},{10... | collective-permute-start | bytes 1572872 | tf_op jit(solution)/shard_map/ppermute | solution.py:394
  (2 other events, 2.6 us)

commit v8 on v7

--- a/solution.py
+++ b/solution.py
@@ -21,8 +21,9 @@
 
 
 def halves(x):
-    high = x.astype(BF16)
-    return high, (x - high.astype(F32)).astype(BF16)
+    scaled = x * 65537.0
+    high = scaled - (scaled - x)
+    return high.astype(BF16), (x - high).astype(BF16)
 
 
 def thirds(x):

time: 187 us -> 188 us (level)
  no operation moved by 1% of the time
where the time goes in v8:
time: 188 us; the launch traced here: 186 us
  waiting for transfers between devices  98 us (52%)
  starting transfers between devices  47 us (25%)
  Pallas kernels  39.3 us (21%)
    ppermute x34, waiting for transfers between devices, flip(): return lax.ppermute(x, axis, [(i, i ^ bit) for i in range(size)])  98 us
    ppermute x34, starting transfers between devices, flip(): return lax.ppermute(x, axis, [(i, i ^ bit) for i in range(size)])  47 us
    pallas_call x1, Pallas kernels, first_coefficients(): pl.pallas_call(functools.partial(first_kernel, total), out_shape=[array(n...  13.7 us
    pallas_call x6, Pallas kernels, corrections(): pl.pallas_call(functools.partial(corrections_kernel, names, len(base)), o...  7.65 us
    pallas_call x3, Pallas kernels, second_coefficients(): pl.pallas_call(functools.partial(second_kernel, count, total, mode), out_...  7.33 us
  transfers between devices with their start and end apart: 34, of which 22 were waited for; matrix products, arithmetic and copies ran while one was open for 0% of the time, Pallas kernels for 10%

profile of v8, /device:TPU:0, one launch (start us, length us, event | category | flops | bytes accessed | tf_op | source)
XLA Modules:
  0.0 185.6 jit_solution(16226608194475910509)
XLA Ops:
  0.6 13.7 %shard_map.50 = (f32[64,256]{1,0:T(8,128)S(1)}, bf16[256,8192]{1,0:T(8,128)(2,1)S(1)}, bf16[256,8192]{1,0:T(8,128)(2,1)S(1)}, bf16[256,8192]{1,0:T(8,128)(2,1)S(...) custom-call(f32[256,16384]{1,0:T(8,128)} %locked.1, ...), custom_call_target="tpu_custom_call" | custom-call | flops 3221225472 | bytes 33554432 | tf_op jit(solution)/shard_map/pallas_call | solution.py:160
  15.8 3.0 %collective-permute-start.1 = (f32[64,256]{1,0:T(8,128)S(1)}, f32[64,256]{1,0:T(8,128)S(1)}, u32[]{:S(2)}, u32[]{:S(2)}) collective-permute-start(f32[64,256]{1,0:T(8,128)S(1)} %add.39), channel_id=1, source_target_pairs={{0,2},{1,3},{2,0},{3,1},{4,6},{5,7},{6,4},{7,5},{8,10},{9,11},{10,... | collective-permute-start | bytes 196616 | tf_op jit(solution)/shard_map/ppermute | solution.py:395
  18.8 2.4 %collective-permute-done.1 = f32[64,256]{1,0:T(8,128)S(1)} collective-permute-done((f32[64,256]{1,0:T(8,128)S(1)}, f32[64,256]{1,0:T(8,128)S(1)}, u32[]{:S(2)}, u32[]{:S(2)}) %collective-permute-start.1) | collective-permute-done | bytes 65568 | tf_op jit(solution)/shard_map/ppermute | solution.py:395
  21.2 2.9 %collective-permute-start.2 = (f32[64,256]{1,0:T(8,128)S(1)}, f32[64,256]{1,0:T(8,128)S(1)}, u32[]{:S(2)}, u32[]{:S(2)}) collective-permute-start(f32[64,256]{1,0:T(8,128)S(1)} %add.40), channel_id=1, source_target_pairs={{0,4},{1,5},{2,6},{3,7},{4,0},{5,1},{6,2},{7,3},{8,12},{9,13},{10,... | collective-permute-start | bytes 196616 | tf_op jit(solution)/shard_map/ppermute | solution.py:395
  24.1 2.4 %collective-permute-done.2 = f32[64,256]{1,0:T(8,128)S(1)} collective-permute-done((f32[64,256]{1,0:T(8,128)S(1)}, f32[64,256]{1,0:T(8,128)S(1)}, u32[]{:S(2)}, u32[]{:S(2)}) %collective-permute-start.2) | collective-permute-done | bytes 65568 | tf_op jit(solution)/shard_map/ppermute | solution.py:395
  27.5 1.8 collective-permute-start.7
  32.7 1.8 shard_map.51
  34.5 7.9 %collective-permute-done.7 = f32[64,2048]{1,0:T(8,128)S(1)} collective-permute-done((f32[64,2048]{1,0:T(8,128)S(1)}, f32[64,2048]{1,0:T(8,128)S(1)}, u32[]{:S(2)}, u32[]{:S(2)}) %collective-permute-start.7) | collective-permute-done | bytes 524320 | tf_op jit(solution)/shard_map/ppermute | solution.py:395
  45.9 9.5 %collective-permute-done.3.refs_2_ = f32[64,2048]{1,0:T(8,128)S(1)} collective-permute-done((f32[64,2048]{1,0:T(8,128)S(1)}, f32[64,2048]{1,0:T(8,128)S(1)}, u32[]{:S(2)}, u32[]{:S(2)}) %collective-permute-start.3) | collective-permute-done | bytes 524320 | tf_op jit(solution)/shard_map/ppermute | solution.py:395
  55.4 7.8 %collective-permute-done.8.refs_5_ = f32[64,2048]{1,0:T(8,128)S(1)} collective-permute-done((f32[64,2048]{1,0:T(8,128)S(1)}, f32[64,2048]{1,0:T(8,128)S(1)}, u32[]{:S(2)}, u32[]{:S(2)}) %collective-permute-start.8) | collective-permute-done | bytes 524320 | tf_op jit(solution)/shard_map/ppermute | solution.py:395
  67.5 10.8 %collective-permute-done.9.refs_0_ = f32[64,2048]{1,0:T(8,128)S(1)} collective-permute-done((f32[64,2048]{1,0:T(8,128)S(1)}, f32[64,2048]{1,0:T(8,128)S(1)}, u32[]{:S(2)}, u32[]{:S(2)}) %collective-permute-start.9) | collective-permute-done | bytes 524320 | tf_op jit(solution)/shard_map/ppermute | solution.py:395
  80.3 2.0 %shard_map.55 = (f32[64,256]{1,0:T(8,128)S(1)}, f32[2,64,64]{2,1,0:T(8,128)S(1)}) custom-call(bf16[256,8192]{1,0:T(8,128)(2,1)S(1)} %get-tuple-element.39.he, bf16[256,8192]{1,0:T(8,128)(2,1)S(1)} %get-tuple-element.40.ho, bf16[256,8192]{1,0:T(8,128)(2,1)S(1)} %get-tuple-element.41.le, bf16[256,8192]{1,0:T(8,128)(2,1)S(1)} %get-tuple-element.42.lo, ...), custom_call_target="tpu_custom_call" | custom-call | flops 939524096 | bytes 5242880 | tf_op jit(solution)/shard_map/pallas_call | solution.py:244
  82.3 8.0 %collective-permute-done.13.refs_2_ = f32[64,2048]{1,0:T(8,128)S(1)} collective-permute-done((f32[64,2048]{1,0:T(8,128)S(1)}, f32[64,2048]{1,0:T(8,128)S(1)}, u32[]{:S(2)}, u32[]{:S(2)}) %collective-permute-start.13) | collective-permute-done | bytes 524320 | tf_op jit(solution)/shard_map/ppermute | solution.py:395
  90.4 3.4 %shard_map.56 = (f32[64,256]{1,0:T(8,128)S(1)}, f32[4,64,64]{2,1,0:T(8,128)S(1)}) custom-call(bf16[256,8192]{1,0:T(8,128)(2,1)S(1)} %get-tuple-element.39.he, bf16[256,8192]{1,0:T(8,128)(2,1)S(1)} %get-tuple-element.40.ho, bf16[256,8192]{1,0:T(8,128)(2,1)S(1)} %get-tuple-element.41.le, bf16[256,8192]{1,0:T(8,128)(2,1)S(1)} %get-tuple-element.42.lo, ...), custom_call_target="tpu_custom_call" | custom-call | flops 1879048192 | bytes 10485760 | tf_op jit(solution)/shard_map/pallas_call | solution.py:244
  93.8 3.8 %collective-permute-done.10.refs_0_ = f32[64,2048]{1,0:T(8,128)S(1)} collective-permute-done((f32[64,2048]{1,0:T(8,128)S(1)}, f32[64,2048]{1,0:T(8,128)S(1)}, u32[]{:S(2)}, u32[]{:S(2)}) %collective-permute-start.10) | collective-permute-done | bytes 524320 | tf_op jit(solution)/shard_map/ppermute | solution.py:395
  97.5 1.9 %shard_map.57 = f32[80,256]{1,0:T(8,128)S(1)} custom-call(bf16[256,8192]{1,0:T(8,128)(2,1)S(1)} %get-tuple-element.39.he, bf16[256,8192]{1,0:T(8,128)(2,1)S(1)} %get-tuple-element.40.ho, bf16[256,8192]{1,0:T(8,128)(2,1)S(1)} %get-tuple-element.41.le, bf16[256,8192]{1,0:T(8,128)(2,1)S(1)} %get-tuple-element.42.lo, f32[1,16384]{1,0:T(1,128)S(1)} %get-tuple-element.38.mass, ...), custom_call_target="tpu_custom_call" | custom-call | flops 939524096 | bytes 5242880 | tf_op jit(solution)/shard_map/pallas_call | solution.py:244
  101.9 3.5 %collective-permute-done.16 = f32[80,256]{1,0:T(8,128)S(1)} collective-permute-done((f32[80,256]{1,0:T(8,128)S(1)}, f32[80,256]{1,0:T(8,128)S(1)}, u32[]{:S(2)}, u32[]{:S(2)}) %collective-permute-start.16) | collective-permute-done | bytes 81952 | tf_op jit(solution)/shard_map/ppermute | solution.py:395
  105.4 2.4 %collective-permute-start.17 = (f32[80,256]{1,0:T(8,128)S(1)}, f32[80,256]{1,0:T(8,128)S(1)}, u32[]{:S(2)}, u32[]{:S(2)}) collective-permute-start(f32[80,256]{1,0:T(8,128)S(1)} %add.45), channel_id=1, source_target_pairs={{0,4},{1,5},{2,6},{3,7},{4,0},{5,1},{6,2},{7,3},{8,12},{9,13},{10,... | collective-permute-start | bytes 245768 | tf_op jit(solution)/shard_map/ppermute | solution.py:395
  107.8 4.0 %collective-permute-done.17 = f32[80,256]{1,0:T(8,128)S(1)} collective-permute-done((f32[80,256]{1,0:T(8,128)S(1)}, f32[80,256]{1,0:T(8,128)S(1)}, u32[]{:S(2)}, u32[]{:S(2)}) %collective-permute-start.17) | collective-permute-done | bytes 81952 | tf_op jit(solution)/shard_map/ppermute | solution.py:395
  118.1 1.8 shard_map.59
  119.9 7.9 %collective-permute-done.22 = f32[64,2048]{1,0:T(8,128)S(1)} collective-permute-done((f32[64,2048]{1,0:T(8,128)S(1)}, f32[64,2048]{1,0:T(8,128)S(1)}, u32[]{:S(2)}, u32[]{:S(2)}) %collective-permute-start.22) | collective-permute-done | bytes 524320 | tf_op jit(solution)/shard_map/ppermute | solution.py:395
  130.8 2.3 %shard_map.58 = (f32[64,64]{1,0:T(8,128)S(1)}, f32[64,64]{1,0:T(8,128)S(1)}) custom-call(f32[80,256]{1,0:T(8,128)S(1)} %add.46.both.coef), custom_call_target="tpu_custom_call" | custom-call | flops 1000000 | bytes 100000 | tf_op jit(solution)/shard_map/pallas_call | solution.py:441
  133.1 7.2 %collective-permute-done.18.refs_2_ = f32[64,2048]{1,0:T(8,128)S(1)} collective-permute-done((f32[64,2048]{1,0:T(8,128)S(1)}, f32[64,2048]{1,0:T(8,128)S(1)}, u32[]{:S(2)}, u32[]{:S(2)}) %collective-permute-start.18) | collective-permute-done | bytes 524320 | tf_op jit(solution)/shard_map/ppermute | solution.py:395
  140.3 7.1 %collective-permute-done.23.refs_5_ = f32[64,2048]{1,0:T(8,128)S(1)} collective-permute-done((f32[64,2048]{1,0:T(8,128)S(1)}, f32[64,2048]{1,0:T(8,128)S(1)}, u32[]{:S(2)}, u32[]{:S(2)}) %collective-permute-start.23) | collective-permute-done | bytes 524320 | tf_op jit(solution)/shard_map/ppermute | solution.py:395
  152.3 2.9 %collective-permute-start.25 = (f32[64,64]{1,0:T(8,128)S(1)}, f32[64,64]{1,0:T(8,128)S(1)}, u32[]{:S(2)}, u32[]{:S(2)}) collective-permute-start(f32[64,64]{1,0:T(8,128)S(1)} %add.49), channel_id=1, source_target_pairs={{0,2},{1,3},{2,0},{3,1},{4,6},{5,7},{6,4},{7,5},{8,10},{9,11},{10,... | collective-permute-start | bytes 49160 | tf_op jit(solution)/shard_map/ppermute | solution.py:395
  155.2 1.9 %collective-permute-done.25 = f32[64,64]{1,0:T(8,128)S(1)} collective-permute-done((f32[64,64]{1,0:T(8,128)S(1)}, f32[64,64]{1,0:T(8,128)S(1)}, u32[]{:S(2)}, u32[]{:S(2)}) %collective-permute-start.25) | collective-permute-done | bytes 16416 | tf_op jit(solution)/shard_map/ppermute | solution.py:395
  157.1 3.5 %collective-permute-start.26 = (f32[64,64]{1,0:T(8,128)S(1)}, f32[64,64]{1,0:T(8,128)S(1)}, u32[]{:S(2)}, u32[]{:S(2)}) collective-permute-start(f32[64,64]{1,0:T(8,128)S(1)} %add.50), channel_id=1, source_target_pairs={{0,4},{1,5},{2,6},{3,7},{4,0},{5,1},{6,2},{7,3},{8,12},{9,13},{10,... | collective-permute-start | bytes 49160 | tf_op jit(solution)/shard_map/ppermute | solution.py:395
  160.7 2.2 %collective-permute-done.26 = f32[64,64]{1,0:T(8,128)S(1)} collective-permute-done((f32[64,64]{1,0:T(8,128)S(1)}, f32[64,64]{1,0:T(8,128)S(1)}, u32[]{:S(2)}, u32[]{:S(2)}) %collective-permute-start.26) | collective-permute-done | bytes 16416 | tf_op jit(solution)/shard_map/ppermute | solution.py:395
  166.4 5.7 %collective-permute-done.30.refs_2_ = f32[128,2048]{1,0:T(8,128)S(1)} collective-permute-done((f32[128,2048]{1,0:T(8,128)S(1)}, f32[128,2048]{1,0:T(8,128)S(1)}, u32[]{:S(2)}, u32[]{:S(2)}) %collective-permute-start.30) | collective-permute-done | bytes 1048608 | tf_op jit(solution)/shard_map/ppermute | solution.py:395
  172.1 2.6 %collective-permute-start.31 = (f32[64,2048]{1,0:T(8,128)S(1)}, f32[64,2048]{1,0:T(8,128)S(1)}, u32[]{:S(2)}, u32[]{:S(2)}) collective-permute-start(f32[64,2048]{1,0:T(8,128)S(1)} %slice.8), channel_id=1, source_target_pairs={{0,8},{8,0},{16,24},{24,16},{1,9},{9,1},{17,25},{25,17},{2,10},{10... | collective-permute-start | bytes 1572872 | tf_op jit(solution)/shard_map/ppermute | solution.py:395
  176.9 3.0 %shard_map.63 = (f32[64,64]{1,0:T(8,128)}, f32[64,64]{1,0:T(8,128)S(1)}) custom-call(f32[64,64]{1,0:T(8,128)S(1)} %add.51.gram, f32[64,64]{1,0:T(8,128)S(1)} %collective-permute-done.27.one, f32[64,64]{1,0:T(8,128)S(1)} %collective-permute-done.28.two, f32[64,64]{1,0:T(8,128)S(1)} %collective-permute-done.29.three, f32[64,64]{1,0:T(8,128)S(1)} %get-tuple-element.70.upper_one), custom_call_target="tpu_custom_call" | custom-call | flops 5000000000 | bytes 100000 | tf_op jit(solution)/shard_map/pallas_call | solution.py:461
  180.0 2.3 %shard_map.64.refs_2_ = f32[64,16384]{1,0:T(8,128)} custom-call(f32[64,64]{1,0:T(8,128)S(1)} %get-tuple-element.71.inverse, f32[128,2048]{1,0:T(8,128)S(1)} %get-tuple-element.72.refs_0_, f32[128,2048]{1,0:T(8,128)S(1)} %collective-permute-done.32.refs_1_, f32[128,2048]{1,0:T(8,128)S(1)} %collective-permute-done.30.refs_2_), custom_call_target="tpu_custom_call" | custom-call | flops 905969664 | bytes 6291456 | tf_op jit(solution)/shard_map/pallas_call | solution.py:381
  (67 shorter events, 41.1 us)
Async XLA Ops:
  14.3 1.4 collective-permute-start
  15.8 5.4 %collective-permute-start.1 = (f32[64,256]{1,0:T(8,128)S(1)}, f32[64,256]{1,0:T(8,128)S(1)}, u32[]{:S(2)}, u32[]{:S(2)}) collective-permute-start(f32[64,256]{1,0:T(8,128)S(1)} %add.39), channel_id=1, source_target_pairs={{0,2},{1,3},{2,0},{3,1},{4,6},{5,7},{6,4},{7,5},{8,10},{9,11},{10,... | collective-permute-start | bytes 196616 | tf_op jit(solution)/shard_map/ppermute | solution.py:395
  21.2 5.3 %collective-permute-start.2 = (f32[64,256]{1,0:T(8,128)S(1)}, f32[64,256]{1,0:T(8,128)S(1)}, u32[]{:S(2)}, u32[]{:S(2)}) collective-permute-start(f32[64,256]{1,0:T(8,128)S(1)} %add.40), channel_id=1, source_target_pairs={{0,4},{1,5},{2,6},{3,7},{4,0},{5,1},{6,2},{7,3},{8,12},{9,13},{10,... | collective-permute-start | bytes 196616 | tf_op jit(solution)/shard_map/ppermute | solution.py:395
  27.5 14.9 %collective-permute-start.7 = (f32[64,2048]{1,0:T(8,128)S(1)}, f32[64,2048]{1,0:T(8,128)S(1)}, u32[]{:S(2)}, u32[]{:S(2)}) collective-permute-start(f32[64,2048]{1,0:T(8,128)S(1)} %get-tuple-element.53), channel_id=1, source_target_pairs={{0,16},{8,24},{16,0},{24,8},{1,17},{9,25},{17,1},{25,9},{2,18},{10... | collective-permute-start | bytes 1572872 | tf_op jit(solution)/shard_map/ppermute | solution.py:395
  29.3 15.0 %collective-permute-start.5 = (f32[64,2048]{1,0:T(8,128)S(1)}, f32[64,2048]{1,0:T(8,128)S(1)}, u32[]{:S(2)}, u32[]{:S(2)}) collective-permute-start(f32[64,2048]{1,0:T(8,128)S(1)} %get-tuple-element.51), channel_id=1, source_target_pairs={{0,8},{8,0},{16,24},{24,16},{1,9},{9,1},{17,25},{25,17},{2,10},{10... | collective-permute-start | bytes 1572872 | tf_op jit(solution)/shard_map/ppermute | solution.py:395
  31.8 23.6 %collective-permute-start.3 = (f32[64,2048]{1,0:T(8,128)S(1)}, f32[64,2048]{1,0:T(8,128)S(1)}, u32[]{:S(2)}, u32[]{:S(2)}) collective-permute-start(f32[64,2048]{1,0:T(8,128)S(1)} %get-tuple-element.48), channel_id=1, source_target_pairs={{0,8},{8,0},{16,24},{24,16},{1,9},{9,1},{17,25},{25,17},{2,10},{10... | collective-permute-start | bytes 1572872 | tf_op jit(solution)/shard_map/ppermute | solution.py:395
  32.4 23.0 %collective-permute-start.4 = (f32[64,2048]{1,0:T(8,128)S(1)}, f32[64,2048]{1,0:T(8,128)S(1)}, u32[]{:S(2)}, u32[]{:S(2)}) collective-permute-start(f32[64,2048]{1,0:T(8,128)S(1)} %get-tuple-element.49), channel_id=1, source_target_pairs={{0,16},{8,24},{16,0},{24,8},{1,17},{9,25},{17,1},{25,9},{2,18},{10... | collective-permute-start | bytes 1572872 | tf_op jit(solution)/shard_map/ppermute | solution.py:395
  42.5 20.7 %collective-permute-start.8 = (f32[64,2048]{1,0:T(8,128)S(1)}, f32[64,2048]{1,0:T(8,128)S(1)}, u32[]{:S(2)}, u32[]{:S(2)}) collective-permute-start(f32[64,2048]{1,0:T(8,128)S(1)} %add.43), channel_id=1, source_target_pairs={{0,8},{8,0},{16,24},{24,16},{1,9},{9,1},{17,25},{25,17},{2,10},{10... | collective-permute-start | bytes 1572872 | tf_op jit(solution)/shard_map/ppermute | solution.py:395
  44.3 18.9 %collective-permute-start.6 = (f32[64,2048]{1,0:T(8,128)S(1)}, f32[64,2048]{1,0:T(8,128)S(1)}, u32[]{:S(2)}, u32[]{:S(2)}) collective-permute-start(f32[64,2048]{1,0:T(8,128)S(1)} %add.42), channel_id=1, source_target_pairs={{0,16},{8,24},{16,0},{24,8},{1,17},{9,25},{17,1},{25,9},{2,18},{10... | collective-permute-start | bytes 1572872 | tf_op jit(solution)/shard_map/ppermute | solution.py:395
  63.3 14.9 %collective-permute-start.9 = (f32[64,2048]{1,0:T(8,128)S(1)}, f32[64,2048]{1,0:T(8,128)S(1)}, u32[]{:S(2)}, u32[]{:S(2)}) collective-permute-start(f32[64,2048]{1,0:T(8,128)S(1)} %get-tuple-element.54.refs_0_), channel_id=1, source_target_pairs={{0,16},{8,24},{16,0},{24,8},{1,17},{9,25},{17,1},{25,9},{2,18},{10... | collective-permute-start | bytes 1572872 | tf_op jit(solution)/shard_map/ppermute | solution.py:395
  64.3 15.7 %collective-permute-start.11 = (f32[64,2048]{1,0:T(8,128)S(1)}, f32[64,2048]{1,0:T(8,128)S(1)}, u32[]{:S(2)}, u32[]{:S(2)}) collective-permute-start(f32[64,2048]{1,0:T(8,128)S(1)} %get-tuple-element.55.refs_1_), channel_id=1, source_target_pairs={{0,8},{8,0},{16,24},{24,16},{1,9},{9,1},{17,25},{25,17},{2,10},{10... | collective-permute-start | bytes 1572872 | tf_op jit(solution)/shard_map/ppermute | solution.py:395
  65.4 25.0 %collective-permute-start.13 = (f32[64,2048]{1,0:T(8,128)S(1)}, f32[64,2048]{1,0:T(8,128)S(1)}, u32[]{:S(2)}, u32[]{:S(2)}) collective-permute-start(f32[64,2048]{1,0:T(8,128)S(1)} %get-tuple-element.54.refs_0_), channel_id=1, source_target_pairs={{0,8},{8,0},{16,24},{24,16},{1,9},{9,1},{17,25},{25,17},{2,10},{10... | collective-permute-start | bytes 1572872 | tf_op jit(solution)/shard_map/ppermute | solution.py:395
  66.3 24.1 %collective-permute-start.14 = (f32[64,2048]{1,0:T(8,128)S(1)}, f32[64,2048]{1,0:T(8,128)S(1)}, u32[]{:S(2)}, u32[]{:S(2)}) collective-permute-start(f32[64,2048]{1,0:T(8,128)S(1)} %get-tuple-element.55.refs_1_), channel_id=1, source_target_pairs={{0,16},{8,24},{16,0},{24,8},{1,17},{9,25},{17,1},{25,9},{2,18},{10... | collective-permute-start | bytes 1572872 | tf_op jit(solution)/shard_map/ppermute | solution.py:395
  78.3 19.3 %collective-permute-start.10 = (f32[64,2048]{1,0:T(8,128)S(1)}, f32[64,2048]{1,0:T(8,128)S(1)}, u32[]{:S(2)}, u32[]{:S(2)}) collective-permute-start(f32[64,2048]{1,0:T(8,128)S(1)} %collective-permute-done.9.refs_0_), channel_id=1, source_target_pairs={{0,8},{8,0},{16,24},{24,16},{1,9},{9,1},{17,25},{25,17},{2,10},{10... | collective-permute-start | bytes 1572872 | tf_op jit(solution)/shard_map/ppermute | solution.py:395
  79.9 17.6 %collective-permute-start.12 = (f32[64,2048]{1,0:T(8,128)S(1)}, f32[64,2048]{1,0:T(8,128)S(1)}, u32[]{:S(2)}, u32[]{:S(2)}) collective-permute-start(f32[64,2048]{1,0:T(8,128)S(1)} %collective-permute-done.11.refs_1_), channel_id=1, source_target_pairs={{0,16},{8,24},{16,0},{24,8},{1,17},{9,25},{17,1},{25,9},{2,18},{10... | collective-permute-start | bytes 1572872 | tf_op jit(solution)/shard_map/ppermute | solution.py:395
  100.8 4.6 %collective-permute-start.16 = (f32[80,256]{1,0:T(8,128)S(1)}, f32[80,256]{1,0:T(8,128)S(1)}, u32[]{:S(2)}, u32[]{:S(2)}) collective-permute-start(f32[80,256]{1,0:T(8,128)S(1)} %add.44), channel_id=1, source_target_pairs={{0,2},{1,3},{2,0},{3,1},{4,6},{5,7},{6,4},{7,5},{8,10},{9,11},{10,... | collective-permute-start | bytes 245768 | tf_op jit(solution)/shard_map/ppermute | solution.py:395
  105.4 6.5 %collective-permute-start.17 = (f32[80,256]{1,0:T(8,128)S(1)}, f32[80,256]{1,0:T(8,128)S(1)}, u32[]{:S(2)}, u32[]{:S(2)}) collective-permute-start(f32[80,256]{1,0:T(8,128)S(1)} %add.45), channel_id=1, source_target_pairs={{0,4},{1,5},{2,6},{3,7},{4,0},{5,1},{6,2},{7,3},{8,12},{9,13},{10,... | collective-permute-start | bytes 245768 | tf_op jit(solution)/shard_map/ppermute | solution.py:395
  112.9 14.9 %collective-permute-start.22 = (f32[64,2048]{1,0:T(8,128)S(1)}, f32[64,2048]{1,0:T(8,128)S(1)}, u32[]{:S(2)}, u32[]{:S(2)}) collective-permute-start(f32[64,2048]{1,0:T(8,128)S(1)} %get-tuple-element.68), channel_id=1, source_target_pairs={{0,16},{8,24},{16,0},{24,8},{1,17},{9,25},{17,1},{25,9},{2,18},{10... | collective-permute-start | bytes 1572872 | tf_op jit(solution)/shard_map/ppermute | solution.py:395
  114.2 15.3 %collective-permute-start.20 = (f32[64,2048]{1,0:T(8,128)S(1)}, f32[64,2048]{1,0:T(8,128)S(1)}, u32[]{:S(2)}, u32[]{:S(2)}) collective-permute-start(f32[64,2048]{1,0:T(8,128)S(1)} %get-tuple-element.66), channel_id=1, source_target_pairs={{0,8},{8,0},{16,24},{24,16},{1,9},{9,1},{17,25},{25,17},{2,10},{10... | collective-permute-start | bytes 1572872 | tf_op jit(solution)/shard_map/ppermute | solution.py:395
  116.7 23.6 %collective-permute-start.18 = (f32[64,2048]{1,0:T(8,128)S(1)}, f32[64,2048]{1,0:T(8,128)S(1)}, u32[]{:S(2)}, u32[]{:S(2)}) collective-permute-start(f32[64,2048]{1,0:T(8,128)S(1)} %get-tuple-element.63), channel_id=1, source_target_pairs={{0,8},{8,0},{16,24},{24,16},{1,9},{9,1},{17,25},{25,17},{2,10},{10... | collective-permute-start | bytes 1572872 | tf_op jit(solution)/shard_map/ppermute | solution.py:395
  117.3 23.0 %collective-permute-start.19 = (f32[64,2048]{1,0:T(8,128)S(1)}, f32[64,2048]{1,0:T(8,128)S(1)}, u32[]{:S(2)}, u32[]{:S(2)}) collective-permute-start(f32[64,2048]{1,0:T(8,128)S(1)} %get-tuple-element.64), channel_id=1, source_target_pairs={{0,16},{8,24},{16,0},{24,8},{1,17},{9,25},{17,1},{25,9},{2,18},{10... | collective-permute-start | bytes 1572872 | tf_op jit(solution)/shard_map/ppermute | solution.py:395
  127.9 19.5 %collective-permute-start.23 = (f32[64,2048]{1,0:T(8,128)S(1)}, f32[64,2048]{1,0:T(8,128)S(1)}, u32[]{:S(2)}, u32[]{:S(2)}) collective-permute-start(f32[64,2048]{1,0:T(8,128)S(1)} %add.48), channel_id=1, source_target_pairs={{0,8},{8,0},{16,24},{24,16},{1,9},{9,1},{17,25},{25,17},{2,10},{10... | collective-permute-start | bytes 1572872 | tf_op jit(solution)/shard_map/ppermute | solution.py:395
  129.5 17.9 %collective-permute-start.21 = (f32[64,2048]{1,0:T(8,128)S(1)}, f32[64,2048]{1,0:T(8,128)S(1)}, u32[]{:S(2)}, u32[]{:S(2)}) collective-permute-start(f32[64,2048]{1,0:T(8,128)S(1)} %add.47), channel_id=1, source_target_pairs={{0,16},{8,24},{16,0},{24,8},{1,17},{9,25},{17,1},{25,9},{2,18},{10... | collective-permute-start | bytes 1572872 | tf_op jit(solution)/shard_map/ppermute | solution.py:395
  148.8 23.3 %collective-permute-start.30 = (f32[128,2048]{1,0:T(8,128)S(1)}, f32[128,2048]{1,0:T(8,128)S(1)}, u32[]{:S(2)}, u32[]{:S(2)}) collective-permute-start(f32[128,2048]{1,0:T(8,128)S(1)} %get-tuple-element.72.refs_0_), channel_id=1, source_target_pairs={{0,16},{8,24},{16,0},{24,8},{1,17},{9,25},{17,1},{25,9},{2,18},{10... | collective-permute-start | bytes 3145736 | tf_op jit(solution)/shard_map/ppermute | solution.py:395
  149.6 25.1 %collective-permute-start.32 = (f32[128,2048]{1,0:T(8,128)S(1)}, f32[128,2048]{1,0:T(8,128)S(1)}, u32[]{:S(2)}, u32[]{:S(2)}) collective-permute-start(f32[128,2048]{1,0:T(8,128)S(1)} %get-tuple-element.72.refs_0_), channel_id=1, source_target_pairs={{0,8},{8,0},{16,24},{24,16},{1,9},{9,1},{17,25},{25,17},{2,10},{10... | collective-permute-start | bytes 3145736 | tf_op jit(solution)/shard_map/ppermute | solution.py:395
  152.3 4.8 %collective-permute-start.25 = (f32[64,64]{1,0:T(8,128)S(1)}, f32[64,64]{1,0:T(8,128)S(1)}, u32[]{:S(2)}, u32[]{:S(2)}) collective-permute-start(f32[64,64]{1,0:T(8,128)S(1)} %add.49), channel_id=1, source_target_pairs={{0,2},{1,3},{2,0},{3,1},{4,6},{5,7},{6,4},{7,5},{8,10},{9,11},{10,... | collective-permute-start | bytes 49160 | tf_op jit(solution)/shard_map/ppermute | solution.py:395
  157.1 5.8 %collective-permute-start.26 = (f32[64,64]{1,0:T(8,128)S(1)}, f32[64,64]{1,0:T(8,128)S(1)}, u32[]{:S(2)}, u32[]{:S(2)}) collective-permute-start(f32[64,64]{1,0:T(8,128)S(1)} %add.50), channel_id=1, source_target_pairs={{0,4},{1,5},{2,6},{3,7},{4,0},{5,1},{6,2},{7,3},{8,12},{9,13},{10,... | collective-permute-start | bytes 49160 | tf_op jit(solution)/shard_map/ppermute | solution.py:395
  162.9 13.3 %collective-permute-start.27 = (f32[64,64]{1,0:T(8,128)S(1)}, f32[64,64]{1,0:T(8,128)S(1)}, u32[]{:S(2)}, u32[]{:S(2)}) collective-permute-start(f32[64,64]{1,0:T(8,128)S(1)} %add.51.gram), channel_id=1, source_target_pairs={{0,8},{8,0},{16,24},{24,16},{1,9},{9,1},{17,25},{25,17},{2,10},{10... | collective-permute-start | bytes 49160 | tf_op jit(solution)/shard_map/ppermute | solution.py:395
  163.4 12.8 %collective-permute-start.28 = (f32[64,64]{1,0:T(8,128)S(1)}, f32[64,64]{1,0:T(8,128)S(1)}, u32[]{:S(2)}, u32[]{:S(2)}) collective-permute-start(f32[64,64]{1,0:T(8,128)S(1)} %add.51.gram), channel_id=1, source_target_pairs={{0,16},{8,24},{16,0},{24,8},{1,17},{9,25},{17,1},{25,9},{2,18},{10... | collective-permute-start | bytes 49160 | tf_op jit(solution)/shard_map/ppermute | solution.py:395
  164.7 12.3 %collective-permute-start.29 = (f32[64,64]{1,0:T(8,128)S(1)}, f32[64,64]{1,0:T(8,128)S(1)}, u32[]{:S(2)}, u32[]{:S(2)}) collective-permute-start(f32[64,64]{1,0:T(8,128)S(1)} %add.51.gram), channel_id=1, source_target_pairs={{0,24},{8,16},{16,8},{24,0},{1,25},{9,17},{17,9},{25,1},{2,26},{10... | collective-permute-start | bytes 49160 | tf_op jit(solution)/shard_map/ppermute | solution.py:395
  172.1 10.9 %collective-permute-start.31 = (f32[64,2048]{1,0:T(8,128)S(1)}, f32[64,2048]{1,0:T(8,128)S(1)}, u32[]{:S(2)}, u32[]{:S(2)}) collective-permute-start(f32[64,2048]{1,0:T(8,128)S(1)} %slice.8), channel_id=1, source_target_pairs={{0,8},{8,0},{16,24},{24,16},{1,9},{9,1},{17,25},{25,17},{2,10},{10... | collective-permute-start | bytes 1572872 | tf_op jit(solution)/shard_map/ppermute | solution.py:395
  174.7 9.2 %collective-permute-start.33 = (f32[64,2048]{1,0:T(8,128)S(1)}, f32[64,2048]{1,0:T(8,128)S(1)}, u32[]{:S(2)}, u32[]{:S(2)}) collective-permute-start(f32[64,2048]{1,0:T(8,128)S(1)} %slice.9), channel_id=1, source_target_pairs={{0,16},{8,24},{16,0},{24,8},{1,17},{9,25},{17,1},{25,9},{2,18},{10... | collective-permute-start | bytes 1572872 | tf_op jit(solution)/shard_map/ppermute | solution.py:395
  (2 other events, 2.6 us)
